TPU v7x, 512 devices: a whole 4x4x16 slice. The times are simulated.
512 devices in a mesh: group: 16 (over x_lo, y, core), seq: 32 (over x_hi, z).
Axes of the slice: x: 4 (x_hi: 2, x_lo: 2; x = x_hi * 2 + x_lo), y: 4, z: 16, core: 2. Of those that a mesh axis runs over, the one named last changes fastest.
Arguments:
- queries: bfloat16 [16, 768, 4096], P('group', 'seq'), may hold values from -120 to 120
- keys: bfloat16 [16, 768, 4096], P('group', 'seq'), may hold values from -10 to 10
- values: bfloat16 [16, 768, 4096], P('group', 'seq'), may hold values from -6 to 6
- cross_queries: bfloat16 [16, 768, 4096], P('group', 'seq'), may hold values from -120 to 120
- text_keys: bfloat16 [512, 4096], P('group', 'seq'), may hold values from -10 to 10
- text_values: bfloat16 [512, 4096], P('group', 'seq'), may hold values from -6 to 6
- group_gate: float32 [16, 4096], P('group', 'seq'), may hold values from 0.5 to 1.5
- group_ids: int32 [16], replicated, may hold values from 0 to 15, each once
- text_len: int32 [1], replicated, may hold values from 256 to 512
Outputs:
- mixed: bfloat16 [16, 768, 4096], P('group', 'seq')
Inputs may be any that keep to these rules, and one draw needn't show every extreme that they name: `group_ids`: every group number appears once.
All inputs are finite; a program needn't handle non-finite values.
Results may differ from a plain program's by a relative error of at most 0.009.
Values may be sent and summed in bfloat16 or wider, within the bound.
No kernel may reach another device: no remote copies, remote signals or barrier semaphores. Data moves between devices by JAX's collectives and lax.ppermute only.
A program may use at most 64 MiB of HBM per device.

v0:
```python
import math

import jax
import jax.numpy as jnp
from jax import lax
from jax.sharding import PartitionSpec as P

HD = 128


def start_state(head_count, row_count, head_size):
    return (
        jnp.full((head_count, row_count, 1), -1e30, jnp.float32),
        jnp.zeros((head_count, row_count, 1), jnp.float32),
        jnp.zeros((head_count, row_count, head_size), jnp.float32),
    )


def attend_block(carry_state, query_heads, key_block, value_block, visible):
    running_top, running_total, running_sum = carry_state
    scores = jnp.einsum(
        "qhd,khd->hqk", query_heads, key_block, preferred_element_type=jnp.float32
    ) * (1.0 / math.sqrt(query_heads.shape[2]))
    scores = jnp.where(visible[None, None, :], scores, -jnp.inf)
    block_top = jnp.max(scores, axis=2, keepdims=True)
    new_top = jnp.maximum(running_top, block_top)
    weights = jnp.exp(scores - new_top)
    factor = jnp.exp(running_top - new_top)
    new_total = running_total * factor + jnp.sum(weights, axis=2, keepdims=True)
    new_sum = running_sum * factor + jnp.einsum(
        "hqk,khd->hqd",
        weights.astype(jnp.bfloat16),
        value_block,
        preferred_element_type=jnp.float32,
    )
    return (new_top, new_total, new_sum)


def finish_state(carry_state):
    normed = carry_state[2] / carry_state[1]
    return jnp.transpose(normed, (1, 0, 2)).reshape(
        normed.shape[1], normed.shape[0] * normed.shape[2]
    )


def body(
    queries, keys, values, cross_queries, text_keys, text_values, group_gate, group_ids, text_len
):
    query_rows, key_rows, value_rows, cross_rows = (
        lax.all_to_all(queries[0], "seq", split_axis=1, concat_axis=0, tiled=True),
        lax.all_to_all(keys[0], "seq", split_axis=1, concat_axis=0, tiled=True),
        lax.all_to_all(values[0], "seq", split_axis=1, concat_axis=0, tiled=True),
        lax.all_to_all(cross_queries[0], "seq", split_axis=1, concat_axis=0, tiled=True),
    )
    row_count, row_width = query_rows.shape
    head_size = HD
    head_count = row_width // head_size
    own_slot = lax.axis_index("group")
    own_rank = group_ids[own_slot]
    query_heads = query_rows.reshape(row_count, head_count, head_size)
    key_piece = lax.all_gather(key_rows, "group", axis=0, tiled=True)
    value_piece = lax.all_gather(value_rows, "group", axis=0, tiled=True)
    blocks = key_piece.shape[0] // row_count
    key_blocks = key_piece.reshape(blocks, row_count, head_count, head_size)
    value_blocks = value_piece.reshape(blocks, row_count, head_count, head_size)

    def per_block(inner_state, item):
        key_block, value_block, block_rank = item
        visible = block_rank <= own_rank
        inner_state = attend_block(
            inner_state,
            query_heads,
            key_block,
            value_block,
            jnp.broadcast_to(visible, (row_count,)),
        )
        return (inner_state, None)

    final_state, unused = lax.scan(
        per_block,
        start_state(head_count, row_count, head_size),
        (key_blocks, value_blocks, group_ids),
    )
    self_out = finish_state(final_state)
    cross_heads = cross_rows.reshape(row_count, head_count, head_size)
    text_key_piece = lax.all_gather(text_keys, "group", axis=0, tiled=True)
    text_value_piece = lax.all_gather(text_values, "group", axis=0, tiled=True)
    length = text_key_piece.shape[0]
    visible = jnp.arange(length, dtype=jnp.int32) < text_len[0]
    cross_out = finish_state(
        attend_block(
            start_state(head_count, row_count, head_size),
            cross_heads,
            text_key_piece.reshape(length, head_count, head_size),
            text_value_piece.reshape(length, head_count, head_size),
            visible,
        )
    )
    combined = (group_gate[0][None, :] * self_out + cross_out).astype(jnp.bfloat16)
    mixed = lax.all_to_all(combined, "seq", split_axis=0, concat_axis=1, tiled=True)
    return mixed[None]


def solution(mesh):
    return jax.shard_map(
        body,
        mesh=mesh,
        in_specs=(
            P("group", "seq", None),
            P("group", "seq", None),
            P("group", "seq", None),
            P("group", "seq", None),
            P("group", "seq"),
            P("group", "seq"),
            P("group", "seq"),
            P(),
            P(),
        ),
        out_specs=P("group", "seq", None),
        check_vma=False,
    )
```

profile of v0, /device:TPU:1, one launch (start us, length us, event | category | flops | bytes accessed | tf_op | source)
XLA Modules:
  0.0 269.1 jit_solution(10657767780823276701)
XLA Ops:
  6.6 1.0 copy.33
  7.7 37.0 %all_to_all.83 = bf16[24,32,128]{2,0,1:T(8,128)(2,1)} all-to-all(bf16[24,32,128]{2,0,1:T(8,128)(2,1)S(1)} %copy.26), channel_id=1, replica_groups=mesh['group'=16,'seq'=32] {'seq'}, dimensions={1} | all-to-all | bytes 393216 | tf_op jit(solution)/shard_map/all_to_all | solution.py:51
  44.8 1.0 copy.35
  45.8 22.8 %all_to_all.84 = bf16[24,32,128]{2,0,1:T(8,128)(2,1)} all-to-all(bf16[24,32,128]{2,0,1:T(8,128)(2,1)S(1)} %copy.28), channel_id=1, replica_groups=mesh['group'=16,'seq'=32] {'seq'}, dimensions={1} | all-to-all | bytes 393216 | tf_op jit(solution)/shard_map/all_to_all | solution.py:52
  68.7 0.8 copy.31
  69.5 5.2 %all-to-all-start.3 = ((bf16[24,32,128]{2,0,1:T(8,128)(2,1)}), bf16[24,32,128]{2,0,1:T(8,128)(2,1)S(1)}, u32[]{:S(2)}, u32[]{:S(2)}) async-start(bf16[24,32,128]{2,0,1:T(8,128)(2,1)} %copy.31), calls=%async_computation.3 | async-start | bytes 393216 | tf_op jit(solution)/shard_map/all_to_all | solution.py:53
  75.4 0.8 copy.27
  76.2 0.6 dynamic_slice.14
  76.8 22.0 %all_gather.15 = bf16[512,128]{1,0:T(8,128)(2,1)S(1)} all-gather(bf16[32,128]{1,0:T(8,128)(2,1)S(1)} %copy-done.2), channel_id=1, replica_groups=mesh['group'=16,'seq'=32] {'group'}, dimensions={0}, use_global_device_ids=true | all-gather | bytes 139264 | tf_op jit(solution)/shard_map/all_gather | solution.py:87
  98.8 16.8 %all_gather.14 = bf16[512,128]{1,0:T(8,128)(2,1)S(1)} all-gather(bf16[32,128]{1,0:T(8,128)(2,1)S(1)} %copy-done.3), channel_id=1, replica_groups=mesh['group'=16,'seq'=32] {'group'}, dimensions={0}, use_global_device_ids=true | all-gather | bytes 139264 | tf_op jit(solution)/shard_map/all_gather | solution.py:86
  115.5 14.8 %all-to-all-start.1 = ((bf16[24,32,128]{2,0,1:T(8,128)(2,1)}), bf16[24,32,128]{2,0,1:T(8,128)(2,1)S(1)}, u32[]{:S(2)}, u32[]{:S(2)}) async-start(bf16[24,32,128]{2,0,1:T(8,128)(2,1)} %copy.27), calls=%async_computation.1 | async-start | bytes 393216 | tf_op jit(solution)/shard_map/all_to_all | solution.py:50
  131.0 0.5 fusion.23
  131.6 18.4 %all-to-all-done.1 = bf16[24,32,128]{2,0,1:T(8,128)(2,1)S(1)} async-done(((bf16[24,32,128]{2,0,1:T(8,128)(2,1)}), bf16[24,32,128]{2,0,1:T(8,128)(2,1)S(1)}, u32[]{:S(2)}, u32[]{:S(2)}) %all-to-all-start.1) | async-done | bytes 196640 | tf_op jit(solution)/shard_map/all_to_all | solution.py:50
  149.9 89.4 %while.15 = (s32[]{:T(128)}, f32[1,768,1]{1,2,0:T(1,128)S(1)}, f32[1,768,1]{1,2,0:T(1,128)S(1)}, f32[1,768,128]{2,1,0:T(8,128)S(1)}, s32[16]{0:T(128)S(1)}, /*in...) while((s32[]{:T(128)}, f32[1,768,1]{1,2,0:T(1,128)S(1)}, ...), condition=%wide.region_3.4_spmd.clone, body=%wide.region_0.3_spmd.clone.sunk | while | flops 308777472 | bytes 8506529 | solution.py:79
  149.9 0.6 dynamic_slice.33
  151.8 1.4 fusion.40
  153.8 1.7 fusion.44
  155.5 0.6 dynamic_slice.33
  157.4 1.4 fusion.40
  159.3 1.7 fusion.44
  161.1 0.6 dynamic_slice.33
  163.0 1.4 fusion.40
  164.9 1.7 fusion.44
  166.7 0.6 dynamic_slice.33
  168.6 1.4 fusion.40
  170.5 1.7 fusion.44
  172.3 0.6 dynamic_slice.33
  174.1 1.4 fusion.40
  176.1 1.7 fusion.44
  177.9 0.6 dynamic_slice.33
  179.7 1.4 fusion.40
  181.7 1.7 fusion.44
  183.5 0.6 dynamic_slice.33
  185.3 1.4 fusion.40
  187.3 1.7 fusion.44
  189.1 0.6 dynamic_slice.33
  190.9 1.4 fusion.40
  192.9 1.7 fusion.44
  194.7 0.6 dynamic_slice.33
  196.5 1.4 fusion.40
  198.5 1.7 fusion.44
  200.2 0.6 dynamic_slice.33
  202.1 1.4 fusion.40
  204.1 1.7 fusion.44
  205.8 0.6 dynamic_slice.33
  207.7 1.4 fusion.40
  209.7 1.7 fusion.44
  211.4 0.6 dynamic_slice.33
  213.3 1.4 fusion.40
  215.3 1.7 fusion.44
  217.0 0.6 dynamic_slice.33
  218.9 1.4 fusion.40
  220.9 1.7 fusion.44
  222.6 0.6 dynamic_slice.33
  224.5 1.4 fusion.40
  226.4 1.7 fusion.44
  228.2 0.6 dynamic_slice.33
  230.1 1.4 fusion.40
  232.0 1.7 fusion.44
  233.8 0.6 dynamic_slice.33
  235.7 1.4 fusion.40
  237.6 1.7 fusion.44
  239.6 21.8 %all_to_all.85 = bf16[32,24,128]{2,1,0:T(8,128)(2,1)S(1)} all-to-all(bf16[32,24,128]{2,1,0:T(8,128)(2,1)S(1)} %add_convert_fusion), channel_id=1, replica_groups=mesh['group'=16,'seq'=32] {'seq'}, dimensions={0} | all-to-all | bytes 393216 | tf_op jit(solution)/shard_map/all_to_all | solution.py:100
  261.5 0.8 broadcast_in_dim.39
  (99 shorter events, 9.8 us)
Async XLA Ops:
  6.5 62.1 %copy-start = (bf16[1,24,4096]{2,1,0:T(8,128)(2,1)S(1)}, bf16[1,24,4096]{2,1,0:T(8,128)(2,1)}, u32[]{:S(2)}) copy-start(bf16[1,24,4096]{2,1,0:T(8,128)(2,1)} %param.14) | copy-start | bytes 589828
  6.5 68.8 %copy-start.1 = (bf16[1,24,4096]{2,1,0:T(8,128)(2,1)S(1)}, bf16[1,24,4096]{2,1,0:T(8,128)(2,1)}, u32[]{:S(2)}) copy-start(bf16[1,24,4096]{2,1,0:T(8,128)(2,1)} %param.11) | copy-start | bytes 589828
  6.5 143.4 %all-gather.3.cloned.1.call-start = ((), (), s32[]{:S(2)}) async-start(), calls=%async_computation.5 | async-start | bytes 3342336 | tf_op jit(solution)/shard_map/all_gather | solution.py:61
  6.5 69.6 %copy-start.5 = (s32[16]{0:T(128)S(1)}, s32[16]{0:T(128)}, u32[]{:S(2)}) copy-start(s32[16]{0:T(128)} %param.18) | copy-start | bytes 196
  6.5 70.2 %copy-start.2 = (bf16[32,128]{1,0:T(8,128)(2,1)S(1)}, bf16[32,128]{1,0:T(8,128)(2,1)}, u32[]{:S(2)}) copy-start(bf16[32,128]{1,0:T(8,128)(2,1)} %param.16) | copy-start | bytes 24580
  6.5 92.2 %copy-start.3 = (bf16[32,128]{1,0:T(8,128)(2,1)S(1)}, bf16[32,128]{1,0:T(8,128)(2,1)}, u32[]{:S(2)}) copy-start(bf16[32,128]{1,0:T(8,128)(2,1)} %param.15) | copy-start | bytes 24580
  44.7 105.2 %all-gather.5.cloned.1.call-start = ((), (), s32[]{:S(2)}) async-start(), calls=%async_computation.6 | async-start | bytes 3342336 | tf_op jit(solution)/shard_map/all_gather | solution.py:62
  69.5 46.1 %all-to-all-start.3 = ((bf16[24,32,128]{2,0,1:T(8,128)(2,1)}), bf16[24,32,128]{2,0,1:T(8,128)(2,1)S(1)}, u32[]{:S(2)}, u32[]{:S(2)}) async-start(bf16[24,32,128]{2,0,1:T(8,128)(2,1)} %copy.31), calls=%async_computation.3 | async-start | bytes 393216 | tf_op jit(solution)/shard_map/all_to_all | solution.py:53
  115.5 34.4 %all-to-all-start.1 = ((bf16[24,32,128]{2,0,1:T(8,128)(2,1)}), bf16[24,32,128]{2,0,1:T(8,128)(2,1)S(1)}, u32[]{:S(2)}, u32[]{:S(2)}) async-start(bf16[24,32,128]{2,0,1:T(8,128)(2,1)} %copy.27), calls=%async_computation.1 | async-start | bytes 393216 | tf_op jit(solution)/shard_map/all_to_all | solution.py:50
  149.9 89.7 %copy-start.4 = (f32[1,128]{1,0:T(1,128)S(1)}, f32[1,128]{1,0:T(1,128)}, u32[]{:S(2)}) copy-start(f32[1,128]{1,0:T(1,128)} %param.17) | copy-start | bytes 1540
Sparse Core Ops, SparseCore 0:
  44.8 36.6 all-gather.2
  83.6 43.0 all-gather.4
where the time goes:
time: 274 us; the launch traced here: 269 us
  blocking collectives  120 us (44%)
  matrix products  51.3 us (19%)
  loops' own time  21.1 us (8%)
  starting transfers between devices  20.1 us (7%)
  waiting for transfers between devices  18.4 us (7%)
  local copies, waits for them, and re-layouts  14.6 us (5%)
  between operations  14.2 us (5%)
  other arithmetic  9.08 us (3%)
    all_to_all x1, blocking collectives, body(): lax.all_to_all(keys[0], 'seq', split_axis=1, concat_axis=0, tiled=True)  37 us
    dot_general x17, matrix products, attend_block(): jnp.einsum('hqk,khd->hqd', weights.astype(jnp.bfloat16), value_block, pre...  28.3 us
    dot_general x17, matrix products, attend_block(): jnp.einsum('qhd,khd->hqk', query_heads, key_block, preferred_element_type...  23 us
    all_to_all x1, blocking collectives, body(): lax.all_to_all(values[0], 'seq', split_axis=1, concat_axis=0, tiled=True)  22.8 us
    all_gather x1, blocking collectives, body(): text_value_piece = lax.all_gather(text_values, 'group', axis=0, tiled=True)  22 us
    all_to_all x1, blocking collectives, body(): lax.all_to_all(combined, 'seq', split_axis=0, concat_axis=1, tiled=True)  21.8 us
    another operation x1, loops' own time, body(): lax.scan(per_block, start_state(head_count, row_count, head_size), (key_b...  21.1 us
    all_to_all x1, waiting for transfers between devices, body(): lax.all_to_all(queries[0], 'seq', split_axis=1, concat_axis=0, tiled=True)  18.4 us
  transfers between devices with their start and end apart: 4, of which 1 were waited for; matrix products, arithmetic and copies ran while one was open for 2% of the time, Pallas kernels for 0%

commit v1 on v0

v1 whole, which is shorter than its diff:
```python
import functools
import math

import jax
import jax.numpy as jnp
from jax import lax
from jax.experimental import pallas as pl
from jax.experimental.pallas import tpu as pltpu
from jax.sharding import PartitionSpec as P

HD = 128
LOG2 = math.log2(math.e) / math.sqrt(HD)
LOW = -1e30
VMEM = pl.BlockSpec(memory_space=pltpu.VMEM)
SMEM = pl.BlockSpec(memory_space=pltpu.SMEM)
PARAMS = pltpu.CompilerParams(vmem_limit_bytes=40 * 2**20)


def core_of(i):
    return i + 1 - 2 * (i % 2)


def across_x(i):
    return (i + 8) % 16


def across_y1(i):
    y = (i // 2) % 4
    return i + 2 * (1 - 2 * (y % 2))


def across_y2(i):
    y = (i // 2) % 4
    return (i // 8) * 8 + ((y + 2 * (y % 2) + 3) % 4) * 2 + i % 2


def across_xy2(i):
    return across_x(across_y2(i))


def swap(array, partner):
    return lax.ppermute(array, "group", [(i, partner(i)) for i in range(16)])


def pack_kernel(q_ref, k_ref, v_ref, c_ref, out_ref):
    for head in range(out_ref.shape[0]):
        for slot, ref in enumerate((q_ref, k_ref, v_ref, c_ref)):
            out_ref[head, slot] = ref[0, :, head * HD : (head + 1) * HD]


def pack(queries, keys, values, cross_queries):
    rows, width = queries.shape[1:]
    return pl.pallas_call(
        pack_kernel,
        in_specs=[VMEM] * 4,
        out_specs=VMEM,
        out_shape=jax.ShapeDtypeStruct((width // HD, 4, rows, HD), jnp.bfloat16),
        compiler_params=PARAMS,
        name="pack",
    )(queries, keys, values, cross_queries)


def unpack_kernel(in_ref, q_ref, kv_ref, c_ref):
    for part in range(in_ref.shape[0]):
        q_ref[part] = in_ref[part, 0]
        kv_ref[0, part] = in_ref[part, 1]
        kv_ref[1, part] = in_ref[part, 2]
        c_ref[part] = in_ref[part, 3]


def unpack(received):
    parts, _, rows, width = received.shape
    one = jax.ShapeDtypeStruct((parts, rows, width), jnp.bfloat16)
    two = jax.ShapeDtypeStruct((2, parts, rows, width), jnp.bfloat16)
    q, kv, c = pl.pallas_call(
        unpack_kernel,
        in_specs=[VMEM],
        out_specs=[VMEM] * 3,
        out_shape=[one, two, one],
        compiler_params=PARAMS,
        name="unpack",
    )(received)
    count = parts * rows
    return q.reshape(count, width), kv.reshape(2, count, width), c.reshape(count, width)


def scores_of(q, k):
    return lax.dot_general(
        q, k, (((1,), (1,)), ((), ())), preferred_element_type=jnp.float32
    )


def with_ones(v):
    return jnp.concatenate([v, jnp.ones_like(v)], axis=1)


def attend(q_ref, k, v, top_ref, sum_ref, tile, mask=None):
    v = with_ones(v)
    count = q_ref.shape[0] // tile

    def soft(step, s):
        rows = pl.ds(step * tile, tile)
        if mask is not None:
            s = jnp.where(mask, s, LOW)
        old = top_ref[rows, :]
        new = jnp.maximum(old, jnp.max(s, axis=1, keepdims=True))
        p = jnp.exp2((s - new[:, :1]) * LOG2).astype(jnp.bfloat16)
        factor = jnp.exp2((old - new) * LOG2)
        top_ref[rows, :] = new
        return rows, p, jnp.concatenate([factor, factor], axis=1)

    def mix(rows, p, factor):
        sum_ref[rows, :] = sum_ref[rows, :] * factor + jnp.dot(
            p, v, preferred_element_type=jnp.float32
        )

    s = scores_of(q_ref[pl.ds(0, tile), :], k)
    last = None
    for step in range(count):
        ahead = None
        if step + 1 < count:
            ahead = scores_of(q_ref[pl.ds((step + 1) * tile, tile), :], k)
        now = soft(step, s)
        if last is not None:
            mix(*last)
        last, s = now, ahead
    mix(*last)


def attend_pair(q_ref, one_ref, two_ref, see_one, see_two, top_ref, sum_ref):
    @pl.when(see_one & see_two)
    def _():
        k = jnp.concatenate([one_ref[0], two_ref[0]], axis=0)
        v = jnp.concatenate([one_ref[1], two_ref[1]], axis=0)
        attend(q_ref, k, v, top_ref, sum_ref, 256)

    @pl.when(see_one & jnp.logical_not(see_two))
    def _():
        attend(q_ref, one_ref[0], one_ref[1], top_ref, sum_ref, 256)

    @pl.when(see_two & jnp.logical_not(see_one))
    def _():
        attend(q_ref, two_ref[0], two_ref[1], top_ref, sum_ref, 256)


def self_part(whose, ids_ref, q_ref, a0, a1, b0, b1, top_ref, sum_ref):
    slot = lax.axis_index("group")
    rank = ids_ref[whose(slot)]
    near = across_y1(slot)
    see = [ids_ref[j] <= rank for j in (slot, core_of(slot), near, core_of(near))]
    top_ref[...] = jnp.full_like(top_ref, LOW)
    sum_ref[...] = jnp.zeros_like(sum_ref)
    attend_pair(q_ref, a0, a1, see[0], see[1], top_ref, sum_ref)
    attend_pair(q_ref, b0, b1, see[2], see[3], top_ref, sum_ref)


def log_sums(top_ref, sum_ref):
    lines = []
    for step in range(top_ref.shape[0] // HD):
        rows = pl.ds(step * HD, HD)
        total = sum_ref[rows, HD:]
        line = jnp.where(total > 0, jnp.log2(total) + top_ref[rows, :] * LOG2, LOW)
        lines.append(line.T[0:1, :])
    lines.append(jnp.full((8 - len(lines), HD), LOW, jnp.float32))
    return jnp.concatenate(lines, axis=0)


def mean_of(sum_ref):
    total = sum_ref[:, HD:]
    return sum_ref[:, :HD] / jnp.where(total > 0, total, 1.0)


def other_kernel(whose, ids_ref, q_ref, a0, a1, b0, b1, out_ref, top_ref, sum_ref):
    self_part(whose, ids_ref, q_ref, a0, a1, b0, b1, top_ref, sum_ref)
    count = q_ref.shape[0]
    out_ref[pl.ds(0, count), :] = mean_of(sum_ref).astype(jnp.bfloat16)
    logs = log_sums(top_ref, sum_ref)
    high = logs.astype(jnp.bfloat16)
    rest = logs - high.astype(jnp.float32)
    mid = rest.astype(jnp.bfloat16)
    low = (rest - mid.astype(jnp.float32)).astype(jnp.bfloat16)
    tail = jnp.concatenate([high, mid, low, jnp.zeros_like(low)], axis=0)
    out_ref[pl.ds(count, 32), :] = tail


def own_kernel(
    ids_ref, len_ref, q_ref, a0, a1, b0, b1, c_ref, text_ref,
    mean_ref, logs_ref, cross_ref, top_ref, sum_ref,
):
    top_ref[...] = jnp.full_like(top_ref, LOW)
    sum_ref[...] = jnp.zeros_like(sum_ref)
    texts = text_ref.shape[0] * text_ref.shape[2]
    mask = lax.broadcasted_iota(jnp.int32, (1, texts), 1) < len_ref[0]
    attend(
        c_ref,
        text_ref[:, 0].reshape(texts, HD),
        text_ref[:, 1].reshape(texts, HD),
        top_ref,
        sum_ref,
        256,
        mask,
    )
    cross_ref[...] = mean_of(sum_ref)
    self_part(lambda i: i, ids_ref, q_ref, a0, a1, b0, b1, top_ref, sum_ref)
    mean_ref[...] = mean_of(sum_ref)
    logs_ref[...] = log_sums(top_ref, sum_ref)


def scratch(count):
    return [
        pltpu.VMEM((count, HD), jnp.float32),
        pltpu.VMEM((count, 2 * HD), jnp.float32),
    ]


COST = pl.CostEstimate(
    flops=16 * 768 * 768 * 128, bytes_accessed=2**21, transcendentals=4 * 768 * 768
)


def other(whose, group_ids, q, blocks):
    count = q.shape[0]
    return pl.pallas_call(
        functools.partial(other_kernel, whose),
        in_specs=[SMEM] + [VMEM] * 5,
        out_specs=VMEM,
        out_shape=jax.ShapeDtypeStruct((count + 32, HD), jnp.bfloat16),
        scratch_shapes=scratch(count),
        compiler_params=PARAMS,
        cost_estimate=COST,
        name="other",
    )(group_ids, q, *blocks)


def own(group_ids, text_len, q, blocks, cross, text):
    count = q.shape[0]
    full = jax.ShapeDtypeStruct((count, HD), jnp.float32)
    return pl.pallas_call(
        own_kernel,
        in_specs=[SMEM] * 2 + [VMEM] * 7,
        out_specs=[VMEM] * 3,
        out_shape=[full, jax.ShapeDtypeStruct((8, HD), jnp.float32), full],
        scratch_shapes=scratch(count),
        compiler_params=PARAMS,
        cost_estimate=COST,
        name="own",
    )(group_ids, text_len, q, *blocks, cross, text)


def merge_kernel(mean_ref, logs_ref, cross_ref, r0, r1, r2, gate_ref, out_ref):
    count = mean_ref.shape[0]
    logs = [logs_ref[...]]
    for ref in (r0, r1, r2):
        tail = ref[pl.ds(count, 32), :].astype(jnp.float32)
        logs.append(tail[0:8] + tail[8:16] + tail[16:24])
    best = functools.reduce(jnp.maximum, logs)
    weights = [jnp.exp2(line - best) for line in logs]
    total = functools.reduce(jnp.add, weights)
    weights = [w / total for w in weights]
    gate = gate_ref[...]
    for step in range(count // HD):
        rows = pl.ds(step * HD, HD)
        parts = [mean_ref[rows, :]]
        parts += [ref[rows, :].astype(jnp.float32) for ref in (r0, r1, r2)]
        mixed = None
        for w, part in zip(weights, parts):
            column = jnp.broadcast_to(w[step : step + 1, :], (HD, HD)).T
            mixed = column * part if mixed is None else mixed + column * part
        out_ref[rows, :] = (gate * mixed + cross_ref[rows, :]).astype(jnp.bfloat16)


def merge(mean, logs, cross, received, gate):
    return pl.pallas_call(
        merge_kernel,
        in_specs=[VMEM] * 7,
        out_specs=VMEM,
        out_shape=jax.ShapeDtypeStruct(mean.shape, jnp.bfloat16),
        compiler_params=PARAMS,
        name="merge",
    )(mean, logs, cross, *received, gate)


def gather_text(text_keys, text_values):
    both = jnp.stack([text_keys, text_values])
    return lax.all_gather(both, "group", axis=0)


def body(
    queries, keys, values, cross_queries, text_keys, text_values, group_gate, group_ids, text_len
):
    text = gather_text(text_keys, text_values)
    packed = pack(queries, keys, values, cross_queries)
    received = lax.all_to_all(packed, "seq", split_axis=0, concat_axis=0, tiled=True)
    q, kv, cross = unpack(received)
    kv_near = swap(kv, across_y1)
    q_xy, q_x, q_y = swap(q, across_xy2), swap(q, across_x), swap(q, across_y2)
    blocks = [kv, swap(kv, core_of), kv_near, swap(kv_near, core_of)]
    back = []
    for whose, rows in ((across_xy2, q_xy), (across_x, q_x), (across_y2, q_y)):
        back.append(swap(other(whose, group_ids, rows, blocks), whose))
    mean, logs, crossed = own(group_ids, text_len, q, blocks, cross, text)
    mixed = merge(mean, logs, crossed, back, group_gate)
    count = mixed.shape[0]
    heads = lax.axis_size("seq")
    mixed = lax.all_to_all(
        mixed.reshape(heads, count // heads, HD), "seq", split_axis=0, concat_axis=0, tiled=True
    )
    return jnp.transpose(mixed, (1, 0, 2)).reshape(1, count // heads, heads * HD)


def solution(mesh):
    return jax.shard_map(
        body,
        mesh=mesh,
        in_specs=(
            P("group", "seq", None),
            P("group", "seq", None),
            P("group", "seq", None),
            P("group", "seq", None),
            P("group", "seq"),
            P("group", "seq"),
            P("group", "seq"),
            P(),
            P(),
        ),
        out_specs=P("group", "seq", None),
        check_vma=False,
    )
```

time: 274 us -> 167 us (0.61); the launches traced: 269 us -> 167 us
  matrix products: 51.3 us -> 0 us
  loops' own time: 21.1 us -> 0 us
  starting transfers between devices: 20.1 us -> 37 us
  waiting for transfers between devices: 18.4 us -> 4.08 us
  between operations: 14.2 us -> 0.89 us
  Pallas kernels: 0 us -> 12.1 us
  blocking collectives: 120 us -> 108 us
  local copies, waits for them, and re-layouts: 14.6 us -> 5.16 us
  other arithmetic: 9.08 us -> 0.01 us
    dot_general x34 -> x0, matrix products: 51.3 us -> none  [the longest x17 28.3 us: attend_block(): jnp.einsum('hqk,khd->hqd', weights.astype(jnp.bfloat16), value_block, pre...]
    ppermute x0 -> x9, starting transfers between devices: none -> 37 us  [swap(): return lax.ppermute(array, 'group', [(i, partner(i)) for i in range(16)])]
    another operation x1 -> x0, loops' own time: 21.1 us -> none  [body(): lax.scan(per_block, start_state(head_count, row_count, head_size), (key_b...]
    all_to_all x2 -> x0, starting transfers between devices: 20.1 us -> none  [the longest x1 14.8 us: body(): lax.all_to_all(queries[0], 'seq', split_axis=1, concat_axis=0, tiled=True)]
    all_gather x2 -> x1, blocking collectives: 38.7 us -> 20.2 us  [gather_text(): return lax.all_gather(both, 'group', axis=0)]
    all_to_all x2 -> x0, waiting for transfers between devices: 18.4 us -> none  [the longest x1 18.4 us: body(): lax.all_to_all(queries[0], 'seq', split_axis=1, concat_axis=0, tiled=True)]
    pallas_call x0 -> x7, Pallas kernels: none -> 12.1 us  [the longest x3 5.81 us: other(): pl.pallas_call(functools.partial(other_kernel, whose), in_specs=[SMEM] +...]
    dynamic_slice x17 -> x0, local copies, waits for them, and re-layouts: 10 us -> none  [the longest x16 9.42 us: body(): lax.scan(per_block, start_state(head_count, row_count, head_size), (key_b...]
  transfers between devices with their start and end apart: 4 -> 9, of which waited for: 1 -> 1; matrix products, arithmetic and copies ran while one was open for 2% -> 0% of each run, Pallas kernels for 0% -> 7%
where the time goes in v1:
time: 167 us
  blocking collectives  108 us (65%)
  starting transfers between devices  37 us (22%)
  Pallas kernels  12.1 us (7%)
  local copies, waits for them, and re-layouts  5.16 us (3%)
  waiting for transfers between devices  4.08 us (2%)
    all_to_all x1, blocking collectives, body(): lax.all_to_all(packed, 'seq', split_axis=0, concat_axis=0, tiled=True)  60.1 us
    ppermute x9, starting transfers between devices, swap(): return lax.ppermute(array, 'group', [(i, partner(i)) for i in range(16)])  37 us
    all_to_all x1, blocking collectives, body(): lax.all_to_all(mixed.reshape(heads, count // heads, HD), 'seq', split_axi...  27.4 us
    all_gather x1, blocking collectives, gather_text(): return lax.all_gather(both, 'group', axis=0)  20.2 us
    pallas_call x3, Pallas kernels, other(): pl.pallas_call(functools.partial(other_kernel, whose), in_specs=[SMEM] +...  5.81 us
    pallas_call x1, Pallas kernels, own(): pl.pallas_call(own_kernel, in_specs=[SMEM] * 2 + [VMEM] * 7, out_specs=[V...  5.58 us
    unnamed x16, local copies, waits for them, and re-layouts  4.37 us
    ppermute x9, waiting for transfers between devices, swap(): return lax.ppermute(array, 'group', [(i, partner(i)) for i in range(16)])  4.08 us
  transfers between devices with their start and end apart: 9, of which 1 were waited for; matrix products, arithmetic and copies ran while one was open for 0% of the time, Pallas kernels for 7%

profile of v1, /device:TPU:1, one launch (start us, length us, event | category | flops | bytes accessed | tf_op | source)
XLA Modules:
  0.0 166.9 jit_solution(3398156292525780641)
XLA Ops:
  0.0 0.0 copy-start
  0.0 0.9 copy-done
  0.9 0.0 copy-start.1
  0.9 0.9 copy-done.1
  1.9 0.0 copy-start.2
  1.9 0.9 copy-done.2
  2.8 0.0 copy-start.3
  2.8 0.9 copy-done.3
  3.7 0.1 pack.1
  3.9 60.1 %all_to_all.10.in_ref = bf16[32,4,24,128]{3,2,1,0:T(8,128)(2,1)S(1)} all-to-all(bf16[32,4,24,128]{3,2,1,0:T(8,128)(2,1)S(1)} %pack.1), channel_id=1, replica_groups=mesh['group'=16,'seq'=32] {'seq'}, dimensions={0} | all-to-all | bytes 1572864 | tf_op jit(solution)/shard_map/all_to_all | solution.py:293
  63.9 0.0 copy-start.7
  63.9 0.1 unpack.1
  64.0 0.0 copy-start.6
  64.0 3.2 %collective-permute-start.1 = (bf16[2,768,128]{2,1,0:T(8,128)(2,1)S(1)}, bf16[2,768,128]{2,1,0:T(8,128)(2,1)S(1)}, u32[]{:S(2)}, u32[]{:S(2)}) collective-permute-start(bf16[2,768,128]{2,1,0:T(8,128)(2,1)S(1)} %bitcast.10), channel_id=1, source_target_pairs={{0,64},{32,96},{64,0},{96,32},{128,192},{160,224},{192,128},{224,1... | collective-permute-start | bytes 1179656 | tf_op jit(solution)/shard_map/ppermute | solution.py:42
  67.2 3.7 %collective-permute-start = (bf16[2,768,128]{2,1,0:T(8,128)(2,1)S(1)}, bf16[2,768,128]{2,1,0:T(8,128)(2,1)S(1)}, u32[]{:S(2)}, u32[]{:S(2)}) collective-permute-start(bf16[2,768,128]{2,1,0:T(8,128)(2,1)S(1)} %bitcast.11), channel_id=1, source_target_pairs={{0,32},{32,0},{64,96},{96,64},{128,160},{160,128},{192,224},{224,1... | collective-permute-start | bytes 1179656 | tf_op jit(solution)/shard_map/ppermute | solution.py:42
  70.9 4.1 %collective-permute-done.1.b0 = bf16[2,768,128]{2,1,0:T(8,128)(2,1)S(1)} collective-permute-done((bf16[2,768,128]{2,1,0:T(8,128)(2,1)S(1)}, bf16[2,768,128]{2,1,0:T(8,128)(2,1)S(1)}, u32[]{:S(2)}, u32[]{:S(2)}) %collective-permute-start.1) | collective-permute-done | bytes 393248 | tf_op jit(solution)/shard_map/ppermute | solution.py:42
  75.0 4.3 %collective-permute-start.2 = (bf16[2,768,128]{2,1,0:T(8,128)(2,1)S(1)}, bf16[2,768,128]{2,1,0:T(8,128)(2,1)S(1)}, u32[]{:S(2)}, u32[]{:S(2)}) collective-permute-start(bf16[2,768,128]{2,1,0:T(8,128)(2,1)S(1)} %collective-permute-done.1.b0), channel_id=1, source_target_pairs={{0,32},{32,0},{64,96},{96,64},{128,160},{160,128},{192,224},{224,1... | collective-permute-start | bytes 1179656 | tf_op jit(solution)/shard_map/ppermute | solution.py:42
  79.3 4.6 %collective-permute-start.7 = (bf16[768,128]{1,0:T(8,128)(2,1)S(1)}, bf16[768,128]{1,0:T(8,128)(2,1)S(1)}, u32[]{:S(2)}, u32[]{:S(2)}) collective-permute-start(bf16[768,128]{1,0:T(8,128)(2,1)S(1)} %bitcast.16), channel_id=1, source_target_pairs={{0,192},{32,224},{64,128},{96,160},{128,64},{160,96},{192,0},{224,... | collective-permute-start | bytes 589832 | tf_op jit(solution)/shard_map/ppermute | solution.py:42
  84.6 2.2 %collective-permute-start.5 = (bf16[768,128]{1,0:T(8,128)(2,1)S(1)}, bf16[768,128]{1,0:T(8,128)(2,1)S(1)}, u32[]{:S(2)}, u32[]{:S(2)}) collective-permute-start(bf16[768,128]{1,0:T(8,128)(2,1)S(1)} %bitcast.17), channel_id=1, source_target_pairs={{0,256},{32,288},{64,320},{96,352},{128,384},{160,416},{192,448},{... | collective-permute-start | bytes 589832 | tf_op jit(solution)/shard_map/ppermute | solution.py:42
  86.9 0.0 copy-done.7
  86.9 0.0 copy-done.6
  86.9 0.0 copy-start.5
  86.9 2.8 %collective-permute-start.3 = (bf16[768,128]{1,0:T(8,128)(2,1)S(1)}, bf16[768,128]{1,0:T(8,128)(2,1)S(1)}, u32[]{:S(2)}, u32[]{:S(2)}) collective-permute-start(bf16[768,128]{1,0:T(8,128)(2,1)S(1)} %bitcast.18), channel_id=1, source_target_pairs={{0,448},{32,480},{64,384},{96,416},{128,320},{160,352},{192,256},{... | collective-permute-start | bytes 589832 | tf_op jit(solution)/shard_map/ppermute | solution.py:42
  89.7 0.0 collective-permute-done.7.q_ref
  89.7 0.0 collective-permute-done.a1
  89.7 0.0 collective-permute-done.2.b1
  89.7 0.0 copy-done.5
  89.7 0.8 other.5
  90.5 8.0 %collective-permute-start.8 = (bf16[800,128]{1,0:T(8,128)(2,1)S(1)}, bf16[800,128]{1,0:T(8,128)(2,1)S(1)}, u32[]{:S(2)}, u32[]{:S(2)}) collective-permute-start(bf16[800,128]{1,0:T(8,128)(2,1)S(1)} %other.5), channel_id=1, source_target_pairs={{0,192},{32,224},{64,128},{96,160},{128,64},{160,96},{192,0},{224,... | collective-permute-start | bytes 614408 | tf_op jit(solution)/shard_map/ppermute | solution.py:42
  98.6 0.0 collective-permute-done.5.q_ref
  98.6 4.0 %other.4 = bf16[800,128]{1,0:T(8,128)(2,1)S(1)} custom-call(s32[16]{0:T(128)S(1)} %copy-done.5, bf16[768,128]{1,0:T(8,128)(2,1)S(1)} %collective-permute-done.5.q_ref, bf16[2,768,128]{2,1,0:T(8,128)(2,1)S(1)} %bitcast.13, bf16[2,768,128]{2,1,0:T(8,128)(2,1)S(1)} %collective-permute-done.a1, bf16[2,768,128]{2,1,0:T(8,128)(2,1)S(1)} %collective-permute-done.1.b0, ...), custom_call_target="tpu_custom_call" | custom-call | flops 1207959552 | bytes 2097152 | tf_op jit(solution)/shard_map/other/pallas_call | solution.py:223
  102.6 2.2 %collective-permute-start.6 = (bf16[800,128]{1,0:T(8,128)(2,1)S(1)}, bf16[800,128]{1,0:T(8,128)(2,1)S(1)}, u32[]{:S(2)}, u32[]{:S(2)}) collective-permute-start(bf16[800,128]{1,0:T(8,128)(2,1)S(1)} %other.4), channel_id=1, source_target_pairs={{0,256},{32,288},{64,320},{96,352},{128,384},{160,416},{192,448},{... | collective-permute-start | bytes 614408 | tf_op jit(solution)/shard_map/ppermute | solution.py:42
  104.8 0.0 collective-permute-done.3.q_ref
  104.8 1.0 other.3
  105.9 5.8 %collective-permute-start.4 = (bf16[800,128]{1,0:T(8,128)(2,1)S(1)}, bf16[800,128]{1,0:T(8,128)(2,1)S(1)}, u32[]{:S(2)}, u32[]{:S(2)}) collective-permute-start(bf16[800,128]{1,0:T(8,128)(2,1)S(1)} %other.3), channel_id=1, source_target_pairs={{0,448},{32,480},{64,384},{96,416},{128,320},{160,352},{192,256},{... | collective-permute-start | bytes 614408 | tf_op jit(solution)/shard_map/ppermute | solution.py:42
  111.7 20.2 %all-gather = bf16[32,32,128]{2,1,0:T(8,128)(2,1)S(1)} all-gather(bf16[2,32,128]{2,1,0:T(8,128)(2,1)S(1)} %pad_maximum_fusion), channel_id=2, replica_groups=mesh['group'=16,'seq'=32] {'group'}, dimensions={0}, use_global_device_ids=true | all-gather | bytes 278528 | tf_op jit(solution)/shard_map/all_gather | solution.py:285
  131.8 5.6 %own.1 = (f32[768,128]{1,0:T(8,128)S(1)}, f32[8,128]{1,0:T(8,128)S(1)}, f32[768,128]{1,0:T(8,128)S(1)}) custom-call(s32[16]{0:T(128)S(1)} %copy-done.5, s32[1]{0:T(128)S(6)} %copy.12.len_ref, bf16[768,128]{1,0:T(8,128)(2,1)S(1)} %bitcast.19, bf16[2,768,128]{2,1,0:T(8,128)(2,1)S(1)} %bitcast.15, bf16[2,768,128]{2,1,0:T(8,128)(2,1)S(1)} %collective-permute-done.a1, ...), custom_call_target="tpu_custom_call" | custom-call | flops 1207959552 | bytes 2097152 | tf_op jit(solution)/shard_map/own/pallas_call | solution.py:238
  137.4 0.0 collective-permute-done.8.r2
  137.4 0.0 collective-permute-done.6.r1
  137.5 0.0 collective-permute-done.4.r0
  137.5 0.0 copy-start.4
  137.5 0.6 copy-done.4
  138.1 0.5 merge.1
  138.6 27.4 %all_to_all.11 = bf16[32,24,128]{2,1,0:T(8,128)(2,1)S(1)} all-to-all(bf16[32,24,128]{2,1,0:T(8,128)(2,1)S(1)} %bitcast.8), channel_id=1, replica_groups=mesh['group'=16,'seq'=32] {'seq'}, dimensions={0} | all-to-all | bytes 393216 | tf_op jit(solution)/shard_map/all_to_all | solution.py:305
  166.1 0.8 reshape.19
  (2 shorter events, 0.0 us)
Async XLA Ops:
  0.0 0.9 copy-start
  0.9 0.9 copy-start.1
  1.9 0.9 copy-start.2
  2.8 0.9 copy-start.3
  63.9 22.9 %copy-start.7 = (bf16[32,128]{1,0:T(8,128)(2,1)S(1)}, bf16[32,128]{1,0:T(8,128)(2,1)}, u32[]{:S(2)}) copy-start(bf16[32,128]{1,0:T(8,128)(2,1)} %param.13) | copy-start | bytes 24580
  64.0 22.9 %copy-start.6 = (bf16[32,128]{1,0:T(8,128)(2,1)S(1)}, bf16[32,128]{1,0:T(8,128)(2,1)}, u32[]{:S(2)}) copy-start(bf16[32,128]{1,0:T(8,128)(2,1)} %param.14) | copy-start | bytes 24580
  64.0 11.0 %collective-permute-start.1 = (bf16[2,768,128]{2,1,0:T(8,128)(2,1)S(1)}, bf16[2,768,128]{2,1,0:T(8,128)(2,1)S(1)}, u32[]{:S(2)}, u32[]{:S(2)}) collective-permute-start(bf16[2,768,128]{2,1,0:T(8,128)(2,1)S(1)} %bitcast.10), channel_id=1, source_target_pairs={{0,64},{32,96},{64,0},{96,32},{128,192},{160,224},{192,128},{224,1... | collective-permute-start | bytes 1179656 | tf_op jit(solution)/shard_map/ppermute | solution.py:42
  67.2 22.5 %collective-permute-start = (bf16[2,768,128]{2,1,0:T(8,128)(2,1)S(1)}, bf16[2,768,128]{2,1,0:T(8,128)(2,1)S(1)}, u32[]{:S(2)}, u32[]{:S(2)}) collective-permute-start(bf16[2,768,128]{2,1,0:T(8,128)(2,1)S(1)} %bitcast.11), channel_id=1, source_target_pairs={{0,32},{32,0},{64,96},{96,64},{128,160},{160,128},{192,224},{224,1... | collective-permute-start | bytes 1179656 | tf_op jit(solution)/shard_map/ppermute | solution.py:42
  75.0 14.7 %collective-permute-start.2 = (bf16[2,768,128]{2,1,0:T(8,128)(2,1)S(1)}, bf16[2,768,128]{2,1,0:T(8,128)(2,1)S(1)}, u32[]{:S(2)}, u32[]{:S(2)}) collective-permute-start(bf16[2,768,128]{2,1,0:T(8,128)(2,1)S(1)} %collective-permute-done.1.b0), channel_id=1, source_target_pairs={{0,32},{32,0},{64,96},{96,64},{128,160},{160,128},{192,224},{224,1... | collective-permute-start | bytes 1179656 | tf_op jit(solution)/shard_map/ppermute | solution.py:42
  79.3 10.4 %collective-permute-start.7 = (bf16[768,128]{1,0:T(8,128)(2,1)S(1)}, bf16[768,128]{1,0:T(8,128)(2,1)S(1)}, u32[]{:S(2)}, u32[]{:S(2)}) collective-permute-start(bf16[768,128]{1,0:T(8,128)(2,1)S(1)} %bitcast.16), channel_id=1, source_target_pairs={{0,192},{32,224},{64,128},{96,160},{128,64},{160,96},{192,0},{224,... | collective-permute-start | bytes 589832 | tf_op jit(solution)/shard_map/ppermute | solution.py:42
  84.6 14.0 %collective-permute-start.5 = (bf16[768,128]{1,0:T(8,128)(2,1)S(1)}, bf16[768,128]{1,0:T(8,128)(2,1)S(1)}, u32[]{:S(2)}, u32[]{:S(2)}) collective-permute-start(bf16[768,128]{1,0:T(8,128)(2,1)S(1)} %bitcast.17), channel_id=1, source_target_pairs={{0,256},{32,288},{64,320},{96,352},{128,384},{160,416},{192,448},{... | collective-permute-start | bytes 589832 | tf_op jit(solution)/shard_map/ppermute | solution.py:42
  86.9 2.9 %copy-start.5 = (s32[16]{0:T(128)S(1)}, s32[16]{0:T(128)}, u32[]{:S(2)}) copy-start(s32[16]{0:T(128)} %ids_ref.7) | copy-start | bytes 196
  86.9 17.9 %collective-permute-start.3 = (bf16[768,128]{1,0:T(8,128)(2,1)S(1)}, bf16[768,128]{1,0:T(8,128)(2,1)S(1)}, u32[]{:S(2)}, u32[]{:S(2)}) collective-permute-start(bf16[768,128]{1,0:T(8,128)(2,1)S(1)} %bitcast.18), channel_id=1, source_target_pairs={{0,448},{32,480},{64,384},{96,416},{128,320},{160,352},{192,256},{... | collective-permute-start | bytes 589832 | tf_op jit(solution)/shard_map/ppermute | solution.py:42
  90.5 46.9 %collective-permute-start.8 = (bf16[800,128]{1,0:T(8,128)(2,1)S(1)}, bf16[800,128]{1,0:T(8,128)(2,1)S(1)}, u32[]{:S(2)}, u32[]{:S(2)}) collective-permute-start(bf16[800,128]{1,0:T(8,128)(2,1)S(1)} %other.5), channel_id=1, source_target_pairs={{0,192},{32,224},{64,128},{96,160},{128,64},{160,96},{192,0},{224,... | collective-permute-start | bytes 614408 | tf_op jit(solution)/shard_map/ppermute | solution.py:42
  102.6 34.8 %collective-permute-start.6 = (bf16[800,128]{1,0:T(8,128)(2,1)S(1)}, bf16[800,128]{1,0:T(8,128)(2,1)S(1)}, u32[]{:S(2)}, u32[]{:S(2)}) collective-permute-start(bf16[800,128]{1,0:T(8,128)(2,1)S(1)} %other.4), channel_id=1, source_target_pairs={{0,256},{32,288},{64,320},{96,352},{128,384},{160,416},{192,448},{... | collective-permute-start | bytes 614408 | tf_op jit(solution)/shard_map/ppermute | solution.py:42
  105.9 31.6 %collective-permute-start.4 = (bf16[800,128]{1,0:T(8,128)(2,1)S(1)}, bf16[800,128]{1,0:T(8,128)(2,1)S(1)}, u32[]{:S(2)}, u32[]{:S(2)}) collective-permute-start(bf16[800,128]{1,0:T(8,128)(2,1)S(1)} %other.3), channel_id=1, source_target_pairs={{0,448},{32,480},{64,384},{96,416},{128,320},{160,352},{192,256},{... | collective-permute-start | bytes 614408 | tf_op jit(solution)/shard_map/ppermute | solution.py:42
  137.5 0.7 copy-start.4

commit v2 on v0

v2 whole, which is shorter than its diff:
```python
import functools
import math

import jax
import jax.numpy as jnp
from jax import lax
from jax.experimental import pallas as pl
from jax.experimental.pallas import tpu as pltpu
from jax.sharding import PartitionSpec as P

HD = 128
LOG2 = math.log2(math.e) / math.sqrt(HD)
LOW = -1e30
VMEM = pl.BlockSpec(memory_space=pltpu.VMEM)
SMEM = pl.BlockSpec(memory_space=pltpu.SMEM)
PARAMS = pltpu.CompilerParams(vmem_limit_bytes=24 * 2**20)


SMALL, LARGE = 2.0**-60, 2.0**90
TILE = 384


def core_of(i):
    return i + 1 - 2 * (i % 2)


def across_x(i):
    return (i + 8) % 16


def across_y1(i):
    y = (i // 2) % 4
    return i + 2 * (1 - 2 * (y % 2))


def across_y2(i):
    y = (i // 2) % 4
    return (i // 8) * 8 + ((y + 2 * (y % 2) + 3) % 4) * 2 + i % 2


def across_xy2(i):
    return across_x(across_y2(i))


def swap(array, partner):
    return lax.ppermute(array, "group", [(i, partner(i)) for i in range(16)])


CHUNKS = 4


def pack_kernel(q_hbm, k_hbm, v_hbm, c_hbm, out_ref, held, sems):
    sources = (q_hbm, k_hbm, v_hbm, c_hbm)
    heads = out_ref.shape[0]
    chunk = heads // CHUNKS * HD
    copies = []
    for slot, ref in enumerate(sources):
        for part in range(CHUNKS):
            where = pl.ds(part * chunk, chunk)
            copy = pltpu.make_async_copy(
                ref.at[0, :, where], held.at[slot, :, where], sems.at[slot, part]
            )
            copy.start()
            copies.append(copy)
    for slot in range(len(sources)):
        for part in range(CHUNKS):
            copies[slot * CHUNKS + part].wait()
            for head in range(part * heads // CHUNKS, (part + 1) * heads // CHUNKS):
                out_ref[head, slot] = held[slot, :, head * HD : (head + 1) * HD]


def pack(queries, keys, values, cross_queries):
    rows, width = queries.shape[1:]
    heads = width // HD
    return pl.pallas_call(
        pack_kernel,
        in_specs=[pl.BlockSpec(memory_space=pl.ANY)] * 4,
        out_specs=VMEM,
        out_shape=jax.ShapeDtypeStruct((heads, 4, rows, HD), jnp.bfloat16),
        scratch_shapes=[
            pltpu.VMEM((4, rows, width), jnp.bfloat16),
            pltpu.SemaphoreType.DMA((4, CHUNKS)),
        ],
        compiler_params=pltpu.CompilerParams(vmem_limit_bytes=56 * 2**20),
        name="pack",
    )(queries, keys, values, cross_queries)


def unpack_kernel(in_ref, tk_ref, tv_ref, gate_in, q_ref, kv_ref, c_ref, gate_ref, v_ref):
    gate_ref[...] = gate_in[...]
    parts, _, rows, _ = in_ref.shape
    count = parts * rows

    @pl.loop(0, parts // 2)
    def _(part):
        pair = pl.ds(pl.multiple_of(part * 2 * rows, 16), 2 * rows)

        def both(slot):
            return jnp.concatenate(
                [in_ref[2 * part, slot], in_ref[2 * part + 1, slot]], axis=0
            )

        q_ref[pair, :] = both(0)
        kv_ref[0, pair, :] = both(1)
        v_ref[pair, :] = both(2)
        c_ref[pair, :] = both(3)

    @pl.loop(0, count // HD)
    def _(block):
        where = pl.ds(pl.multiple_of(block * HD, HD), HD)
        kv_ref[1, where, :] = v_ref[where, :].T

    tail = pl.ds(count, tk_ref.shape[0])
    kv_ref[0, tail, :] = tk_ref[...]
    kv_ref[1, tail, :] = tv_ref[...]


def unpack(received, text_keys, text_values, gate):
    parts, _, rows, width = received.shape
    count = parts * rows
    one = jax.ShapeDtypeStruct((count, width), jnp.bfloat16)
    two = jax.ShapeDtypeStruct((2, count + text_keys.shape[0], width), jnp.bfloat16)
    return pl.pallas_call(
        unpack_kernel,
        in_specs=[VMEM] * 4,
        out_specs=[VMEM] * 4,
        out_shape=[one, two, one, jax.ShapeDtypeStruct(gate.shape, gate.dtype)],
        scratch_shapes=[pltpu.VMEM((count, width), jnp.bfloat16)],
        compiler_params=PARAMS,
        name="unpack",
    )(received, text_keys, text_values, gate)


def join_kernel(a_ref, b_ref, out_ref):
    @pl.loop(0, a_ref.shape[0] // 32)
    def _(step):
        rows = pl.ds(pl.multiple_of(step * 32, 32), 32)
        out_ref[0, rows, :] = a_ref[rows, :]
        out_ref[1, rows, :] = b_ref[rows, :]


def join(a, b):
    rows = a.size // HD
    out = pl.pallas_call(
        join_kernel,
        in_specs=[VMEM] * 2,
        out_specs=VMEM,
        out_shape=jax.ShapeDtypeStruct((2, rows, HD), a.dtype),
        compiler_params=PARAMS,
        name="join",
    )(a.reshape(rows, HD), b.reshape(rows, HD))
    return out.reshape((2,) + a.shape)


def scores_of(k, q):
    return lax.dot_general(
        k, q, (((1,), (1,)), ((), ())), preferred_element_type=jnp.float32
    )


def with_ones(v):
    return jnp.concatenate([v, jnp.ones((16, v.shape[1]), v.dtype)], axis=0)


def features_first(v_blocks):
    count = v_blocks.shape[0] // HD
    return jnp.concatenate([v_blocks[i * HD : (i + 1) * HD] for i in range(count)], axis=1)


def key_groups(slot):
    near = across_y1(slot)
    return slot, core_of(slot), near, core_of(near)


def self_part(ids_ref, sources, mine, theirs, refs):
    q_ref, k_ref, v_ref, top_ref, sum_ref, s_even, s_odd, list_ref = refs
    slot = lax.axis_index("group")
    count = k_ref.shape[1]
    halves = count // TILE
    for place, (_, ref) in enumerate(sources):
        q_ref[place] = ref[...]

    @pl.loop(0, 2)
    def _(side):
        for place, ref in enumerate((mine, theirs)):
            k_ref[2 * side + place] = ref[side, 0, pl.ds(0, count), :]
            v_ref[2 * side + place] = with_ones(
                features_first(ref[side, 1, pl.ds(0, count), :])
            )

    def queries(place, half):
        return q_ref[place, pl.ds(half * TILE, TILE), :]

    @pl.loop(0, len(sources))
    def _(place):
        for half in range(halves):
            s = scores_of(k_ref[0, pl.ds(0, HD), :], queries(place, half))
            top_ref[place, half] = jnp.max(s, axis=0, keepdims=True)
            sum_ref[place, half] = jnp.zeros_like(sum_ref[place, half])

    list_ref[0] = 0
    length = jnp.int32(0)
    seen = []
    for place, (owner, _) in enumerate(sources):
        rank = ids_ref[owner(slot)]
        before = length
        for number, group in enumerate(key_groups(slot)):
            list_ref[length] = 4 * place + number
            length = length + (ids_ref[group] <= rank).astype(jnp.int32)
        seen.append(length > before)

    def mix(place, number, half, s):
        p = jnp.exp2((s - top_ref[place, half]) * LOG2).astype(jnp.bfloat16)
        sum_ref[place, half] += jnp.dot(
            v_ref[number], p, preferred_element_type=jnp.float32
        )

    def item(index):
        code = list_ref[index]
        return code // 4, code % 4

    place, number = item(0)
    s_even[...] = scores_of(k_ref[number], queries(place, 0))

    @pl.loop(0, length)
    def _(index):
        place, number = item(index)
        s_odd[...] = scores_of(k_ref[number], queries(place, 1))
        mix(place, number, 0, s_even[...])
        next_place, next_number = item(jnp.minimum(index + 1, length - 1))
        s_even[...] = scores_of(k_ref[next_number], queries(next_place, 0))
        mix(place, number, 1, s_odd[...])

    inside = jnp.bool_(True)
    for place, some in enumerate(seen):
        totals = sum_ref[place, :, HD : HD + 1, :]
        good = (jnp.min(totals) > SMALL) & (jnp.max(totals) < LARGE)
        inside = inside & (good | jnp.logical_not(some))

    @pl.when(jnp.logical_not(inside))
    def _():
        top_ref[...] = jnp.full_like(top_ref, LOW)
        sum_ref[...] = jnp.zeros_like(sum_ref)

        @pl.loop(0, length * halves)
        def _(index):
            place, number = item(index // halves)
            half = index % halves
            where = pl.ds(pl.multiple_of(half * TILE, TILE), TILE)
            s = scores_of(k_ref[number], q_ref[place, where, :])
            old = top_ref[place, half]
            new = jnp.maximum(old, jnp.max(s, axis=0, keepdims=True))
            top_ref[place, half] = new
            sum_ref[place, half] = sum_ref[place, half] * jnp.exp2((old - new) * LOG2)
            mix(place, number, half, s)


def log_sums(place, top_ref, sum_ref):
    lines = []
    for half in range(top_ref.shape[1]):
        total = sum_ref[place, half, HD : HD + 1, :]
        logs = jnp.where(total > 0, jnp.log2(total) + top_ref[place, half] * LOG2, LOW)
        lines += [logs[:, start : start + HD] for start in range(0, TILE, HD)]
    lines.append(jnp.full((8 - len(lines), HD), LOW, jnp.float32))
    return jnp.concatenate(lines, axis=0)


def means(sums, write):
    for start in range(0, TILE, HD):
        total = sums[HD : HD + 1, start : start + HD]
        part = sums[:HD, start : start + HD] / jnp.where(total > 0, total, 1.0)
        write(start, part.T)


OTHERS = (across_x, across_y2, across_xy2)


def others_kernel(ids_ref, x_ref, y_ref, mine, theirs, out_x, out_y, out_xy, *refs):
    queries = (x_ref, y_ref.at[0], y_ref.at[1])
    self_part(ids_ref, list(zip(OTHERS, queries)), mine, theirs, refs)
    top_ref, sum_ref = refs[3:5]
    count = x_ref.shape[0]
    texts = mine.shape[2] - count
    for place, out_ref in enumerate((out_x, out_y, out_xy)):

        @pl.loop(0, count // TILE)
        def _(half):
            def write(start, part):
                where = pl.ds(pl.multiple_of(half * TILE + start, HD), HD)
                out_ref[where, :] = part.astype(jnp.bfloat16)

            means(sum_ref[place, half], write)

        logs = log_sums(place, top_ref, sum_ref)
        high = logs.astype(jnp.bfloat16)
        rest = logs - high.astype(jnp.float32)
        mid = rest.astype(jnp.bfloat16)
        low = (rest - mid.astype(jnp.float32)).astype(jnp.bfloat16)
        tail = jnp.concatenate([high, mid, low, jnp.zeros_like(low)], axis=0)
        out_ref[pl.ds(count, 32), :] = tail
        for piece in range(8):
            ref = (mine, theirs)[piece // 2 % 2]
            text = ref[piece // 4, piece % 2, pl.ds(count, texts), :]
            out_ref[pl.ds(count + 32 + piece * texts, texts), :] = text


def own_kernel(ids_ref, q_ref, mine, theirs, mean_ref, logs_ref, *refs):
    self_part(ids_ref, [(lambda i: i, q_ref)], mine, theirs, refs)
    top_ref, sum_ref = refs[3:5]

    @pl.loop(0, q_ref.shape[0] // TILE)
    def _(half):
        def write(start, part):
            where = pl.ds(pl.multiple_of(half * TILE + start, HD), HD)
            mean_ref[where, :] = part

        means(sum_ref[0, half], write)

    logs_ref[...] = log_sums(0, top_ref, sum_ref)


def scratch(places, count):
    halves = count // TILE
    return [
        pltpu.VMEM((places, count, HD), jnp.bfloat16),
        pltpu.VMEM((4, count, HD), jnp.bfloat16),
        pltpu.VMEM((4, HD + 16, count), jnp.bfloat16),
        pltpu.VMEM((places, halves, 1, TILE), jnp.float32),
        pltpu.VMEM((places, halves, HD + 16, TILE), jnp.float32),
        pltpu.VMEM((count, TILE), jnp.float32),
        pltpu.VMEM((count, TILE), jnp.float32),
        pltpu.SMEM((4 * places + 1,), jnp.int32),
    ]


def cost(parts):
    return pl.CostEstimate(
        flops=parts * 16 * 768 * 768 * 128,
        bytes_accessed=parts * 2**21,
        transcendentals=parts * 4 * 768 * 768,
    )


def others(group_ids, q_x, q_y, mine, theirs):
    count = q_x.shape[0]
    texts = 8 * (mine.shape[2] - count)
    out = jax.ShapeDtypeStruct((count + 32 + texts, HD), jnp.bfloat16)
    return pl.pallas_call(
        others_kernel,
        in_specs=[SMEM] + [VMEM] * 4,
        out_specs=[VMEM] * 3,
        out_shape=[out] * 3,
        scratch_shapes=scratch(3, count),
        compiler_params=PARAMS,
        cost_estimate=cost(3),
        name="others",
    )(group_ids, q_x, q_y, mine, theirs)


def own(group_ids, q, mine, theirs):
    count = q.shape[0]
    return pl.pallas_call(
        own_kernel,
        in_specs=[SMEM] + [VMEM] * 3,
        out_specs=[VMEM] * 2,
        out_shape=[
            jax.ShapeDtypeStruct((count, HD), jnp.float32),
            jax.ShapeDtypeStruct((8, HD), jnp.float32),
        ],
        scratch_shapes=scratch(1, count),
        compiler_params=PARAMS,
        cost_estimate=cost(1),
        name="own",
    )(group_ids, q, mine, theirs)


def merge_kernel(
    len_ref, mean_ref, logs_ref, c_ref, mine, theirs, r0, r1, r2, gate_ref,
    out_ref, tk_ref, tv_ref, cross_ref, weight_ref,
):
    count = mean_ref.shape[0]
    pieces, texts, _ = tk_ref.shape
    slot = lax.axis_index("group")
    for side, held in enumerate((tk_ref, tv_ref)):
        for place, group in enumerate(key_groups(slot)):
            ref = (mine, theirs)[place % 2]
            held[group] = ref[place // 2, side, pl.ds(count, texts), :]
        for whose, ref in zip(OTHERS, (r0, r1, r2)):
            for place, group in enumerate(key_groups(whose(slot))):
                start = count + 32 + (2 * place + side) * texts
                held[group] = ref[pl.ds(start, texts), :]
    length = pieces * texts
    mask = lax.broadcasted_iota(jnp.int32, (length, 1), 0) < len_ref[0]
    k = tk_ref[...].reshape(length, HD)
    v = with_ones(tv_ref[...].reshape(length, HD).T)

    @pl.loop(0, count // TILE)
    def _(half):
        queries = c_ref[pl.ds(pl.multiple_of(half * TILE, TILE), TILE), :]
        s = jnp.where(mask, scores_of(k, queries), LOW)
        top = jnp.max(s, axis=0, keepdims=True)
        p = jnp.exp2((s - top) * LOG2).astype(jnp.bfloat16)
        sums = jnp.dot(v, p, preferred_element_type=jnp.float32)

        def write(start, part):
            cross_ref[pl.ds(pl.multiple_of(half * TILE + start, HD), HD), :] = part

        means(sums, write)

    logs = [logs_ref[...]]
    for ref in (r0, r1, r2):
        tail = ref[pl.ds(count, 32), :].astype(jnp.float32)
        logs.append(tail[0:8] + tail[8:16] + tail[16:24])
    best = functools.reduce(jnp.maximum, logs)
    weights = [jnp.exp2(line - best) for line in logs]
    total = functools.reduce(jnp.add, weights)
    for place, weight in enumerate(weights):
        weight_ref[place] = weight / total
    gate = gate_ref[...]

    @pl.loop(0, count // HD)
    def _(step):
        rows = pl.ds(pl.multiple_of(step * HD, HD), HD)
        parts = [mean_ref[rows, :]]
        parts += [ref[rows, :].astype(jnp.float32) for ref in (r0, r1, r2)]
        mixed = None
        for place, part in enumerate(parts):
            line = weight_ref[place, pl.ds(step, 1), :]
            column = jnp.broadcast_to(line, (HD, HD)).T
            mixed = column * part if mixed is None else mixed + column * part
        out_ref[rows, :] = (gate * mixed + cross_ref[rows, :]).astype(jnp.bfloat16)


def merge(text_len, mean, logs, cross, mine, theirs, received, gate):
    count = cross.shape[0]
    held = pltpu.VMEM((16, mine.shape[2] - count, HD), jnp.bfloat16)
    return pl.pallas_call(
        merge_kernel,
        in_specs=[SMEM] + [VMEM] * 9,
        out_specs=VMEM,
        out_shape=jax.ShapeDtypeStruct(mean.shape, jnp.bfloat16),
        scratch_shapes=[
            held,
            held,
            pltpu.VMEM((count, HD), jnp.float32),
            pltpu.VMEM((4, 8, HD), jnp.float32),
        ],
        compiler_params=PARAMS,
        cost_estimate=cost(1),
        name="merge",
    )(text_len, mean, logs, cross, mine, theirs, *received, gate)


def to_heads(array):
    return lax.all_to_all(array, "seq", split_axis=0, concat_axis=0, tiled=True)


def body(
    queries, keys, values, cross_queries, text_keys, text_values, group_gate, group_ids, text_len
):
    packed = pack(queries, keys, values, cross_queries)
    received = to_heads(packed)
    q, kv, cross, gate = unpack(received, text_keys, text_values, group_gate)
    kv_near, q_x = lax.optimization_barrier((swap(kv, across_y1), swap(q, across_x)))
    mine = join(kv, kv_near)
    q_y = swap(join(q, q_x), across_y2)
    theirs = swap(mine, core_of)
    sent = others(group_ids, q_x, q_y, mine, theirs)
    back = [swap(one, whose) for one, whose in zip(sent, OTHERS)]
    mean, logs = own(group_ids, q, mine, theirs)
    mixed = merge(text_len, mean, logs, cross, mine, theirs, back, gate)
    count = mixed.shape[0]
    heads = lax.axis_size("seq")
    mixed = to_heads(mixed.reshape(heads, count // heads, HD))
    return jnp.transpose(mixed, (1, 0, 2)).reshape(1, count // heads, heads * HD)


def solution(mesh):
    return jax.shard_map(
        body,
        mesh=mesh,
        in_specs=(
            P("group", "seq", None),
            P("group", "seq", None),
            P("group", "seq", None),
            P("group", "seq", None),
            P("group", "seq"),
            P("group", "seq"),
            P("group", "seq"),
            P(),
            P(),
        ),
        out_specs=P("group", "seq", None),
        check_vma=False,
    )
```

time: 274 us -> 168 us (0.61)
  the two profiles are of different devices: /device:TPU:1 before, /device:TPU:2 now
where the time goes in v2:
time: 168 us; the launch traced here: 167 us
  blocking collectives  94.6 us (56%)
  starting transfers between devices  31.1 us (19%)
  Pallas kernels  24.6 us (15%)
  waiting for transfers between devices  15.2 us (9%)
    all_to_all x2, blocking collectives, to_heads(): return lax.all_to_all(array, 'seq', split_axis=0, concat_axis=0, tiled=True)  94.6 us
    ppermute x7, starting transfers between devices, swap(): return lax.ppermute(array, 'group', [(i, partner(i)) for i in range(16)])  31.1 us
    ppermute x7, waiting for transfers between devices, swap(): return lax.ppermute(array, 'group', [(i, partner(i)) for i in range(16)])  15.2 us
    pallas_call x1, Pallas kernels, others(): pl.pallas_call(others_kernel, in_specs=[SMEM] + [VMEM] * 4, out_specs=[VM...  12.6 us
    pallas_call x1, Pallas kernels, own(): pl.pallas_call(own_kernel, in_specs=[SMEM] + [VMEM] * 3, out_specs=[VMEM]...  6.4 us
  transfers between devices with their start and end apart: 7, of which 3 were waited for; matrix products, arithmetic and copies ran while one was open for 0% of the time, Pallas kernels for 4%

profile of v2, /device:TPU:2, one launch (start us, length us, event | category | flops | bytes accessed | tf_op | source)
XLA Modules:
  0.0 167.1 jit_solution(5161526927655345989)
XLA Ops:
  0.0 2.2 %pack.1 = bf16[32,4,24,128]{3,2,1,0:T(8,128)(2,1)} custom-call(bf16[1,24,4096]{2,1,0:T(8,128)(2,1)} %q_hbm.1, bf16[1,24,4096]{2,1,0:T(8,128)(2,1)} %k_hbm.1, bf16[1,24,4096]{2,1,0:T(8,128)(2,1)} %v_hbm.1, bf16[1,24,4096]{2,1,0:T(8,128)(2,1)} %c_hbm.1), custom_call_target="tpu_custom_call" | custom-call | tf_op jit(solution)/shard_map/pack/pallas_call | solution.py:75
  2.2 0.0 copy-start
  2.2 0.0 copy-start.1
  2.2 0.0 copy-start.2
  2.2 59.5 %all_to_all.10.in_ref = bf16[32,4,24,128]{3,2,1,0:T(8,128)(2,1)S(1)} all-to-all(bf16[32,4,24,128]{3,2,1,0:T(8,128)(2,1)} %pack.1), channel_id=1, replica_groups=mesh['group'=16,'seq'=32] {'seq'}, dimensions={0} | all-to-all | bytes 1572864 | tf_op jit(solution)/shard_map/all_to_all | solution.py:455
  61.7 0.0 copy-done
  61.7 0.0 copy-done.1
  61.7 0.0 copy-done.2
  61.7 0.6 unpack.1
  62.4 3.5 %collective-permute-start = (bf16[2,800,128]{2,1,0:T(8,128)(2,1)S(1)}, bf16[2,800,128]{2,1,0:T(8,128)(2,1)S(1)}, u32[]{:S(2)}, u32[]{:S(2)}) collective-permute-start(bf16[2,800,128]{2,1,0:T(8,128)(2,1)S(1)} %get-tuple-element.17), channel_id=1, source_target_pairs={{0,64},{32,96},{64,0},{96,32},{128,192},{160,224},{192,128},{224,1... | collective-permute-start | bytes 1228808 | tf_op jit(solution)/shard_map/ppermute | solution.py:46
  65.9 3.3 %collective-permute-start.1 = (bf16[768,128]{1,0:T(8,128)(2,1)S(1)}, bf16[768,128]{1,0:T(8,128)(2,1)S(1)}, u32[]{:S(2)}, u32[]{:S(2)}) collective-permute-start(bf16[768,128]{1,0:T(8,128)(2,1)S(1)} %get-tuple-element.16.q_ref.a_ref), channel_id=1, source_target_pairs={{0,256},{32,288},{64,320},{96,352},{128,384},{160,416},{192,448},{... | collective-permute-start | bytes 589832 | tf_op jit(solution)/shard_map/ppermute | solution.py:46
  69.2 4.2 %collective-permute-done.1.b_ref.x_ref = bf16[768,128]{1,0:T(8,128)(2,1)S(1)} collective-permute-done((bf16[768,128]{1,0:T(8,128)(2,1)S(1)}, bf16[768,128]{1,0:T(8,128)(2,1)S(1)}, u32[]{:S(2)}, u32[]{:S(2)}) %collective-permute-start.1) | collective-permute-done | bytes 196640 | tf_op jit(solution)/shard_map/ppermute | solution.py:46
  73.4 1.2 collective-permute-done
  74.6 0.3 join.2
  74.9 0.0 copy-start.3
  74.9 1.9 %collective-permute-start.2 = (bf16[2,2,800,128]{3,2,1,0:T(8,128)(2,1)S(1)}, bf16[2,2,800,128]{3,2,1,0:T(8,128)(2,1)S(1)}, u32[]{:S(2)}, u32[]{:S(2)}) collective-permute-start(bf16[2,2,800,128]{3,2,1,0:T(8,128)(2,1)S(1)} %bitcast.5), channel_id=1, source_target_pairs={{0,32},{32,0},{64,96},{96,64},{128,160},{160,128},{192,224},{224,1... | collective-permute-start | bytes 2457608 | tf_op jit(solution)/shard_map/ppermute | solution.py:46
  76.8 0.1 join.3
  77.0 4.9 %collective-permute-start.3 = (bf16[2,768,128]{2,1,0:T(8,128)(2,1)S(1)}, bf16[2,768,128]{2,1,0:T(8,128)(2,1)S(1)}, u32[]{:S(2)}, u32[]{:S(2)}) collective-permute-start(bf16[2,768,128]{2,1,0:T(8,128)(2,1)S(1)} %join.3), channel_id=1, source_target_pairs={{0,192},{32,224},{64,128},{96,160},{128,64},{160,96},{192,0},{224,... | collective-permute-start | bytes 1179656 | tf_op jit(solution)/shard_map/ppermute | solution.py:46
  81.9 9.8 %collective-permute-done.3.y_ref = bf16[2,768,128]{2,1,0:T(8,128)(2,1)S(1)} collective-permute-done((bf16[2,768,128]{2,1,0:T(8,128)(2,1)S(1)}, bf16[2,768,128]{2,1,0:T(8,128)(2,1)S(1)}, u32[]{:S(2)}, u32[]{:S(2)}) %collective-permute-start.3) | collective-permute-done | bytes 393248 | tf_op jit(solution)/shard_map/ppermute | solution.py:46
  91.7 0.0 collective-permute-done.2.theirs
  91.7 0.0 copy-done.3
  91.7 12.6 %others.1 = (bf16[1056,128]{1,0:T(8,128)(2,1)S(1)}, bf16[1056,128]{1,0:T(8,128)(2,1)S(1)}, bf16[1056,128]{1,0:T(8,128)(2,1)S(1)}) custom-call(s32[16]{0:T(128)S(1)} %copy-done.3, bf16[768,128]{1,0:T(8,128)(2,1)S(1)} %collective-permute-done.1.b_ref.x_ref, bf16[2,768,128]{2,1,0:T(8,128)(2,1)S(1)} %collective-permute-done.3.y_ref, ...), custom_call_target="tpu_custom_call" | custom-call | flops 3623878656 | bytes 6291456 | tf_op jit(solution)/shard_map/others/pallas_call | solution.py:348
  104.3 1.9 %collective-permute-start.4 = (bf16[1056,128]{1,0:T(8,128)(2,1)S(1)}, bf16[1056,128]{1,0:T(8,128)(2,1)S(1)}, u32[]{:S(2)}, u32[]{:S(2)}) collective-permute-start(bf16[1056,128]{1,0:T(8,128)(2,1)S(1)} %get-tuple-element.23), channel_id=1, source_target_pairs={{0,256},{32,288},{64,320},{96,352},{128,384},{160,416},{192,448},{... | collective-permute-start | bytes 811016 | tf_op jit(solution)/shard_map/ppermute | solution.py:46
  106.2 12.1 %collective-permute-start.5 = (bf16[1056,128]{1,0:T(8,128)(2,1)S(1)}, bf16[1056,128]{1,0:T(8,128)(2,1)S(1)}, u32[]{:S(2)}, u32[]{:S(2)}) collective-permute-start(bf16[1056,128]{1,0:T(8,128)(2,1)S(1)} %get-tuple-element.24), channel_id=1, source_target_pairs={{0,192},{32,224},{64,128},{96,160},{128,64},{160,96},{192,0},{224,... | collective-permute-start | bytes 811016 | tf_op jit(solution)/shard_map/ppermute | solution.py:46
  118.3 3.4 %collective-permute-start.6 = (bf16[1056,128]{1,0:T(8,128)(2,1)S(1)}, bf16[1056,128]{1,0:T(8,128)(2,1)S(1)}, u32[]{:S(2)}, u32[]{:S(2)}) collective-permute-start(bf16[1056,128]{1,0:T(8,128)(2,1)S(1)} %get-tuple-element.25), channel_id=1, source_target_pairs={{0,448},{32,480},{64,384},{96,416},{128,320},{160,352},{192,256},{... | collective-permute-start | bytes 811016 | tf_op jit(solution)/shard_map/ppermute | solution.py:46
  122.3 6.4 %own.1 = (f32[768,128]{1,0:T(8,128)S(1)}, f32[8,128]{1,0:T(8,128)S(1)}) custom-call(s32[16]{0:T(128)S(1)} %copy-done.3, bf16[768,128]{1,0:T(8,128)(2,1)S(1)} %get-tuple-element.16.q_ref.a_ref, bf16[2,2,800,128]{3,2,1,0:T(8,128)(2,1)S(1)} %bitcast.7, bf16[2,2,800,128]{3,2,1,0:T(8,128)(2,1)S(1)} %collective-permute-done.2.theirs), custom_call_target="tpu_custom_call" | custom-call | flops 1207959552 | bytes 2097152 | tf_op jit(solution)/shard_map/own/pallas_call | solution.py:362
  128.8 0.0 collective-permute-done.4.r0
  128.8 0.0 collective-permute-done.5.r1
  128.8 0.0 collective-permute-done.6.r2
  128.8 2.4 %merge.1 = bf16[768,128]{1,0:T(8,128)(2,1)S(1)} custom-call(s32[1]{0:T(128)S(6)} %copy.11.len_ref, f32[768,128]{1,0:T(8,128)S(1)} %get-tuple-element.19.mean_ref, f32[8,128]{1,0:T(8,128)S(1)} %get-tuple-element.20.logs_ref, bf16[768,128]{1,0:T(8,128)(2,1)S(1)} %get-tuple-element.21.c_ref, bf16[2,2,800,128]{3,2,1,0:T(8,128)(2,1)S(1)} %bitcast.8, ...), custom_call_target="tpu_custom_call" | custom-call | flops 1207959552 | bytes 2097152 | tf_op jit(solution)/shard_map/merge/pallas_call | solution.py:437
  131.2 35.1 %all_to_all.11 = bf16[32,24,128]{2,1,0:T(8,128)(2,1)S(1)} all-to-all(bf16[32,24,128]{2,1,0:T(8,128)(2,1)S(1)} %bitcast.11), channel_id=1, replica_groups=mesh['group'=16,'seq'=32] {'seq'}, dimensions={0} | all-to-all | bytes 393216 | tf_op jit(solution)/shard_map/all_to_all | solution.py:455
  166.3 0.8 reshape.19
  (1 shorter events, 0.0 us)
Async XLA Ops:
  2.2 59.6 %copy-start = (bf16[32,128]{1,0:T(8,128)(2,1)S(1)}, bf16[32,128]{1,0:T(8,128)(2,1)}, u32[]{:S(2)}) copy-start(bf16[32,128]{1,0:T(8,128)(2,1)} %tk_ref.1) | copy-start | bytes 24580
  2.2 59.5 %copy-start.1 = (bf16[32,128]{1,0:T(8,128)(2,1)S(1)}, bf16[32,128]{1,0:T(8,128)(2,1)}, u32[]{:S(2)}) copy-start(bf16[32,128]{1,0:T(8,128)(2,1)} %tv_ref.1) | copy-start | bytes 24580
  2.2 59.5 %copy-start.2 = (f32[1,128]{1,0:T(1,128)S(1)}, f32[1,128]{1,0:T(1,128)}, u32[]{:S(2)}) copy-start(f32[1,128]{1,0:T(1,128)} %gate_in.1) | copy-start | bytes 1540
  62.4 12.3 %collective-permute-start = (bf16[2,800,128]{2,1,0:T(8,128)(2,1)S(1)}, bf16[2,800,128]{2,1,0:T(8,128)(2,1)S(1)}, u32[]{:S(2)}, u32[]{:S(2)}) collective-permute-start(bf16[2,800,128]{2,1,0:T(8,128)(2,1)S(1)} %get-tuple-element.17), channel_id=1, source_target_pairs={{0,64},{32,96},{64,0},{96,32},{128,192},{160,224},{192,128},{224,1... | collective-permute-start | bytes 1228808 | tf_op jit(solution)/shard_map/ppermute | solution.py:46
  65.9 7.6 %collective-permute-start.1 = (bf16[768,128]{1,0:T(8,128)(2,1)S(1)}, bf16[768,128]{1,0:T(8,128)(2,1)S(1)}, u32[]{:S(2)}, u32[]{:S(2)}) collective-permute-start(bf16[768,128]{1,0:T(8,128)(2,1)S(1)} %get-tuple-element.16.q_ref.a_ref), channel_id=1, source_target_pairs={{0,256},{32,288},{64,320},{96,352},{128,384},{160,416},{192,448},{... | collective-permute-start | bytes 589832 | tf_op jit(solution)/shard_map/ppermute | solution.py:46
  74.9 16.8 %copy-start.3 = (s32[16]{0:T(128)S(1)}, s32[16]{0:T(128)}, u32[]{:S(2)}) copy-start(s32[16]{0:T(128)} %ids_ref.3) | copy-start | bytes 196
  74.9 16.8 %collective-permute-start.2 = (bf16[2,2,800,128]{3,2,1,0:T(8,128)(2,1)S(1)}, bf16[2,2,800,128]{3,2,1,0:T(8,128)(2,1)S(1)}, u32[]{:S(2)}, u32[]{:S(2)}) collective-permute-start(bf16[2,2,800,128]{3,2,1,0:T(8,128)(2,1)S(1)} %bitcast.5), channel_id=1, source_target_pairs={{0,32},{32,0},{64,96},{96,64},{128,160},{160,128},{192,224},{224,1... | collective-permute-start | bytes 2457608 | tf_op jit(solution)/shard_map/ppermute | solution.py:46
  77.0 14.7 %collective-permute-start.3 = (bf16[2,768,128]{2,1,0:T(8,128)(2,1)S(1)}, bf16[2,768,128]{2,1,0:T(8,128)(2,1)S(1)}, u32[]{:S(2)}, u32[]{:S(2)}) collective-permute-start(bf16[2,768,128]{2,1,0:T(8,128)(2,1)S(1)} %join.3), channel_id=1, source_target_pairs={{0,192},{32,224},{64,128},{96,160},{128,64},{160,96},{192,0},{224,... | collective-permute-start | bytes 1179656 | tf_op jit(solution)/shard_map/ppermute | solution.py:46
  104.3 24.5 %collective-permute-start.4 = (bf16[1056,128]{1,0:T(8,128)(2,1)S(1)}, bf16[1056,128]{1,0:T(8,128)(2,1)S(1)}, u32[]{:S(2)}, u32[]{:S(2)}) collective-permute-start(bf16[1056,128]{1,0:T(8,128)(2,1)S(1)} %get-tuple-element.23), channel_id=1, source_target_pairs={{0,256},{32,288},{64,320},{96,352},{128,384},{160,416},{192,448},{... | collective-permute-start | bytes 811016 | tf_op jit(solution)/shard_map/ppermute | solution.py:46
  106.2 22.6 %collective-permute-start.5 = (bf16[1056,128]{1,0:T(8,128)(2,1)S(1)}, bf16[1056,128]{1,0:T(8,128)(2,1)S(1)}, u32[]{:S(2)}, u32[]{:S(2)}) collective-permute-start(bf16[1056,128]{1,0:T(8,128)(2,1)S(1)} %get-tuple-element.24), channel_id=1, source_target_pairs={{0,192},{32,224},{64,128},{96,160},{128,64},{160,96},{192,0},{224,... | collective-permute-start | bytes 811016 | tf_op jit(solution)/shard_map/ppermute | solution.py:46
  118.3 10.5 %collective-permute-start.6 = (bf16[1056,128]{1,0:T(8,128)(2,1)S(1)}, bf16[1056,128]{1,0:T(8,128)(2,1)S(1)}, u32[]{:S(2)}, u32[]{:S(2)}) collective-permute-start(bf16[1056,128]{1,0:T(8,128)(2,1)S(1)} %get-tuple-element.25), channel_id=1, source_target_pairs={{0,448},{32,480},{64,384},{96,416},{128,320},{160,352},{192,256},{... | collective-permute-start | bytes 811016 | tf_op jit(solution)/shard_map/ppermute | solution.py:46

commit v3 on v2

v3 whole, which is shorter than its diff:
```python
import functools
import math

import jax
import jax.numpy as jnp
from jax import lax
from jax.experimental import pallas as pl
from jax.experimental.pallas import tpu as pltpu
from jax.sharding import PartitionSpec as P

HD = 128
LOG2 = math.log2(math.e) / math.sqrt(HD)
LOW = -1e30
VMEM = pl.BlockSpec(memory_space=pltpu.VMEM)
SMEM = pl.BlockSpec(memory_space=pltpu.SMEM)
PARAMS = pltpu.CompilerParams(vmem_limit_bytes=14 * 2**20)


SMALL, LARGE = 2.0**-60, 2.0**90
TILE = 384


def core_of(i):
    return i + 1 - 2 * (i % 2)


def across_x(i):
    return (i + 8) % 16


def across_y1(i):
    y = (i // 2) % 4
    return i + 2 * (1 - 2 * (y % 2))


def across_y2(i):
    y = (i // 2) % 4
    return (i // 8) * 8 + ((y + 2 * (y % 2) + 3) % 4) * 2 + i % 2


def across_xy2(i):
    return across_x(across_y2(i))


CLUSTERS = [
    [i, across_x(i), across_y2(i), across_xy2(i)] for i in (2, 3, 6, 7)
]
OWNERS = (lambda i: i, across_x, across_y2, across_xy2)


def place_of(i):
    y = (i // 2) % 4
    return i // 8 + 2 * ((y + 1) % 2)


def place_across(i, step):
    place = place_of(i)
    x, y = place % 2, place // 2
    if step % 2:
        x = 1 - x
    if step // 2:
        y = 1 - y
    return x + 2 * y


def in_cluster(array):
    return lax.all_to_all(
        array, "group", split_axis=0, concat_axis=0, axis_index_groups=CLUSTERS, tiled=True
    )


def swap(array, partner):
    return lax.ppermute(array, "group", [(i, partner(i)) for i in range(16)])


CHUNKS = 4


def pack_kernel(q_hbm, k_hbm, v_hbm, c_hbm, out_ref, held, sems):
    sources = (q_hbm, k_hbm, v_hbm, c_hbm)
    heads = out_ref.shape[0]
    chunk = heads // CHUNKS * HD
    copies = []
    for slot, ref in enumerate(sources):
        for part in range(CHUNKS):
            where = pl.ds(part * chunk, chunk)
            copy = pltpu.make_async_copy(
                ref.at[0, :, where], held.at[slot, :, where], sems.at[slot, part]
            )
            copy.start()
            copies.append(copy)
    for slot in range(len(sources)):
        for part in range(CHUNKS):
            copies[slot * CHUNKS + part].wait()
            for head in range(part * heads // CHUNKS, (part + 1) * heads // CHUNKS):
                out_ref[head, slot] = held[slot, :, head * HD : (head + 1) * HD]


def pack(queries, keys, values, cross_queries):
    rows, width = queries.shape[1:]
    heads = width // HD
    return pl.pallas_call(
        pack_kernel,
        in_specs=[pl.BlockSpec(memory_space=pl.ANY)] * 4,
        out_specs=VMEM,
        out_shape=jax.ShapeDtypeStruct((heads, 4, rows, HD), jnp.bfloat16),
        scratch_shapes=[
            pltpu.VMEM((4, rows, width), jnp.bfloat16),
            pltpu.SemaphoreType.DMA((4, CHUNKS)),
        ],
        compiler_params=pltpu.CompilerParams(vmem_limit_bytes=56 * 2**20),
        name="pack",
    )(queries, keys, values, cross_queries)


def pairs_of(in_ref, slot, write):
    parts, _, rows, _ = in_ref.shape

    @pl.loop(0, parts // 2)
    def _(part):
        where = pl.ds(pl.multiple_of(part * 2 * rows, 16), 2 * rows)
        pieces = [in_ref[2 * part, slot], in_ref[2 * part + 1, slot]]
        write(where, jnp.concatenate(pieces, axis=0))


def unpack_kernel(in_ref, tk_hbm, tv_hbm, q_ref, kv_ref, v_ref, text_ref, sems):
    copies = [
        pltpu.make_async_copy(ref, text_ref.at[side], sems.at[side])
        for side, ref in enumerate((tk_hbm, tv_hbm))
    ]
    for copy in copies:
        copy.start()

    def into(ref):
        def write(where, piece):
            ref[where, :] = piece

        return write

    count = v_ref.shape[0]

    def write_queries(where, piece):
        for place in range(q_ref.shape[0]):
            q_ref[place, where, :] = piece

    pairs_of(in_ref, 0, write_queries)
    pairs_of(in_ref, 1, into(kv_ref.at[0]))
    pairs_of(in_ref, 2, into(v_ref))

    @pl.loop(0, count // HD)
    def _(block):
        where = pl.ds(pl.multiple_of(block * HD, HD), HD)
        kv_ref[1, where, :] = v_ref[where, :].T

    tail = pl.ds(count, text_ref.shape[1])
    for side, copy in enumerate(copies):
        copy.wait()
        kv_ref[side, tail, :] = text_ref[side]


def unpack(received, text_keys, text_values):
    parts, _, rows, width = received.shape
    count = parts * rows
    return pl.pallas_call(
        unpack_kernel,
        in_specs=[VMEM] + [pl.BlockSpec(memory_space=pl.ANY)] * 2,
        out_specs=[VMEM] * 2,
        out_shape=[
            jax.ShapeDtypeStruct((4, count, width), jnp.bfloat16),
            jax.ShapeDtypeStruct((2, count + text_keys.shape[0], width), jnp.bfloat16),
        ],
        scratch_shapes=[
            pltpu.VMEM((count, width), jnp.bfloat16),
            pltpu.VMEM((2,) + text_keys.shape, jnp.bfloat16),
            pltpu.SemaphoreType.DMA((2,)),
        ],
        compiler_params=PARAMS,
        name="unpack",
    )(received, text_keys, text_values)


def unpack_cross_kernel(in_ref, c_hbm, c_ref, sem):
    def write(where, piece):
        c_ref[where, :] = piece

    pairs_of(in_ref, 3, write)
    copy = pltpu.make_async_copy(c_ref, c_hbm, sem)
    copy.start()
    copy.wait()


def unpack_cross(received):
    parts, _, rows, width = received.shape
    count = parts * rows
    return pl.pallas_call(
        unpack_cross_kernel,
        in_specs=[VMEM],
        out_specs=pl.BlockSpec(memory_space=pl.ANY),
        out_shape=jax.ShapeDtypeStruct((count, width), jnp.bfloat16),
        scratch_shapes=[pltpu.VMEM((count, width), jnp.bfloat16), pltpu.SemaphoreType.DMA],
        compiler_params=PARAMS,
        name="unpack_cross",
    )(received)


def scores_of(k, q):
    return lax.dot_general(
        k, q, (((1,), (1,)), ((), ())), preferred_element_type=jnp.float32
    )


def with_ones(v):
    return jnp.concatenate([v, jnp.ones((16, v.shape[1]), v.dtype)], axis=0)


def features_first(v_blocks):
    count = v_blocks.shape[0] // HD
    return jnp.concatenate([v_blocks[i * HD : (i + 1) * HD] for i in range(count)], axis=1)


def key_groups(slot):
    near = across_y1(slot)
    return slot, core_of(slot), near, core_of(near)


def pieces_of(block, count):
    return block[0, pl.ds(0, count), :], with_ones(features_first(block[1, pl.ds(0, count), :]))


def half_of(q_ref, half):
    return q_ref[pl.ds(half * TILE, TILE), :]


def hold(held, blocks):
    @pl.loop(0, held.shape[2] // 32)
    def _(step):
        rows = pl.ds(pl.multiple_of(step * 32, 32), 32)
        for number, block in enumerate(blocks):
            for side in range(2):
                held[number, side, rows, :] = block[side, rows, :]


def mix(place, half, s, v, top_ref, sum_ref):
    p = jnp.exp2((s - top_ref[place, half]) * LOG2).astype(jnp.bfloat16)
    sum_ref[place, half] += jnp.dot(v, p, preferred_element_type=jnp.float32)


def estimate(place, q_ref, keys, top_ref):
    for half in range(q_ref.shape[0] // TILE):
        s = scores_of(keys, half_of(q_ref, half))
        top_ref[place, half] = jnp.max(s, axis=0, keepdims=True)


def add_listed(length, list_ref, held, queries, top_ref, sum_ref, scores):
    count = held.shape[2]
    last = len(scores) - 1

    def item(index):
        code = list_ref[index]
        return code // 4, held.at[code % 4]

    def keys(block):
        return block[0, pl.ds(0, count), :]

    place, block = item(0)
    scores[0][...] = scores_of(keys(block), half_of(queries.at[place], 0))

    @pl.loop(0, length)
    def _(index):
        place, block = item(index)
        k, v = pieces_of(block, count)
        after, block = item(jnp.minimum(index + 1, length - 1))
        for tile in range(last + 1):
            if tile < last:
                scores[tile + 1][...] = scores_of(k, half_of(queries.at[place], tile + 1))
                mix(place, tile, scores[tile][...], v, top_ref, sum_ref)
            else:
                held_scores = scores[last][...]
                scores[0][...] = scores_of(keys(block), half_of(queries.at[after], 0))
                mix(place, tile, held_scores, v, top_ref, sum_ref)


def first_kernel(
    ids_ref, q4_ref, one, two, top_hbm, sum_hbm, held, top_ref, sum_ref, sems, list_ref, *scores
):
    slot = lax.axis_index("group")
    q_ref = q4_ref.at[0]
    hold(held, (one, two))
    sum_ref[...] = jnp.zeros_like(sum_ref)
    estimate(0, q_ref, one[0, pl.ds(0, HD), :], top_ref)
    list_ref[0] = 0
    list_ref[1] = 1
    length = 1 + (ids_ref[core_of(slot)] <= ids_ref[slot]).astype(jnp.int32)
    add_listed(length, list_ref, held, q4_ref, top_ref, sum_ref, scores)
    copies = [
        pltpu.make_async_copy(top_ref, top_hbm, sems.at[0]),
        pltpu.make_async_copy(sum_ref, sum_hbm, sems.at[1]),
    ]
    for copy in copies:
        copy.start()
    for copy in copies:
        copy.wait()


def attend_kernel(
    ids_ref, q_ref, b0, b1, b2, b3, top_hbm, sum_hbm,
    out_ref, queries, held, top_ref, sum_ref, sems, list_ref, full_ref, *scores,
):
    copies = [
        pltpu.make_async_copy(top_hbm.at[0], top_ref.at[0], sems.at[0]),
        pltpu.make_async_copy(sum_hbm.at[0], sum_ref.at[0], sems.at[1]),
    ]
    for copy in copies:
        copy.start()
    slot = lax.axis_index("group")
    blocks = (b0, b1, b2, b3)
    hold(held, blocks)
    count = held.shape[2]
    for step in range(4):
        queries[step] = q_ref[place_across(slot, step)]
    @pl.loop(1, 4)
    def _(place):
        sum_ref[place] = jnp.zeros_like(sum_ref[place])
        estimate(place, queries.at[place], b0[0, pl.ds(0, HD), :], top_ref)

    list_ref[0] = 0
    length = jnp.int32(0)
    full_length = jnp.int32(0)
    seen = []
    for place, owner in enumerate(OWNERS):
        rank = ids_ref[owner(slot)]
        before = full_length
        for number, group in enumerate(key_groups(slot)):
            see = (ids_ref[group] <= rank).astype(jnp.int32)
            full_ref[full_length] = 4 * place + number
            full_length = full_length + see
            if place > 0 or number > 1:
                list_ref[length] = 4 * place + number
                length = length + see
        seen.append(full_length > before)
    for copy in copies:
        copy.wait()
    add_listed(length, list_ref, held, queries, top_ref, sum_ref, scores)

    inside = jnp.bool_(True)
    for place, some in enumerate(seen):
        totals = sum_ref[place, :, HD : HD + 1, :]
        good = (jnp.min(totals) > SMALL) & (jnp.max(totals) < LARGE)
        inside = inside & (good | jnp.logical_not(some))

    @pl.when(jnp.logical_not(inside))
    def _():
        top_ref[...] = jnp.full_like(top_ref, LOW)
        sum_ref[...] = jnp.zeros_like(sum_ref)
        halves = count // TILE

        @pl.loop(0, full_length * halves)
        def _(index):
            code = full_ref[index // halves]
            place, number = code // 4, code % 4
            half = index % halves
            k, v = pieces_of(held.at[number], count)
            where = pl.ds(pl.multiple_of(half * TILE, TILE), TILE)
            s = scores_of(k, queries[place, where, :])
            old = top_ref[place, half]
            new = jnp.maximum(old, jnp.max(s, axis=0, keepdims=True))
            top_ref[place, half] = new
            sum_ref[place, half] = sum_ref[place, half] * jnp.exp2((old - new) * LOG2)
            mix(place, half, s, v, top_ref, sum_ref)

    texts = b0.shape[1] - count
    for number in range(4):
        place = place_across(slot, number)

        @pl.loop(0, count // TILE)
        def _(half):
            def write(start, part):
                where = pl.ds(pl.multiple_of(half * TILE + start, HD), HD)
                out_ref[place, where, :] = part.astype(jnp.bfloat16)

            means(sum_ref[number, half], write)

        logs = log_sums(number, top_ref, sum_ref)
        high = logs.astype(jnp.bfloat16)
        rest = logs - high.astype(jnp.float32)
        mid = rest.astype(jnp.bfloat16)
        low = (rest - mid.astype(jnp.float32)).astype(jnp.bfloat16)
        tail = jnp.concatenate([high, mid, low, jnp.zeros_like(low)], axis=0)
        out_ref[place, pl.ds(count, 32), :] = tail
        for piece in range(8):
            text = blocks[piece // 2][piece % 2, pl.ds(count, texts), :]
            out_ref[place, pl.ds(count + 32 + piece * texts, texts), :] = text


def log_sums(place, top_ref, sum_ref):
    lines = []
    for half in range(top_ref.shape[1]):
        total = sum_ref[place, half, HD : HD + 1, :]
        logs = jnp.where(total > 0, jnp.log2(total) + top_ref[place, half] * LOG2, LOW)
        lines += [logs[:, start : start + HD] for start in range(0, TILE, HD)]
    lines.append(jnp.full((8 - len(lines), HD), LOW, jnp.float32))
    return jnp.concatenate(lines, axis=0)


def means(sums, write):
    for start in range(0, TILE, HD):
        total = sums[HD : HD + 1, start : start + HD]
        write(start, sums[:HD, start : start + HD] / jnp.where(total > 0, total, 1.0))


def cost(parts):
    return pl.CostEstimate(
        flops=parts * 4 * 768 * 768 * 128,
        bytes_accessed=parts * 2**19,
        transcendentals=parts * 768 * 768,
    )


def state(places, count):
    halves = count // TILE
    return [
        jax.ShapeDtypeStruct((places, halves, 1, TILE), jnp.float32),
        jax.ShapeDtypeStruct((places, halves, HD + 16, TILE), jnp.float32),
    ]


def scores_scratch(count):
    return [pltpu.VMEM((count, TILE), jnp.float32)] * (count // TILE)


def first(group_ids, q, one, two):
    count = q.shape[1]
    return pl.pallas_call(
        first_kernel,
        in_specs=[SMEM] + [VMEM] * 3,
        out_specs=[pl.BlockSpec(memory_space=pl.ANY)] * 2,
        out_shape=state(1, count),
        scratch_shapes=[
            pltpu.VMEM((2, 2, count, HD), jnp.bfloat16),
            *(pltpu.VMEM(one.shape, one.dtype) for one in state(1, count)),
            pltpu.SemaphoreType.DMA((2,)),
            pltpu.SMEM((4,), jnp.int32),
            *scores_scratch(count),
        ],
        compiler_params=PARAMS,
        cost_estimate=cost(2),
        name="first",
    )(group_ids, q, one, two)


def attend(group_ids, queries, blocks, begun):
    count = queries.shape[1]
    texts = 8 * (blocks[0].shape[1] - count)
    return pl.pallas_call(
        attend_kernel,
        in_specs=[SMEM] + [VMEM] * 5 + [pl.BlockSpec(memory_space=pl.ANY)] * 2,
        out_specs=VMEM,
        out_shape=jax.ShapeDtypeStruct((4, count + 32 + texts, HD), jnp.bfloat16),
        scratch_shapes=[
            pltpu.VMEM((4, count, HD), jnp.bfloat16),
            pltpu.VMEM((4, 2, count, HD), jnp.bfloat16),
            *(pltpu.VMEM(one.shape, one.dtype) for one in state(4, count)),
            pltpu.SemaphoreType.DMA((2,)),
            pltpu.SMEM((20,), jnp.int32),
            pltpu.SMEM((20,), jnp.int32),
            *scores_scratch(count),
        ],
        compiler_params=PARAMS,
        cost_estimate=cost(12),
        name="attend",
    )(group_ids, queries, *blocks, *begun)


def merge_kernel(
    len_ref, c_hbm, back_ref, gate_hbm, out_ref, c_ref, tk_ref, tv_ref, cross_ref, weight_ref, gate_ref, sems
):
    copy = pltpu.make_async_copy(c_hbm, c_ref, sems.at[0])
    copy.start()
    gate_copy = pltpu.make_async_copy(gate_hbm, gate_ref, sems.at[1])
    gate_copy.start()
    count = c_ref.shape[0]
    pieces, texts, _ = tk_ref.shape
    slot = lax.axis_index("group")
    for step, owner in enumerate(OWNERS):
        ref = back_ref.at[place_across(slot, step)]
        for place, group in enumerate(key_groups(owner(slot))):
            for side, held in enumerate((tk_ref, tv_ref)):
                start = count + 32 + (2 * place + side) * texts
                held[group] = ref[pl.ds(start, texts), :]
    logs = []
    for place in range(4):
        tail = back_ref[place, pl.ds(count, 32), :].astype(jnp.float32)
        logs.append(tail[0:8] + tail[8:16] + tail[16:24])
    best = functools.reduce(jnp.maximum, logs)
    weights = [jnp.exp2(line - best) for line in logs]
    total = functools.reduce(jnp.add, weights)
    for place, weight in enumerate(weights):
        weight_ref[place] = weight / total
    length = pieces * texts
    mask = lax.broadcasted_iota(jnp.int32, (length, 1), 0) < len_ref[0]
    k = tk_ref[...].reshape(length, HD)
    v = with_ones(tv_ref[...].reshape(length, HD).T)
    copy.wait()

    @pl.loop(0, count // TILE)
    def _(half):
        queries = c_ref[pl.ds(pl.multiple_of(half * TILE, TILE), TILE), :]
        s = jnp.where(mask, scores_of(k, queries), LOW)
        top = jnp.max(s, axis=0, keepdims=True)
        p = jnp.exp2((s - top) * LOG2).astype(jnp.bfloat16)
        sums = jnp.dot(v, p, preferred_element_type=jnp.float32)

        def write(start, part):
            cross_ref[pl.ds(pl.multiple_of(half * TILE + start, HD), HD), :] = part

        means(sums, write)

    gate_copy.wait()
    gate = jnp.broadcast_to(gate_ref[...], (HD, HD)).T

    @pl.loop(0, count // HD)
    def _(step):
        rows = pl.ds(pl.multiple_of(step * HD, HD), HD)
        mixed = None
        for place in range(4):
            line = weight_ref[place, pl.ds(step, 1), :]
            part = line * back_ref[place, rows, :].astype(jnp.float32)
            mixed = part if mixed is None else mixed + part
        out_ref[rows, :] = (gate * mixed + cross_ref[rows, :]).astype(jnp.bfloat16).T


def merge(text_len, cross, back, gate):
    anywhere = pl.BlockSpec(memory_space=pl.ANY)
    count = cross.shape[0]
    held = pltpu.VMEM((16, (back.shape[1] - count - 32) // 8, HD), jnp.bfloat16)
    return pl.pallas_call(
        merge_kernel,
        in_specs=[SMEM, anywhere, VMEM, anywhere],
        out_specs=VMEM,
        out_shape=jax.ShapeDtypeStruct((count, HD), jnp.bfloat16),
        scratch_shapes=[
            pltpu.VMEM((count, HD), jnp.bfloat16),
            held,
            held,
            pltpu.VMEM((count, HD), jnp.float32),
            pltpu.VMEM((4, 8, HD), jnp.float32),
            pltpu.VMEM(gate.shape, jnp.float32),
            pltpu.SemaphoreType.DMA((2,)),
        ],
        compiler_params=PARAMS,
        cost_estimate=cost(1),
        name="merge",
    )(text_len, cross, back, gate)


def to_heads(array):
    return lax.all_to_all(array, "seq", split_axis=0, concat_axis=0, tiled=True)


def body(
    queries, keys, values, cross_queries, text_keys, text_values, group_gate, group_ids, text_len
):
    packed = pack(queries, keys, values, cross_queries)
    received = to_heads(packed)
    q, kv = unpack(received, text_keys, text_values)
    cross = unpack_cross(received)
    kv_core = swap(kv, core_of)
    kv_near = swap(kv, across_y1)
    begun = first(group_ids, q, kv, kv_core)
    q, kv_core = lax.optimization_barrier((q, kv_core))
    blocks = (kv, kv_core, kv_near, swap(kv_near, core_of))
    back = in_cluster(attend(group_ids, in_cluster(q), blocks, begun))
    mixed = merge(text_len, cross, back, group_gate)
    count = mixed.shape[0]
    heads = lax.axis_size("seq")
    mixed = to_heads(mixed.reshape(heads, count // heads, HD))
    return jnp.transpose(mixed, (1, 0, 2)).reshape(1, count // heads, heads * HD)


def solution(mesh):
    return jax.shard_map(
        body,
        mesh=mesh,
        in_specs=(
            P("group", "seq", None),
            P("group", "seq", None),
            P("group", "seq", None),
            P("group", "seq", None),
            P("group", "seq"),
            P("group", "seq"),
            P("group", "seq"),
            P(),
            P(),
        ),
        out_specs=P("group", "seq", None),
        check_vma=False,
    )
```

time: 168 us -> 165 us (0.982)
  the two profiles are of different devices: /device:TPU:2 before, /device:TPU:24 now
where the time goes in v3:
time: 165 us; the launch traced here: 164 us
  blocking collectives  87.8 us (53%)
  starting transfers between devices  31.6 us (19%)
  Pallas kernels  21.9 us (13%)
  waiting for transfers between devices  19.2 us (12%)
  local copies, waits for them, and re-layouts  2.59 us (2%)
    all_to_all x2, blocking collectives, to_heads(): return lax.all_to_all(array, 'seq', split_axis=0, concat_axis=0, tiled=True)  87.8 us
    all_to_all x2, starting transfers between devices, in_cluster(): lax.all_to_all(array, 'group', split_axis=0, concat_axis=0, axis_index_gr...  25.2 us
    pallas_call x1, Pallas kernels, attend(): pl.pallas_call(attend_kernel, in_specs=[SMEM] + [VMEM] * 5 + [pl.BlockSpe...  12.5 us
    all_to_all x2, waiting for transfers between devices, in_cluster(): lax.all_to_all(array, 'group', split_axis=0, concat_axis=0, axis_index_gr...  11.6 us
    ppermute x3, waiting for transfers between devices, swap(): return lax.ppermute(array, 'group', [(i, partner(i)) for i in range(16)])  7.59 us
    ppermute x3, starting transfers between devices, swap(): return lax.ppermute(array, 'group', [(i, partner(i)) for i in range(16)])  6.48 us
  transfers between devices with their start and end apart: 5, of which 2 were waited for; matrix products, arithmetic and copies ran while one was open for 0% of the time, Pallas kernels for 2%

profile of v3, /device:TPU:24, one launch (start us, length us, event | category | flops | bytes accessed | tf_op | source)
XLA Modules:
  0.0 163.9 jit_solution(8606000339182019763)
XLA Ops:
  0.0 2.2 %pack.1 = bf16[32,4,24,128]{3,2,1,0:T(8,128)(2,1)} custom-call(bf16[1,24,4096]{2,1,0:T(8,128)(2,1)} %q_hbm.1, bf16[1,24,4096]{2,1,0:T(8,128)(2,1)} %k_hbm.1, bf16[1,24,4096]{2,1,0:T(8,128)(2,1)} %v_hbm.1, bf16[1,24,4096]{2,1,0:T(8,128)(2,1)} %c_hbm.1), custom_call_target="tpu_custom_call" | custom-call | tf_op jit(solution)/shard_map/pack/pallas_call | solution.py:102
  2.2 0.0 copy-start
  2.2 0.0 copy-start.1
  2.2 60.3 %all_to_all.20.in_ref = bf16[32,4,24,128]{3,2,1,0:T(8,128)(2,1)S(1)} all-to-all(bf16[32,4,24,128]{3,2,1,0:T(8,128)(2,1)} %pack.1), channel_id=1, replica_groups=mesh['group'=16,'seq'=32] {'seq'}, dimensions={0} | all-to-all | bytes 1572864 | tf_op jit(solution)/shard_map/all_to_all | solution.py:557
  62.5 0.0 copy-done
  62.5 0.0 copy-done.1
  62.5 0.0 copy-start.3
  62.5 1.7 %unpack.1 = (bf16[4,768,128]{2,1,0:T(8,128)(2,1)}, bf16[2,800,128]{2,1,0:T(8,128)(2,1)S(1)}) custom-call(bf16[32,4,24,128]{3,2,1,0:T(8,128)(2,1)S(1)} %all_to_all.20.in_ref, bf16[32,128]{1,0:T(8,128)(2,1)S(1)} %copy-done, bf16[32,128]{1,0:T(8,128)(2,1)S(1)} %copy-done.1), custom_call_target="tpu_custom_call" | custom-call | tf_op jit(solution)/shard_map/unpack/pallas_call | solution.py:164
  64.2 1.9 %collective-permute-start = (bf16[2,800,128]{2,1,0:T(8,128)(2,1)S(1)}, bf16[2,800,128]{2,1,0:T(8,128)(2,1)S(1)}, u32[]{:S(2)}, u32[]{:S(2)}) collective-permute-start(bf16[2,800,128]{2,1,0:T(8,128)(2,1)S(1)} %get-tuple-element.12.one.b0), channel_id=1, source_target_pairs={{0,32},{32,0},{64,96},{96,64},{128,160},{160,128},{192,224},{224,1... | collective-permute-start | bytes 1228808 | tf_op jit(solution)/shard_map/ppermute | solution.py:73
  66.2 2.7 %collective-permute-start.1 = (bf16[2,800,128]{2,1,0:T(8,128)(2,1)S(1)}, bf16[2,800,128]{2,1,0:T(8,128)(2,1)S(1)}, u32[]{:S(2)}, u32[]{:S(2)}) collective-permute-start(bf16[2,800,128]{2,1,0:T(8,128)(2,1)S(1)} %get-tuple-element.12.one.b0), channel_id=1, source_target_pairs={{0,64},{32,96},{64,0},{96,32},{128,192},{160,224},{192,128},{224,1... | collective-permute-start | bytes 1228808 | tf_op jit(solution)/shard_map/ppermute | solution.py:73
  68.8 0.0 collective-permute-done.two.b1
  68.8 3.5 %all-to-all-start.1 = ((bf16[4,768,128]{2,1,0:T(8,128)(2,1)}), bf16[4,768,128]{2,1,0:T(8,128)(2,1)S(1)}, u32[]{:S(2)}, u32[]{:S(2)}) async-start(bf16[4,768,128]{2,1,0:T(8,128)(2,1)} %get-tuple-element.13.q4_ref), calls=%async_computation.1 | async-start | bytes 1572864 | tf_op jit(solution)/shard_map/all_to_all | solution.py:67
  72.3 7.6 %collective-permute-done.1.b2 = bf16[2,800,128]{2,1,0:T(8,128)(2,1)S(1)} collective-permute-done((bf16[2,800,128]{2,1,0:T(8,128)(2,1)S(1)}, bf16[2,800,128]{2,1,0:T(8,128)(2,1)S(1)}, u32[]{:S(2)}, u32[]{:S(2)}) %collective-permute-start.1) | collective-permute-done | bytes 409632 | tf_op jit(solution)/shard_map/ppermute | solution.py:73
  79.9 1.9 %collective-permute-start.2 = (bf16[2,800,128]{2,1,0:T(8,128)(2,1)S(1)}, bf16[2,800,128]{2,1,0:T(8,128)(2,1)S(1)}, u32[]{:S(2)}, u32[]{:S(2)}) collective-permute-start(bf16[2,800,128]{2,1,0:T(8,128)(2,1)S(1)} %collective-permute-done.1.b2), channel_id=1, source_target_pairs={{0,32},{32,0},{64,96},{96,64},{128,160},{160,128},{192,224},{224,1... | collective-permute-start | bytes 1228808 | tf_op jit(solution)/shard_map/ppermute | solution.py:73
  81.8 0.0 copy-done.3
  81.8 2.7 %first.1 = (f32[1,2,1,384]{3,2,1,0:T(1,128)S(1)}, f32[1,2,144,384]{3,2,1,0:T(8,128)S(1)}) custom-call(s32[16]{0:T(128)S(1)} %copy-done.3, bf16[4,768,128]{2,1,0:T(8,128)(2,1)} %get-tuple-element.13.q4_ref, bf16[2,800,128]{2,1,0:T(8,128)(2,1)S(1)} %get-tuple-element.12.one.b0, bf16[2,800,128]{2,1,0:T(8,128)(2,1)S(1)} %collective-permute-done.two.b1), custom_call_target="tpu_custom_call" | custom-call | flops 603979776 | bytes 1048576 | tf_op jit(solution)/shard_map/first/pallas_call | solution.py:433
  84.6 0.0 copy-start.4
  84.6 0.8 copy-done.4
  85.4 0.0 collective-permute-done.2.b3
  85.4 0.0 all-to-all-done.1.q_ref
  85.4 0.0 copy-start.5
  85.4 1.0 copy-done.5
  86.4 12.5 %attend.1 = bf16[4,1056,128]{2,1,0:T(8,128)(2,1)} custom-call(s32[16]{0:T(128)S(1)} %copy-done.3, bf16[4,768,128]{2,1,0:T(8,128)(2,1)S(1)} %all-to-all-done.1.q_ref, bf16[2,800,128]{2,1,0:T(8,128)(2,1)S(1)} %get-tuple-element.12.one.b0, bf16[2,800,128]{2,1,0:T(8,128)(2,1)S(1)} %collective-permute-done.two.b1, ...), custom_call_target="tpu_custom_call" | custom-call | flops 3623878656 | bytes 6291456 | tf_op jit(solution)/shard_map/attend/pallas_call | solution.py:454
  98.9 0.0 copy-start.2
  99.0 21.7 %all-to-all-start.2 = ((bf16[4,1056,128]{2,1,0:T(8,128)(2,1)}), bf16[4,1056,128]{2,1,0:T(8,128)(2,1)S(1)}, u32[]{:S(2)}, u32[]{:S(2)}) async-start(bf16[4,1056,128]{2,1,0:T(8,128)(2,1)} %attend.1), calls=%async_computation.2 | async-start | bytes 2162688 | tf_op jit(solution)/shard_map/all_to_all | solution.py:67
  121.3 0.4 unpack_cross.1.c_hbm
  121.6 11.6 %all-to-all-done.2.back_ref = bf16[4,1056,128]{2,1,0:T(8,128)(2,1)S(1)} async-done(((bf16[4,1056,128]{2,1,0:T(8,128)(2,1)}), bf16[4,1056,128]{2,1,0:T(8,128)(2,1)S(1)}, u32[]{:S(2)}, u32[]{:S(2)}) %all-to-all-start.2) | async-done | bytes 1081376 | tf_op jit(solution)/shard_map/all_to_all | solution.py:67
  133.2 0.0 copy-done.2
  133.2 2.3 %merge.1 = bf16[768,128]{1,0:T(8,128)(2,1)S(1)} custom-call(s32[1]{0:T(128)S(6)} %copy.11.len_ref, bf16[768,128]{1,0:T(8,128)(2,1)S(1)} %unpack_cross.1.c_hbm, bf16[4,1056,128]{2,1,0:T(8,128)(2,1)S(1)} %all-to-all-done.2.back_ref, f32[1,128]{1,0:T(1,128)S(1)} %copy-done.2), custom_call_target="tpu_custom_call" | custom-call | flops 301989888 | bytes 524288 | tf_op jit(solution)/shard_map/merge/pallas_call | solution.py:536
  135.5 27.6 %all_to_all.21 = bf16[32,24,128]{2,1,0:T(8,128)(2,1)S(1)} all-to-all(bf16[32,24,128]{2,1,0:T(8,128)(2,1)S(1)} %bitcast.2), channel_id=1, replica_groups=mesh['group'=16,'seq'=32] {'seq'}, dimensions={0} | all-to-all | bytes 393216 | tf_op jit(solution)/shard_map/all_to_all | solution.py:557
  163.1 0.8 reshape.7
  (1 shorter events, 0.0 us)
Async XLA Ops:
  2.2 60.3 %copy-start = (bf16[32,128]{1,0:T(8,128)(2,1)S(1)}, bf16[32,128]{1,0:T(8,128)(2,1)}, u32[]{:S(2)}) copy-start(bf16[32,128]{1,0:T(8,128)(2,1)} %tk_hbm.1) | copy-start | bytes 24580
  2.2 60.3 %copy-start.1 = (bf16[32,128]{1,0:T(8,128)(2,1)S(1)}, bf16[32,128]{1,0:T(8,128)(2,1)}, u32[]{:S(2)}) copy-start(bf16[32,128]{1,0:T(8,128)(2,1)} %tv_hbm.1) | copy-start | bytes 24580
  62.5 19.3 %copy-start.3 = (s32[16]{0:T(128)S(1)}, s32[16]{0:T(128)}, u32[]{:S(2)}) copy-start(s32[16]{0:T(128)} %ids_ref.3) | copy-start | bytes 196
  64.2 4.6 %collective-permute-start = (bf16[2,800,128]{2,1,0:T(8,128)(2,1)S(1)}, bf16[2,800,128]{2,1,0:T(8,128)(2,1)S(1)}, u32[]{:S(2)}, u32[]{:S(2)}) collective-permute-start(bf16[2,800,128]{2,1,0:T(8,128)(2,1)S(1)} %get-tuple-element.12.one.b0), channel_id=1, source_target_pairs={{0,32},{32,0},{64,96},{96,64},{128,160},{160,128},{192,224},{224,1... | collective-permute-start | bytes 1228808 | tf_op jit(solution)/shard_map/ppermute | solution.py:73
  66.2 13.8 %collective-permute-start.1 = (bf16[2,800,128]{2,1,0:T(8,128)(2,1)S(1)}, bf16[2,800,128]{2,1,0:T(8,128)(2,1)S(1)}, u32[]{:S(2)}, u32[]{:S(2)}) collective-permute-start(bf16[2,800,128]{2,1,0:T(8,128)(2,1)S(1)} %get-tuple-element.12.one.b0), channel_id=1, source_target_pairs={{0,64},{32,96},{64,0},{96,32},{128,192},{160,224},{192,128},{224,1... | collective-permute-start | bytes 1228808 | tf_op jit(solution)/shard_map/ppermute | solution.py:73
  68.8 16.5 %all-to-all-start.1 = ((bf16[4,768,128]{2,1,0:T(8,128)(2,1)}), bf16[4,768,128]{2,1,0:T(8,128)(2,1)S(1)}, u32[]{:S(2)}, u32[]{:S(2)}) async-start(bf16[4,768,128]{2,1,0:T(8,128)(2,1)} %get-tuple-element.13.q4_ref), calls=%async_computation.1 | async-start | bytes 1572864 | tf_op jit(solution)/shard_map/all_to_all | solution.py:67
  79.9 5.4 %collective-permute-start.2 = (bf16[2,800,128]{2,1,0:T(8,128)(2,1)S(1)}, bf16[2,800,128]{2,1,0:T(8,128)(2,1)S(1)}, u32[]{:S(2)}, u32[]{:S(2)}) collective-permute-start(bf16[2,800,128]{2,1,0:T(8,128)(2,1)S(1)} %collective-permute-done.1.b2), channel_id=1, source_target_pairs={{0,32},{32,0},{64,96},{96,64},{128,160},{160,128},{192,224},{224,1... | collective-permute-start | bytes 1228808 | tf_op jit(solution)/shard_map/ppermute | solution.py:73
  84.6 0.8 copy-start.4
  85.4 1.0 copy-start.5
  98.9 34.3 %copy-start.2 = (f32[1,128]{1,0:T(1,128)S(1)}, f32[1,128]{1,0:T(1,128)}, u32[]{:S(2)}) copy-start(f32[1,128]{1,0:T(1,128)} %gate_hbm.1) | copy-start | bytes 1540
  99.0 34.2 %all-to-all-start.2 = ((bf16[4,1056,128]{2,1,0:T(8,128)(2,1)}), bf16[4,1056,128]{2,1,0:T(8,128)(2,1)S(1)}, u32[]{:S(2)}, u32[]{:S(2)}) async-start(bf16[4,1056,128]{2,1,0:T(8,128)(2,1)} %attend.1), calls=%async_computation.2 | async-start | bytes 2162688 | tf_op jit(solution)/shard_map/all_to_all | solution.py:67

commit v4 on v3

--- a/solution.py
+++ b/solution.py
@@ -13,6 +13,7 @@
 LOW = -1e30
 VMEM = pl.BlockSpec(memory_space=pltpu.VMEM)
 SMEM = pl.BlockSpec(memory_space=pltpu.SMEM)
+HBM = pl.BlockSpec(memory_space=pltpu.HBM)
 PARAMS = pltpu.CompilerParams(vmem_limit_bytes=14 * 2**20)
 
 
@@ -123,7 +124,7 @@
         write(where, jnp.concatenate(pieces, axis=0))
 
 
-def unpack_kernel(in_ref, tk_hbm, tv_hbm, q_ref, kv_ref, v_ref, text_ref, sems):
+def unpack_kernel(in_ref, tk_hbm, tv_hbm, q_ref, kv_ref, all_ref, v_ref, text_ref, sems):
     copies = [
         pltpu.make_async_copy(ref, text_ref.at[side], sems.at[side])
         for side, ref in enumerate((tk_hbm, tv_hbm))
@@ -152,10 +153,10 @@
         where = pl.ds(pl.multiple_of(block * HD, HD), HD)
         kv_ref[1, where, :] = v_ref[where, :].T
 
-    tail = pl.ds(count, text_ref.shape[1])
-    for side, copy in enumerate(copies):
+    for copy in copies:
         copy.wait()
-        kv_ref[side, tail, :] = text_ref[side]
+    for place in range(all_ref.shape[0]):
+        all_ref[place] = text_ref[...]
 
 
 def unpack(received, text_keys, text_values):
@@ -163,11 +164,12 @@
     count = parts * rows
     return pl.pallas_call(
         unpack_kernel,
-        in_specs=[VMEM] + [pl.BlockSpec(memory_space=pl.ANY)] * 2,
-        out_specs=[VMEM] * 2,
+        in_specs=[VMEM] + [HBM] * 2,
+        out_specs=[VMEM] * 3,
         out_shape=[
             jax.ShapeDtypeStruct((4, count, width), jnp.bfloat16),
-            jax.ShapeDtypeStruct((2, count + text_keys.shape[0], width), jnp.bfloat16),
+            jax.ShapeDtypeStruct((2, count, width), jnp.bfloat16),
+            jax.ShapeDtypeStruct((16, 2) + text_keys.shape, jnp.bfloat16),
         ],
         scratch_shapes=[
             pltpu.VMEM((count, width), jnp.bfloat16),
@@ -177,30 +179,6 @@
         compiler_params=PARAMS,
         name="unpack",
     )(received, text_keys, text_values)
-
-
-def unpack_cross_kernel(in_ref, c_hbm, c_ref, sem):
-    def write(where, piece):
-        c_ref[where, :] = piece
-
-    pairs_of(in_ref, 3, write)
-    copy = pltpu.make_async_copy(c_ref, c_hbm, sem)
-    copy.start()
-    copy.wait()
-
-
-def unpack_cross(received):
-    parts, _, rows, width = received.shape
-    count = parts * rows
-    return pl.pallas_call(
-        unpack_cross_kernel,
-        in_specs=[VMEM],
-        out_specs=pl.BlockSpec(memory_space=pl.ANY),
-        out_shape=jax.ShapeDtypeStruct((count, width), jnp.bfloat16),
-        scratch_shapes=[pltpu.VMEM((count, width), jnp.bfloat16), pltpu.SemaphoreType.DMA],
-        compiler_params=PARAMS,
-        name="unpack_cross",
-    )(received)
 
 
 def scores_of(k, q):
@@ -302,49 +280,45 @@
         copy.wait()
 
 
-def attend_kernel(
-    ids_ref, q_ref, b0, b1, b2, b3, top_hbm, sum_hbm,
-    out_ref, queries, held, top_ref, sum_ref, sems, list_ref, full_ref, *scores,
+def attend_to(
+    steps, begun, ids_ref, q_ref, blocks, queries, held, top_ref, sum_ref, list_ref, full_ref, scores
 ):
-    copies = [
-        pltpu.make_async_copy(top_hbm.at[0], top_ref.at[0], sems.at[0]),
-        pltpu.make_async_copy(sum_hbm.at[0], sum_ref.at[0], sems.at[1]),
-    ]
-    for copy in copies:
-        copy.start()
     slot = lax.axis_index("group")
-    blocks = (b0, b1, b2, b3)
     hold(held, blocks)
     count = held.shape[2]
-    for step in range(4):
-        queries[step] = q_ref[place_across(slot, step)]
-    @pl.loop(1, 4)
-    def _(place):
-        sum_ref[place] = jnp.zeros_like(sum_ref[place])
-        estimate(place, queries.at[place], b0[0, pl.ds(0, HD), :], top_ref)
+    for number, step in enumerate(steps):
+        queries[number] = q_ref[place_across(slot, step)]
+
+    if not begun:
+
+        @pl.loop(0, len(steps))
+        def _(number):
+            sum_ref[number] = jnp.zeros_like(sum_ref[number])
+            estimate(number, queries.at[number], blocks[0][0, pl.ds(0, HD), :], top_ref)
 
     list_ref[0] = 0
     length = jnp.int32(0)
     full_length = jnp.int32(0)
     seen = []
-    for place, owner in enumerate(OWNERS):
-        rank = ids_ref[owner(slot)]
+    for number, step in enumerate(steps):
+        rank = ids_ref[OWNERS[step](slot)]
         before = full_length
-        for number, group in enumerate(key_groups(slot)):
+        for block, group in enumerate(key_groups(slot)):
             see = (ids_ref[group] <= rank).astype(jnp.int32)
-            full_ref[full_length] = 4 * place + number
+            full_ref[full_length] = 4 * number + block
             full_length = full_length + see
-            if place > 0 or number > 1:
-                list_ref[length] = 4 * place + number
+            if block > 1 or not begun:
+                list_ref[length] = 4 * number + block
                 length = length + see
         seen.append(full_length > before)
-    for copy in copies:
-        copy.wait()
+    if begun:
+        for copy in begun:
+            copy.wait()
     add_listed(length, list_ref, held, queries, top_ref, sum_ref, scores)
 
     inside = jnp.bool_(True)
-    for place, some in enumerate(seen):
-        totals = sum_ref[place, :, HD : HD + 1, :]
+    for number, some in enumerate(seen):
+        totals = sum_ref[number, :, HD : HD + 1, :]
         good = (jnp.min(totals) > SMALL) & (jnp.max(totals) < LARGE)
         inside = inside & (good | jnp.logical_not(some))
 
@@ -357,20 +331,30 @@
         @pl.loop(0, full_length * halves)
         def _(index):
             code = full_ref[index // halves]
-            place, number = code // 4, code % 4
+            number, block = code // 4, code % 4
             half = index % halves
-            k, v = pieces_of(held.at[number], count)
+            k, v = pieces_of(held.at[block], count)
             where = pl.ds(pl.multiple_of(half * TILE, TILE), TILE)
-            s = scores_of(k, queries[place, where, :])
-            old = top_ref[place, half]
+            s = scores_of(k, queries[number, where, :])
+            old = top_ref[number, half]
             new = jnp.maximum(old, jnp.max(s, axis=0, keepdims=True))
-            top_ref[place, half] = new
-            sum_ref[place, half] = sum_ref[place, half] * jnp.exp2((old - new) * LOG2)
-            mix(place, half, s, v, top_ref, sum_ref)
-
-    texts = b0.shape[1] - count
-    for number in range(4):
-        place = place_across(slot, number)
+            top_ref[number, half] = new
+            sum_ref[number, half] = sum_ref[number, half] * jnp.exp2((old - new) * LOG2)
+            mix(number, half, s, v, top_ref, sum_ref)
+
+
+def attend_kernel(
+    ids_ref, q_ref, b0, b1, b2, b3,
+    out_ref, queries, held, top_ref, sum_ref, list_ref, full_ref, *scores,
+):
+    attend_to(
+        (1, 2, 3), (), ids_ref, q_ref, (b0, b1, b2, b3),
+        queries, held, top_ref, sum_ref, list_ref, full_ref, scores,
+    )
+    slot = lax.axis_index("group")
+    count = held.shape[2]
+    for number in range(3):
+        place = place_across(slot, number + 1)
 
         @pl.loop(0, count // TILE)
         def _(half):
@@ -387,9 +371,32 @@
         low = (rest - mid.astype(jnp.float32)).astype(jnp.bfloat16)
         tail = jnp.concatenate([high, mid, low, jnp.zeros_like(low)], axis=0)
         out_ref[place, pl.ds(count, 32), :] = tail
-        for piece in range(8):
-            text = blocks[piece // 2][piece % 2, pl.ds(count, texts), :]
-            out_ref[place, pl.ds(count + 32 + piece * texts, texts), :] = text
+
+
+def own_kernel(
+    ids_ref, q_ref, b0, b1, b2, b3, top_hbm, sum_hbm,
+    out_ref, queries, held, top_ref, sum_ref, sems, list_ref, full_ref, *scores,
+):
+    copies = [
+        pltpu.make_async_copy(top_hbm, top_ref, sems.at[0]),
+        pltpu.make_async_copy(sum_hbm, sum_ref, sems.at[1]),
+    ]
+    for copy in copies:
+        copy.start()
+    attend_to(
+        (0,), copies, ids_ref, q_ref, (b0, b1, b2, b3),
+        queries, held, top_ref, sum_ref, list_ref, full_ref, scores,
+    )
+    count = held.shape[2]
+
+    @pl.loop(0, count // TILE)
+    def _(half):
+        def write(start, part):
+            out_ref[pl.ds(pl.multiple_of(half * TILE + start, HD), HD), :] = part
+
+        means(sum_ref[0, half], write)
+
+    out_ref[pl.ds(count, 8), :] = log_sums(0, top_ref, sum_ref)
 
 
 def log_sums(place, top_ref, sum_ref):
@@ -433,7 +440,7 @@
     return pl.pallas_call(
         first_kernel,
         in_specs=[SMEM] + [VMEM] * 3,
-        out_specs=[pl.BlockSpec(memory_space=pl.ANY)] * 2,
+        out_specs=[HBM] * 2,
         out_shape=state(1, count),
         scratch_shapes=[
             pltpu.VMEM((2, 2, count, HD), jnp.bfloat16),
@@ -448,61 +455,63 @@
     )(group_ids, q, one, two)
 
 
-def attend(group_ids, queries, blocks, begun):
+def attend_scratch(places, count):
+    return [
+        pltpu.VMEM((places, count, HD), jnp.bfloat16),
+        pltpu.VMEM((4, 2, count, HD), jnp.bfloat16),
+        *(pltpu.VMEM(one.shape, one.dtype) for one in state(places, count)),
+    ]
+
+
+def lists(places):
+    return [pltpu.SMEM((4 * places + 4,), jnp.int32)] * 2
+
+
+def attend(group_ids, queries, blocks):
     count = queries.shape[1]
-    texts = 8 * (blocks[0].shape[1] - count)
     return pl.pallas_call(
         attend_kernel,
-        in_specs=[SMEM] + [VMEM] * 5 + [pl.BlockSpec(memory_space=pl.ANY)] * 2,
+        in_specs=[SMEM] + [VMEM] * 5,
         out_specs=VMEM,
-        out_shape=jax.ShapeDtypeStruct((4, count + 32 + texts, HD), jnp.bfloat16),
+        out_shape=jax.ShapeDtypeStruct((4, count + 32, HD), jnp.bfloat16),
+        scratch_shapes=[*attend_scratch(3, count), *lists(3), *scores_scratch(count)],
+        compiler_params=PARAMS,
+        cost_estimate=cost(12),
+        name="attend",
+    )(group_ids, queries, *blocks)
+
+
+def own(group_ids, queries, blocks, begun):
+    count = queries.shape[1]
+    return pl.pallas_call(
+        own_kernel,
+        in_specs=[SMEM] + [VMEM] * 5 + [HBM] * 2,
+        out_specs=VMEM,
+        out_shape=jax.ShapeDtypeStruct((count + 8, HD), jnp.float32),
         scratch_shapes=[
-            pltpu.VMEM((4, count, HD), jnp.bfloat16),
-            pltpu.VMEM((4, 2, count, HD), jnp.bfloat16),
-            *(pltpu.VMEM(one.shape, one.dtype) for one in state(4, count)),
+            *attend_scratch(1, count),
             pltpu.SemaphoreType.DMA((2,)),
-            pltpu.SMEM((20,), jnp.int32),
-            pltpu.SMEM((20,), jnp.int32),
+            *lists(1),
             *scores_scratch(count),
         ],
         compiler_params=PARAMS,
-        cost_estimate=cost(12),
-        name="attend",
+        cost_estimate=cost(2),
+        name="own",
     )(group_ids, queries, *blocks, *begun)
 
 
-def merge_kernel(
-    len_ref, c_hbm, back_ref, gate_hbm, out_ref, c_ref, tk_ref, tv_ref, cross_ref, weight_ref, gate_ref, sems
-):
-    copy = pltpu.make_async_copy(c_hbm, c_ref, sems.at[0])
-    copy.start()
-    gate_copy = pltpu.make_async_copy(gate_hbm, gate_ref, sems.at[1])
-    gate_copy.start()
-    count = c_ref.shape[0]
-    pieces, texts, _ = tk_ref.shape
-    slot = lax.axis_index("group")
-    for step, owner in enumerate(OWNERS):
-        ref = back_ref.at[place_across(slot, step)]
-        for place, group in enumerate(key_groups(owner(slot))):
-            for side, held in enumerate((tk_ref, tv_ref)):
-                start = count + 32 + (2 * place + side) * texts
-                held[group] = ref[pl.ds(start, texts), :]
-    logs = []
-    for place in range(4):
-        tail = back_ref[place, pl.ds(count, 32), :].astype(jnp.float32)
-        logs.append(tail[0:8] + tail[8:16] + tail[16:24])
-    best = functools.reduce(jnp.maximum, logs)
-    weights = [jnp.exp2(line - best) for line in logs]
-    total = functools.reduce(jnp.add, weights)
-    for place, weight in enumerate(weights):
-        weight_ref[place] = weight / total
+def cross_kernel(len_ref, in_ref, text_ref, out_hbm, c_ref, cross_ref, sem):
+    def write_queries(where, piece):
+        c_ref[where, :] = piece
+
+    pairs_of(in_ref, 3, write_queries)
+    pieces, _, texts, _ = text_ref.shape
     length = pieces * texts
     mask = lax.broadcasted_iota(jnp.int32, (length, 1), 0) < len_ref[0]
-    k = tk_ref[...].reshape(length, HD)
-    v = with_ones(tv_ref[...].reshape(length, HD).T)
-    copy.wait()
-
-    @pl.loop(0, count // TILE)
+    k = text_ref[:, 0].reshape(length, HD)
+    v = with_ones(text_ref[:, 1].reshape(length, HD).T)
+
+    @pl.loop(0, c_ref.shape[0] // TILE)
     def _(half):
         queries = c_ref[pl.ds(pl.multiple_of(half * TILE, TILE), TILE), :]
         s = jnp.where(mask, scores_of(k, queries), LOW)
@@ -515,42 +524,85 @@
 
         means(sums, write)
 
-    gate_copy.wait()
+    copy = pltpu.make_async_copy(cross_ref, out_hbm, sem)
+    copy.start()
+    copy.wait()
+
+
+def cross_part(text_len, received, text):
+    parts, _, rows, width = received.shape
+    count = parts * rows
+    return pl.pallas_call(
+        cross_kernel,
+        in_specs=[SMEM] + [VMEM] * 2,
+        out_specs=HBM,
+        out_shape=jax.ShapeDtypeStruct((count, width), jnp.float32),
+        scratch_shapes=[
+            pltpu.VMEM((count, width), jnp.bfloat16),
+            pltpu.VMEM((count, width), jnp.float32),
+            pltpu.SemaphoreType.DMA,
+        ],
+        compiler_params=PARAMS,
+        cost_estimate=cost(2),
+        name="cross",
+    )(text_len, received, text)
+
+
+def merge_kernel(
+    own_hbm, cross_hbm, back_ref, gate_hbm, out_ref, own_ref, cross_ref, weight_ref, gate_ref, sems
+):
+    copies = [
+        pltpu.make_async_copy(source, target, sems.at[number])
+        for number, (source, target) in enumerate(
+            ((own_hbm, own_ref), (cross_hbm, cross_ref), (gate_hbm, gate_ref))
+        )
+    ]
+    for copy in copies:
+        copy.start()
+    slot = lax.axis_index("group")
+    count = cross_ref.shape[0]
+    received = [back_ref.at[place_across(slot, step)] for step in (1, 2, 3)]
+    logs = []
+    for ref in received:
+        tail = ref[pl.ds(count, 32), :].astype(jnp.float32)
+        logs.append(tail[0:8] + tail[8:16] + tail[16:24])
+    for copy in copies:
+        copy.wait()
+    logs.append(own_ref[pl.ds(count, 8), :])
+    best = functools.reduce(jnp.maximum, logs)
+    weights = [jnp.exp2(line - best) for line in logs]
+    total = functools.reduce(jnp.add, weights)
+    for place, weight in enumerate(weights):
+        weight_ref[place] = weight / total
     gate = jnp.broadcast_to(gate_ref[...], (HD, HD)).T
 
     @pl.loop(0, count // HD)
     def _(step):
         rows = pl.ds(pl.multiple_of(step * HD, HD), HD)
-        mixed = None
-        for place in range(4):
+        mixed = weight_ref[3, pl.ds(step, 1), :] * own_ref[rows, :]
+        for place, ref in enumerate(received):
             line = weight_ref[place, pl.ds(step, 1), :]
-            part = line * back_ref[place, rows, :].astype(jnp.float32)
-            mixed = part if mixed is None else mixed + part
+            mixed = mixed + line * ref[rows, :].astype(jnp.float32)
         out_ref[rows, :] = (gate * mixed + cross_ref[rows, :]).astype(jnp.bfloat16).T
 
 
-def merge(text_len, cross, back, gate):
-    anywhere = pl.BlockSpec(memory_space=pl.ANY)
-    count = cross.shape[0]
-    held = pltpu.VMEM((16, (back.shape[1] - count - 32) // 8, HD), jnp.bfloat16)
+def merge(mine, cross, back, gate):
     return pl.pallas_call(
         merge_kernel,
-        in_specs=[SMEM, anywhere, VMEM, anywhere],
+        in_specs=[HBM, HBM, VMEM, HBM],
         out_specs=VMEM,
-        out_shape=jax.ShapeDtypeStruct((count, HD), jnp.bfloat16),
+        out_shape=jax.ShapeDtypeStruct(cross.shape, jnp.bfloat16),
         scratch_shapes=[
-            pltpu.VMEM((count, HD), jnp.bfloat16),
-            held,
-            held,
-            pltpu.VMEM((count, HD), jnp.float32),
+            pltpu.VMEM(mine.shape, jnp.float32),
+            pltpu.VMEM(cross.shape, jnp.float32),
             pltpu.VMEM((4, 8, HD), jnp.float32),
             pltpu.VMEM(gate.shape, jnp.float32),
-            pltpu.SemaphoreType.DMA((2,)),
+            pltpu.SemaphoreType.DMA((3,)),
         ],
         compiler_params=PARAMS,
         cost_estimate=cost(1),
         name="merge",
-    )(text_len, cross, back, gate)
+    )(mine, cross, back, gate)
 
 
 def to_heads(array):
@@ -562,15 +614,19 @@
 ):
     packed = pack(queries, keys, values, cross_queries)
     received = to_heads(packed)
-    q, kv = unpack(received, text_keys, text_values)
-    cross = unpack_cross(received)
+    q, kv, text = unpack(received, text_keys, text_values)
     kv_core = swap(kv, core_of)
     kv_near = swap(kv, across_y1)
     begun = first(group_ids, q, kv, kv_core)
     q, kv_core = lax.optimization_barrier((q, kv_core))
+    text, begun = lax.optimization_barrier((text, begun))
+    text = lax.all_to_all(text, "group", split_axis=0, concat_axis=0, tiled=True)
     blocks = (kv, kv_core, kv_near, swap(kv_near, core_of))
-    back = in_cluster(attend(group_ids, in_cluster(q), blocks, begun))
-    mixed = merge(text_len, cross, back, group_gate)
+    q = in_cluster(q)
+    sent, q, text = lax.optimization_barrier((attend(group_ids, q, blocks), q, text))
+    back = in_cluster(sent)
+    mine = own(group_ids, q, blocks, begun)
+    mixed = merge(mine, cross_part(text_len, received, text), back, group_gate)
     count = mixed.shape[0]
     heads = lax.axis_size("seq")
     mixed = to_heads(mixed.reshape(heads, count // heads, HD))

time: 165 us -> 169 us (1.024)
  the two profiles are of different devices: /device:TPU:24 before, /device:TPU:1 now
where the time goes in v4:
time: 169 us; the launch traced here: 168 us
  blocking collectives  87.4 us (52%)
  starting transfers between devices  44.6 us (26%)
  Pallas kernels  28.5 us (17%)
  waiting for transfers between devices  4.17 us (2%)
  local copies, waits for them, and re-layouts  2.56 us (2%)
    all_to_all x2, blocking collectives, to_heads(): return lax.all_to_all(array, 'seq', split_axis=0, concat_axis=0, tiled=True)  87.4 us
    all_to_all x2, starting transfers between devices, in_cluster(): lax.all_to_all(array, 'group', split_axis=0, concat_axis=0, axis_index_gr...  30.2 us
    pallas_call x1, Pallas kernels, own(): pl.pallas_call(own_kernel, in_specs=[SMEM] + [VMEM] * 5 + [HBM] * 2, out_...  10.2 us
    ppermute x3, starting transfers between devices, swap(): return lax.ppermute(array, 'group', [(i, partner(i)) for i in range(16)])  9.32 us
    pallas_call x1, Pallas kernels, attend(): pl.pallas_call(attend_kernel, in_specs=[SMEM] + [VMEM] * 5, out_specs=VME...  8.22 us
    all_to_all x1, starting transfers between devices, body(): lax.all_to_all(text, 'group', split_axis=0, concat_axis=0, tiled=True)  5.03 us
    ppermute x3, waiting for transfers between devices, swap(): return lax.ppermute(array, 'group', [(i, partner(i)) for i in range(16)])  3.88 us
    pallas_call x1, Pallas kernels, first(): pl.pallas_call(first_kernel, in_specs=[SMEM] + [VMEM] * 3, out_specs=[HBM...  3.51 us
  transfers between devices with their start and end apart: 6, of which 2 were waited for; matrix products, arithmetic and copies ran while one was open for 0% of the time, Pallas kernels for 14%

profile of v4, /device:TPU:1, one launch (start us, length us, event | category | flops | bytes accessed | tf_op | source)
XLA Modules:
  0.0 168.1 jit_solution(16630831727660278186)
XLA Ops:
  0.0 2.2 %pack.1 = bf16[32,4,24,128]{3,2,1,0:T(8,128)(2,1)} custom-call(bf16[1,24,4096]{2,1,0:T(8,128)(2,1)} %q_hbm.1, bf16[1,24,4096]{2,1,0:T(8,128)(2,1)} %k_hbm.1, bf16[1,24,4096]{2,1,0:T(8,128)(2,1)} %v_hbm.1, bf16[1,24,4096]{2,1,0:T(8,128)(2,1)} %c_hbm.1), custom_call_target="tpu_custom_call" | custom-call | tf_op jit(solution)/shard_map/pack/pallas_call | solution.py:103
  2.2 0.0 copy-start.6
  2.2 0.0 copy-start.7
  2.2 60.3 %all_to_all.25.in_ref = bf16[32,4,24,128]{3,2,1,0:T(8,128)(2,1)S(1)} all-to-all(bf16[32,4,24,128]{3,2,1,0:T(8,128)(2,1)} %pack.1), channel_id=1, replica_groups=mesh['group'=16,'seq'=32] {'seq'}, dimensions={0} | all-to-all | bytes 1572864 | tf_op jit(solution)/shard_map/all_to_all | solution.py:609
  62.5 0.0 copy-done.6
  62.5 0.0 copy-done.7
  62.5 1.8 %unpack.1 = (bf16[4,768,128]{2,1,0:T(8,128)(2,1)}, bf16[2,768,128]{2,1,0:T(8,128)(2,1)S(1)}, bf16[16,2,32,128]{3,2,1,0:T(8,128)(2,1)}) custom-call(bf16[32,4,24,128]{3,2,1,0:T(8,128)(2,1)S(1)} %all_to_all.25.in_ref, bf16[32,128]{1,0:T(8,128)(2,1)S(1)} %copy-done.6, bf16[32,128]{1,0:T(8,128)(2,1)S(1)} %copy-done.7), custom_call_target="tpu_custom_call" | custom-call | tf_op jit(solution)/shard_map/unpack/pallas_call | solution.py:165
  64.3 3.4 %collective-permute-start = (bf16[2,768,128]{2,1,0:T(8,128)(2,1)S(1)}, bf16[2,768,128]{2,1,0:T(8,128)(2,1)S(1)}, u32[]{:S(2)}, u32[]{:S(2)}) collective-permute-start(bf16[2,768,128]{2,1,0:T(8,128)(2,1)S(1)} %get-tuple-element.19.b0.one), channel_id=1, source_target_pairs={{0,32},{32,0},{64,96},{96,64},{128,160},{160,128},{192,224},{224,1... | collective-permute-start | bytes 1179656 | tf_op jit(solution)/shard_map/ppermute | solution.py:74
  67.7 3.2 %collective-permute-start.1 = (bf16[2,768,128]{2,1,0:T(8,128)(2,1)S(1)}, bf16[2,768,128]{2,1,0:T(8,128)(2,1)S(1)}, u32[]{:S(2)}, u32[]{:S(2)}) collective-permute-start(bf16[2,768,128]{2,1,0:T(8,128)(2,1)S(1)} %get-tuple-element.19.b0.one), channel_id=1, source_target_pairs={{0,64},{32,96},{64,0},{96,32},{128,192},{160,224},{192,128},{224,1... | collective-permute-start | bytes 1179656 | tf_op jit(solution)/shard_map/ppermute | solution.py:74
  70.9 0.0 collective-permute-done.b1.two
  70.9 0.0 copy-start
  70.9 0.0 copy-start.8
  71.0 5.5 %all-to-all-start.1 = ((bf16[4,768,128]{2,1,0:T(8,128)(2,1)}), bf16[4,768,128]{2,1,0:T(8,128)(2,1)S(1)}, u32[]{:S(2)}, u32[]{:S(2)}) async-start(bf16[4,768,128]{2,1,0:T(8,128)(2,1)} %get-tuple-element.20.q4_ref), calls=%async_computation.1 | async-start | bytes 1572864 | tf_op jit(solution)/shard_map/all_to_all | solution.py:68
  76.5 3.9 %collective-permute-done.1.b2 = bf16[2,768,128]{2,1,0:T(8,128)(2,1)S(1)} collective-permute-done((bf16[2,768,128]{2,1,0:T(8,128)(2,1)S(1)}, bf16[2,768,128]{2,1,0:T(8,128)(2,1)S(1)}, u32[]{:S(2)}, u32[]{:S(2)}) %collective-permute-start.1) | collective-permute-done | bytes 393248 | tf_op jit(solution)/shard_map/ppermute | solution.py:74
  80.3 0.0 copy-start.2
  80.3 2.7 %collective-permute-start.2 = (bf16[2,768,128]{2,1,0:T(8,128)(2,1)S(1)}, bf16[2,768,128]{2,1,0:T(8,128)(2,1)}, u32[]{:S(2)}, u32[]{:S(2)}) collective-permute-start(bf16[2,768,128]{2,1,0:T(8,128)(2,1)S(1)} %collective-permute-done.1.b2), channel_id=1, source_target_pairs={{0,32},{32,0},{64,96},{96,64},{128,160},{160,128},{192,224},{224,1... | collective-permute-start | bytes 1179656 | tf_op jit(solution)/shard_map/ppermute | solution.py:74
  83.0 0.0 copy-done.8
  83.0 3.5 %first.1 = (f32[1,2,1,384]{3,2,1,0:T(1,128)S(1)}, f32[1,2,144,384]{3,2,1,0:T(8,128)S(1)}) custom-call(s32[16]{0:T(128)S(1)} %copy-done.8, bf16[4,768,128]{2,1,0:T(8,128)(2,1)} %get-tuple-element.20.q4_ref, bf16[2,768,128]{2,1,0:T(8,128)(2,1)S(1)} %get-tuple-element.19.b0.one, bf16[2,768,128]{2,1,0:T(8,128)(2,1)S(1)} %collective-permute-done.b1.two), custom_call_target="tpu_custom_call" | custom-call | flops 603979776 | bytes 1048576 | tf_op jit(solution)/shard_map/first/pallas_call | solution.py:440
  86.6 0.3 all-to-all-done.1.q_ref
  86.9 5.0 %all-to-all-start.2 = ((bf16[16,2,32,128]{3,2,1,0:T(8,128)(2,1)}), bf16[16,2,32,128]{3,2,1,0:T(8,128)(2,1)S(1)}, u32[]{:S(2)}, u32[]{:S(2)}) async-start(bf16[16,2,32,128]{3,2,1,0:T(8,128)(2,1)} %get-tuple-element.25), calls=%async_computation.2 | async-start | bytes 524288 | tf_op jit(solution)/shard_map/all_to_all | solution.py:623
  91.9 0.0 collective-permute-done.2.b3
  91.9 0.0 copy-done
  91.9 0.0 copy-done.2
  91.9 8.2 %attend.1 = bf16[4,800,128]{2,1,0:T(8,128)(2,1)} custom-call(s32[16]{0:T(128)S(1)} %copy-done.8, bf16[4,768,128]{2,1,0:T(8,128)(2,1)S(1)} %all-to-all-done.1.q_ref, bf16[2,768,128]{2,1,0:T(8,128)(2,1)S(1)} %get-tuple-element.19.b0.one, bf16[2,768,128]{2,1,0:T(8,128)(2,1)S(1)} %collective-permute-done.b1.two, ...), custom_call_target="tpu_custom_call" | custom-call | flops 3623878656 | bytes 6291456 | tf_op jit(solution)/shard_map/attend/pallas_call | solution.py:472
  100.1 0.0 all-to-all-done.2.text_ref
  100.1 24.7 %all-to-all-start.3 = ((bf16[4,800,128]{2,1,0:T(8,128)(2,1)}), bf16[4,800,128]{2,1,0:T(8,128)(2,1)S(1)}, u32[]{:S(2)}, u32[]{:S(2)}) async-start(bf16[4,800,128]{2,1,0:T(8,128)(2,1)} %attend.1), calls=%async_computation.3 | async-start | bytes 1638400 | tf_op jit(solution)/shard_map/all_to_all | solution.py:68
  125.5 0.0 copy-start.1
  125.5 0.0 copy-start.3
  125.5 1.6 cross.1.cross_hbm
  127.1 0.0 copy-start.4
  127.1 0.7 copy-done.4
  127.8 0.0 copy-done.1
  127.8 0.0 copy-done.3
  127.8 0.0 copy-start.9
  127.8 10.2 %own.1.own_hbm = f32[776,128]{1,0:T(8,128)S(1)} custom-call(s32[16]{0:T(128)S(1)} %copy-done.8, bf16[4,768,128]{2,1,0:T(8,128)(2,1)S(1)} %all-to-all-done.1.q_ref, bf16[2,768,128]{2,1,0:T(8,128)(2,1)S(1)} %get-tuple-element.19.b0.one, bf16[2,768,128]{2,1,0:T(8,128)(2,1)S(1)} %copy-done.1, bf16[2,768,128]{2,1,0:T(8,128)(2,1)S(1)} %copy-done.3, ...), custom_call_target="tpu_custom_call" | custom-call | flops 603979776 | bytes 1048576 | tf_op jit(solution)/shard_map/own/pallas_call | solution.py:486
  138.0 0.0 all-to-all-done.3.back_ref
  138.0 0.0 copy-done.9
  138.0 0.0 copy-start.5
  138.0 1.0 copy-done.5
  139.0 1.1 merge.1
  140.1 27.1 %all_to_all.26 = bf16[32,24,128]{2,1,0:T(8,128)(2,1)S(1)} all-to-all(bf16[32,24,128]{2,1,0:T(8,128)(2,1)S(1)} %bitcast.2), channel_id=1, replica_groups=mesh['group'=16,'seq'=32] {'seq'}, dimensions={0} | all-to-all | bytes 393216 | tf_op jit(solution)/shard_map/all_to_all | solution.py:609
  167.3 0.8 reshape.7
  (1 shorter events, 0.0 us)
Async XLA Ops:
  2.2 60.3 %copy-start.6 = (bf16[32,128]{1,0:T(8,128)(2,1)S(1)}, bf16[32,128]{1,0:T(8,128)(2,1)}, u32[]{:S(2)}) copy-start(bf16[32,128]{1,0:T(8,128)(2,1)} %tk_hbm.1) | copy-start | bytes 24580
  2.2 60.3 %copy-start.7 = (bf16[32,128]{1,0:T(8,128)(2,1)S(1)}, bf16[32,128]{1,0:T(8,128)(2,1)}, u32[]{:S(2)}) copy-start(bf16[32,128]{1,0:T(8,128)(2,1)} %tv_hbm.1) | copy-start | bytes 24580
  64.3 6.6 %collective-permute-start = (bf16[2,768,128]{2,1,0:T(8,128)(2,1)S(1)}, bf16[2,768,128]{2,1,0:T(8,128)(2,1)S(1)}, u32[]{:S(2)}, u32[]{:S(2)}) collective-permute-start(bf16[2,768,128]{2,1,0:T(8,128)(2,1)S(1)} %get-tuple-element.19.b0.one), channel_id=1, source_target_pairs={{0,32},{32,0},{64,96},{96,64},{128,160},{160,128},{192,224},{224,1... | collective-permute-start | bytes 1179656 | tf_op jit(solution)/shard_map/ppermute | solution.py:74
  67.7 12.6 %collective-permute-start.1 = (bf16[2,768,128]{2,1,0:T(8,128)(2,1)S(1)}, bf16[2,768,128]{2,1,0:T(8,128)(2,1)S(1)}, u32[]{:S(2)}, u32[]{:S(2)}) collective-permute-start(bf16[2,768,128]{2,1,0:T(8,128)(2,1)S(1)} %get-tuple-element.19.b0.one), channel_id=1, source_target_pairs={{0,64},{32,96},{64,0},{96,32},{128,192},{160,224},{192,128},{224,1... | collective-permute-start | bytes 1179656 | tf_op jit(solution)/shard_map/ppermute | solution.py:74
  70.9 21.0 %copy-start = (bf16[2,768,128]{2,1,0:T(8,128)(2,1)}, bf16[2,768,128]{2,1,0:T(8,128)(2,1)S(1)}, u32[]{:S(2)}) copy-start(bf16[2,768,128]{2,1,0:T(8,128)(2,1)S(1)} %collective-permute-done.b1.two) | copy-start | bytes 1179652
  70.9 12.1 %copy-start.8 = (s32[16]{0:T(128)S(1)}, s32[16]{0:T(128)}, u32[]{:S(2)}) copy-start(s32[16]{0:T(128)} %ids_ref.5) | copy-start | bytes 196
  71.0 15.9 %all-to-all-start.1 = ((bf16[4,768,128]{2,1,0:T(8,128)(2,1)}), bf16[4,768,128]{2,1,0:T(8,128)(2,1)S(1)}, u32[]{:S(2)}, u32[]{:S(2)}) async-start(bf16[4,768,128]{2,1,0:T(8,128)(2,1)} %get-tuple-element.20.q4_ref), calls=%async_computation.1 | async-start | bytes 1572864 | tf_op jit(solution)/shard_map/all_to_all | solution.py:68
  80.3 11.6 %copy-start.2 = (bf16[2,768,128]{2,1,0:T(8,128)(2,1)}, bf16[2,768,128]{2,1,0:T(8,128)(2,1)S(1)}, u32[]{:S(2)}) copy-start(bf16[2,768,128]{2,1,0:T(8,128)(2,1)S(1)} %collective-permute-done.1.b2) | copy-start | bytes 1179652
  80.3 11.5 %collective-permute-start.2 = (bf16[2,768,128]{2,1,0:T(8,128)(2,1)S(1)}, bf16[2,768,128]{2,1,0:T(8,128)(2,1)}, u32[]{:S(2)}, u32[]{:S(2)}) collective-permute-start(bf16[2,768,128]{2,1,0:T(8,128)(2,1)S(1)} %collective-permute-done.1.b2), channel_id=1, source_target_pairs={{0,32},{32,0},{64,96},{96,64},{128,160},{160,128},{192,224},{224,1... | collective-permute-start | bytes 1179656 | tf_op jit(solution)/shard_map/ppermute | solution.py:74
  86.9 13.3 %all-to-all-start.2 = ((bf16[16,2,32,128]{3,2,1,0:T(8,128)(2,1)}), bf16[16,2,32,128]{3,2,1,0:T(8,128)(2,1)S(1)}, u32[]{:S(2)}, u32[]{:S(2)}) async-start(bf16[16,2,32,128]{3,2,1,0:T(8,128)(2,1)} %get-tuple-element.25), calls=%async_computation.2 | async-start | bytes 524288 | tf_op jit(solution)/shard_map/all_to_all | solution.py:623
  100.1 37.9 %all-to-all-start.3 = ((bf16[4,800,128]{2,1,0:T(8,128)(2,1)}), bf16[4,800,128]{2,1,0:T(8,128)(2,1)S(1)}, u32[]{:S(2)}, u32[]{:S(2)}) async-start(bf16[4,800,128]{2,1,0:T(8,128)(2,1)} %attend.1), calls=%async_computation.3 | async-start | bytes 1638400 | tf_op jit(solution)/shard_map/all_to_all | solution.py:68
  125.5 2.3 %copy-start.1 = (bf16[2,768,128]{2,1,0:T(8,128)(2,1)S(1)}, bf16[2,768,128]{2,1,0:T(8,128)(2,1)}, u32[]{:S(2)}) copy-start(bf16[2,768,128]{2,1,0:T(8,128)(2,1)} %copy-done) | copy-start | bytes 1179652
  125.5 2.3 %copy-start.3 = (bf16[2,768,128]{2,1,0:T(8,128)(2,1)S(1)}, bf16[2,768,128]{2,1,0:T(8,128)(2,1)}, u32[]{:S(2)}) copy-start(bf16[2,768,128]{2,1,0:T(8,128)(2,1)} %copy-done.2) | copy-start | bytes 1179652
  127.1 0.7 copy-start.4
  127.8 10.2 %copy-start.9 = (f32[1,128]{1,0:T(1,128)S(1)}, f32[1,128]{1,0:T(1,128)}, u32[]{:S(2)}) copy-start(f32[1,128]{1,0:T(1,128)} %gate_hbm.1) | copy-start | bytes 1540
  138.0 1.0 copy-start.5

commit v5 on v4

--- a/solution.py
+++ b/solution.py
@@ -201,8 +201,13 @@
     return slot, core_of(slot), near, core_of(near)
 
 
-def pieces_of(block, count):
-    return block[0, pl.ds(0, count), :], with_ones(features_first(block[1, pl.ds(0, count), :]))
+def keys_of(blocks, count):
+    return jnp.concatenate([block[0, pl.ds(0, count), :] for block in blocks], axis=0)
+
+
+def values_of(blocks, count):
+    parts = [features_first(block[1, pl.ds(0, count), :]) for block in blocks]
+    return with_ones(jnp.concatenate(parts, axis=1))
 
 
 def half_of(q_ref, half):
@@ -229,47 +234,61 @@
         top_ref[place, half] = jnp.max(s, axis=0, keepdims=True)
 
 
-def add_listed(length, list_ref, held, queries, top_ref, sum_ref, scores):
+def add_listed(length, list_ref, width, held, queries, top_ref, sum_ref, scores):
     count = held.shape[2]
     last = len(scores) - 1
+    scores = [ref.at[pl.ds(0, width * count), :] for ref in scores]
 
     def item(index):
         code = list_ref[index]
-        return code // 4, held.at[code % 4]
-
-    def keys(block):
-        return block[0, pl.ds(0, count), :]
-
-    place, block = item(0)
-    scores[0][...] = scores_of(keys(block), half_of(queries.at[place], 0))
-
-    @pl.loop(0, length)
-    def _(index):
-        place, block = item(index)
-        k, v = pieces_of(block, count)
-        after, block = item(jnp.minimum(index + 1, length - 1))
-        for tile in range(last + 1):
-            if tile < last:
+        blocks = [held.at[code // 4**digit % 4] for digit in range(width)]
+        return code // 4**width, blocks
+
+    @pl.when(length > 0)
+    def _():
+        place, blocks = item(0)
+        scores[0][...] = scores_of(keys_of(blocks, count), half_of(queries.at[place], 0))
+
+        @pl.loop(0, length)
+        def _(index):
+            place, blocks = item(index)
+            k, v = keys_of(blocks, count), values_of(blocks, count)
+            after, blocks = item(jnp.minimum(index + 1, length - 1))
+            for tile in range(last):
                 scores[tile + 1][...] = scores_of(k, half_of(queries.at[place], tile + 1))
                 mix(place, tile, scores[tile][...], v, top_ref, sum_ref)
-            else:
-                held_scores = scores[last][...]
-                scores[0][...] = scores_of(keys(block), half_of(queries.at[after], 0))
-                mix(place, tile, held_scores, v, top_ref, sum_ref)
+            final = scores[last][...]
+            scores[0][...] = scores_of(keys_of(blocks, count), half_of(queries.at[after], 0))
+            mix(place, last, final, v, top_ref, sum_ref)
+
+
+def add_seen(sees, held, queries, top_ref, sum_ref, pair_ref, one_ref, scores):
+    pairs, ones = jnp.int32(0), jnp.int32(0)
+    for place, row in enumerate(sees):
+        waiting, waits = jnp.int32(0), jnp.int32(0)
+        for block, see in row:
+            pair_ref[pairs] = 16 * place + 4 * waiting + block
+            pairs = pairs + see * waits
+            waiting = jnp.where(waits > 0, waiting, block)
+            waits = (waits + see) % 2
+            waiting = jnp.where(waits > 0, waiting, 0)
+        one_ref[ones] = 4 * place + waiting
+        ones = ones + waits
+    add_listed(pairs, pair_ref, 2, held, queries, top_ref, sum_ref, scores)
+    add_listed(ones, one_ref, 1, held, queries, top_ref, sum_ref, scores)
 
 
 def first_kernel(
-    ids_ref, q4_ref, one, two, top_hbm, sum_hbm, held, top_ref, sum_ref, sems, list_ref, *scores
+    ids_ref, q4_ref, one, two, top_hbm, sum_hbm, held, top_ref, sum_ref, sems, pair_ref, one_ref, *scores
 ):
     slot = lax.axis_index("group")
     q_ref = q4_ref.at[0]
     hold(held, (one, two))
     sum_ref[...] = jnp.zeros_like(sum_ref)
     estimate(0, q_ref, one[0, pl.ds(0, HD), :], top_ref)
-    list_ref[0] = 0
-    list_ref[1] = 1
-    length = 1 + (ids_ref[core_of(slot)] <= ids_ref[slot]).astype(jnp.int32)
-    add_listed(length, list_ref, held, q4_ref, top_ref, sum_ref, scores)
+    see = (ids_ref[core_of(slot)] <= ids_ref[slot]).astype(jnp.int32)
+    sees = [[(0, jnp.int32(1)), (1, see)]]
+    add_seen(sees, held, q4_ref, top_ref, sum_ref, pair_ref, one_ref, scores)
     copies = [
         pltpu.make_async_copy(top_ref, top_hbm, sems.at[0]),
         pltpu.make_async_copy(sum_ref, sum_hbm, sems.at[1]),
@@ -281,7 +300,7 @@
 
 
 def attend_to(
-    steps, begun, ids_ref, q_ref, blocks, queries, held, top_ref, sum_ref, list_ref, full_ref, scores
+    steps, begun, ids_ref, q_ref, blocks, queries, held, top_ref, sum_ref, pair_ref, one_ref, full_ref, scores
 ):
     slot = lax.axis_index("group")
     hold(held, blocks)
@@ -296,25 +315,25 @@
             sum_ref[number] = jnp.zeros_like(sum_ref[number])
             estimate(number, queries.at[number], blocks[0][0, pl.ds(0, HD), :], top_ref)
 
-    list_ref[0] = 0
-    length = jnp.int32(0)
+    sees = []
     full_length = jnp.int32(0)
     seen = []
     for number, step in enumerate(steps):
         rank = ids_ref[OWNERS[step](slot)]
         before = full_length
+        row = []
         for block, group in enumerate(key_groups(slot)):
             see = (ids_ref[group] <= rank).astype(jnp.int32)
             full_ref[full_length] = 4 * number + block
             full_length = full_length + see
             if block > 1 or not begun:
-                list_ref[length] = 4 * number + block
-                length = length + see
+                row.append((block, see))
+        sees.append(row)
         seen.append(full_length > before)
     if begun:
         for copy in begun:
             copy.wait()
-    add_listed(length, list_ref, held, queries, top_ref, sum_ref, scores)
+    add_seen(sees, held, queries, top_ref, sum_ref, pair_ref, one_ref, scores)
 
     inside = jnp.bool_(True)
     for number, some in enumerate(seen):
@@ -333,7 +352,7 @@
             code = full_ref[index // halves]
             number, block = code // 4, code % 4
             half = index % halves
-            k, v = pieces_of(held.at[block], count)
+            k, v = keys_of([held.at[block]], count), values_of([held.at[block]], count)
             where = pl.ds(pl.multiple_of(half * TILE, TILE), TILE)
             s = scores_of(k, queries[number, where, :])
             old = top_ref[number, half]
@@ -345,11 +364,11 @@
 
 def attend_kernel(
     ids_ref, q_ref, b0, b1, b2, b3,
-    out_ref, queries, held, top_ref, sum_ref, list_ref, full_ref, *scores,
+    out_ref, queries, held, top_ref, sum_ref, pair_ref, one_ref, full_ref, *scores,
 ):
     attend_to(
         (1, 2, 3), (), ids_ref, q_ref, (b0, b1, b2, b3),
-        queries, held, top_ref, sum_ref, list_ref, full_ref, scores,
+        queries, held, top_ref, sum_ref, pair_ref, one_ref, full_ref, scores,
     )
     slot = lax.axis_index("group")
     count = held.shape[2]
@@ -375,7 +394,7 @@
 
 def own_kernel(
     ids_ref, q_ref, b0, b1, b2, b3, top_hbm, sum_hbm,
-    out_ref, queries, held, top_ref, sum_ref, sems, list_ref, full_ref, *scores,
+    out_ref, queries, held, top_ref, sum_ref, sems, pair_ref, one_ref, full_ref, *scores,
 ):
     copies = [
         pltpu.make_async_copy(top_hbm, top_ref, sems.at[0]),
@@ -385,7 +404,7 @@
         copy.start()
     attend_to(
         (0,), copies, ids_ref, q_ref, (b0, b1, b2, b3),
-        queries, held, top_ref, sum_ref, list_ref, full_ref, scores,
+        queries, held, top_ref, sum_ref, pair_ref, one_ref, full_ref, scores,
     )
     count = held.shape[2]
 
@@ -432,7 +451,7 @@
 
 
 def scores_scratch(count):
-    return [pltpu.VMEM((count, TILE), jnp.float32)] * (count // TILE)
+    return [pltpu.VMEM((2 * count, TILE), jnp.float32)] * (count // TILE)
 
 
 def first(group_ids, q, one, two):
@@ -447,6 +466,7 @@
             *(pltpu.VMEM(one.shape, one.dtype) for one in state(1, count)),
             pltpu.SemaphoreType.DMA((2,)),
             pltpu.SMEM((4,), jnp.int32),
+            pltpu.SMEM((4,), jnp.int32),
             *scores_scratch(count),
         ],
         compiler_params=PARAMS,
@@ -464,7 +484,7 @@
 
 
 def lists(places):
-    return [pltpu.SMEM((4 * places + 4,), jnp.int32)] * 2
+    return [pltpu.SMEM((4 * places + 4,), jnp.int32)] * 3
 
 
 def attend(group_ids, queries, blocks):

time: 169 us -> 166 us (0.982)
  the two profiles are of different devices: /device:TPU:1 before, /device:TPU:11 now
where the time goes in v5:
time: 166 us; the launch traced here: 165 us
  blocking collectives  83.8 us (50%)
  Pallas kernels  45.2 us (27%)
  starting transfers between devices  27.3 us (16%)
  waiting for transfers between devices  5.77 us (3%)
  local copies, waits for them, and re-layouts  2.56 us (2%)
    all_to_all x2, blocking collectives, to_heads(): return lax.all_to_all(array, 'seq', split_axis=0, concat_axis=0, tiled=True)  83.8 us
    pallas_call x1, Pallas kernels, attend(): pl.pallas_call(attend_kernel, in_specs=[SMEM] + [VMEM] * 5, out_specs=VME...  25 us
    all_to_all x2, starting transfers between devices, in_cluster(): lax.all_to_all(array, 'group', split_axis=0, concat_axis=0, axis_index_gr...  12.9 us
    pallas_call x1, Pallas kernels, own(): pl.pallas_call(own_kernel, in_specs=[SMEM] + [VMEM] * 5 + [HBM] * 2, out_...  10 us
    ppermute x3, starting transfers between devices, swap(): return lax.ppermute(array, 'group', [(i, partner(i)) for i in range(16)])  8.19 us
    all_to_all x1, starting transfers between devices, body(): lax.all_to_all(text, 'group', split_axis=0, concat_axis=0, tiled=True)  6.22 us
    ppermute x3, waiting for transfers between devices, swap(): return lax.ppermute(array, 'group', [(i, partner(i)) for i in range(16)])  5.76 us
    pallas_call x1, Pallas kernels, first(): pl.pallas_call(first_kernel, in_specs=[SMEM] + [VMEM] * 3, out_specs=[HBM...  3.55 us
  transfers between devices with their start and end apart: 6, of which 1 were waited for; matrix products, arithmetic and copies ran while one was open for 0% of the time, Pallas kernels for 24%

profile of v5, /device:TPU:11, one launch (start us, length us, event | category | flops | bytes accessed | tf_op | source)
XLA Modules:
  0.0 165.4 jit_solution(18004841010528827715)
XLA Ops:
  0.0 2.2 %pack.1 = bf16[32,4,24,128]{3,2,1,0:T(8,128)(2,1)} custom-call(bf16[1,24,4096]{2,1,0:T(8,128)(2,1)} %q_hbm.1, bf16[1,24,4096]{2,1,0:T(8,128)(2,1)} %k_hbm.1, bf16[1,24,4096]{2,1,0:T(8,128)(2,1)} %v_hbm.1, bf16[1,24,4096]{2,1,0:T(8,128)(2,1)} %c_hbm.1), custom_call_target="tpu_custom_call" | custom-call | tf_op jit(solution)/shard_map/pack/pallas_call | solution.py:103
  2.2 0.0 copy-start.6
  2.2 0.0 copy-start.7
  2.2 58.5 %all_to_all.25.in_ref = bf16[32,4,24,128]{3,2,1,0:T(8,128)(2,1)S(1)} all-to-all(bf16[32,4,24,128]{3,2,1,0:T(8,128)(2,1)} %pack.1), channel_id=1, replica_groups=mesh['group'=16,'seq'=32] {'seq'}, dimensions={0} | all-to-all | bytes 1572864 | tf_op jit(solution)/shard_map/all_to_all | solution.py:629
  60.7 0.0 copy-done.6
  60.7 0.0 copy-done.7
  60.7 1.8 %unpack.1 = (bf16[4,768,128]{2,1,0:T(8,128)(2,1)}, bf16[2,768,128]{2,1,0:T(8,128)(2,1)S(1)}, bf16[16,2,32,128]{3,2,1,0:T(8,128)(2,1)}) custom-call(bf16[32,4,24,128]{3,2,1,0:T(8,128)(2,1)S(1)} %all_to_all.25.in_ref, bf16[32,128]{1,0:T(8,128)(2,1)S(1)} %copy-done.6, bf16[32,128]{1,0:T(8,128)(2,1)S(1)} %copy-done.7), custom_call_target="tpu_custom_call" | custom-call | tf_op jit(solution)/shard_map/unpack/pallas_call | solution.py:165
  62.5 3.4 %collective-permute-start = (bf16[2,768,128]{2,1,0:T(8,128)(2,1)S(1)}, bf16[2,768,128]{2,1,0:T(8,128)(2,1)S(1)}, u32[]{:S(2)}, u32[]{:S(2)}) collective-permute-start(bf16[2,768,128]{2,1,0:T(8,128)(2,1)S(1)} %get-tuple-element.19.b0.one), channel_id=1, source_target_pairs={{0,32},{32,0},{64,96},{96,64},{128,160},{160,128},{192,224},{224,1... | collective-permute-start | bytes 1179656 | tf_op jit(solution)/shard_map/ppermute | solution.py:74
  66.0 2.1 %collective-permute-start.1 = (bf16[2,768,128]{2,1,0:T(8,128)(2,1)S(1)}, bf16[2,768,128]{2,1,0:T(8,128)(2,1)S(1)}, u32[]{:S(2)}, u32[]{:S(2)}) collective-permute-start(bf16[2,768,128]{2,1,0:T(8,128)(2,1)S(1)} %get-tuple-element.19.b0.one), channel_id=1, source_target_pairs={{0,64},{32,96},{64,0},{96,32},{128,192},{160,224},{192,128},{224,1... | collective-permute-start | bytes 1179656 | tf_op jit(solution)/shard_map/ppermute | solution.py:74
  68.1 0.0 collective-permute-done.b1.two
  68.1 0.0 copy-start
  68.1 0.0 copy-start.8
  68.1 4.8 %all-to-all-start.1 = ((bf16[4,768,128]{2,1,0:T(8,128)(2,1)}), bf16[4,768,128]{2,1,0:T(8,128)(2,1)S(1)}, u32[]{:S(2)}, u32[]{:S(2)}) async-start(bf16[4,768,128]{2,1,0:T(8,128)(2,1)} %get-tuple-element.20.q4_ref), calls=%async_computation.1 | async-start | bytes 1572864 | tf_op jit(solution)/shard_map/all_to_all | solution.py:68
  72.9 5.8 %collective-permute-done.1.b2 = bf16[2,768,128]{2,1,0:T(8,128)(2,1)S(1)} collective-permute-done((bf16[2,768,128]{2,1,0:T(8,128)(2,1)S(1)}, bf16[2,768,128]{2,1,0:T(8,128)(2,1)S(1)}, u32[]{:S(2)}, u32[]{:S(2)}) %collective-permute-start.1) | collective-permute-done | bytes 393248 | tf_op jit(solution)/shard_map/ppermute | solution.py:74
  78.6 0.0 copy-start.2
  78.6 2.7 %collective-permute-start.2 = (bf16[2,768,128]{2,1,0:T(8,128)(2,1)S(1)}, bf16[2,768,128]{2,1,0:T(8,128)(2,1)}, u32[]{:S(2)}, u32[]{:S(2)}) collective-permute-start(bf16[2,768,128]{2,1,0:T(8,128)(2,1)S(1)} %collective-permute-done.1.b2), channel_id=1, source_target_pairs={{0,32},{32,0},{64,96},{96,64},{128,160},{160,128},{192,224},{224,1... | collective-permute-start | bytes 1179656 | tf_op jit(solution)/shard_map/ppermute | solution.py:74
  81.3 0.0 copy-done.8
  81.3 3.6 %first.1 = (f32[1,2,1,384]{3,2,1,0:T(1,128)S(1)}, f32[1,2,144,384]{3,2,1,0:T(8,128)S(1)}) custom-call(s32[16]{0:T(128)S(1)} %copy-done.8, bf16[4,768,128]{2,1,0:T(8,128)(2,1)} %get-tuple-element.20.q4_ref, bf16[2,768,128]{2,1,0:T(8,128)(2,1)S(1)} %get-tuple-element.19.b0.one, bf16[2,768,128]{2,1,0:T(8,128)(2,1)S(1)} %collective-permute-done.b1.two), custom_call_target="tpu_custom_call" | custom-call | flops 603979776 | bytes 1048576 | tf_op jit(solution)/shard_map/first/pallas_call | solution.py:459
  84.9 0.0 all-to-all-done.1.q_ref
  84.9 6.2 %all-to-all-start.2 = ((bf16[16,2,32,128]{3,2,1,0:T(8,128)(2,1)}), bf16[16,2,32,128]{3,2,1,0:T(8,128)(2,1)S(1)}, u32[]{:S(2)}, u32[]{:S(2)}) async-start(bf16[16,2,32,128]{3,2,1,0:T(8,128)(2,1)} %get-tuple-element.25), calls=%async_computation.2 | async-start | bytes 524288 | tf_op jit(solution)/shard_map/all_to_all | solution.py:643
  91.1 0.0 collective-permute-done.2.b3
  91.1 0.0 copy-done
  91.1 0.0 copy-done.2
  91.1 25.0 %attend.1 = bf16[4,800,128]{2,1,0:T(8,128)(2,1)} custom-call(s32[16]{0:T(128)S(1)} %copy-done.8, bf16[4,768,128]{2,1,0:T(8,128)(2,1)S(1)} %all-to-all-done.1.q_ref, bf16[2,768,128]{2,1,0:T(8,128)(2,1)S(1)} %get-tuple-element.19.b0.one, bf16[2,768,128]{2,1,0:T(8,128)(2,1)S(1)} %collective-permute-done.b1.two, ...), custom_call_target="tpu_custom_call" | custom-call | flops 3623878656 | bytes 6291456 | tf_op jit(solution)/shard_map/attend/pallas_call | solution.py:492
  116.1 0.0 all-to-all-done.2.text_ref
  116.1 8.1 %all-to-all-start.3 = ((bf16[4,800,128]{2,1,0:T(8,128)(2,1)}), bf16[4,800,128]{2,1,0:T(8,128)(2,1)S(1)}, u32[]{:S(2)}, u32[]{:S(2)}) async-start(bf16[4,800,128]{2,1,0:T(8,128)(2,1)} %attend.1), calls=%async_computation.3 | async-start | bytes 1638400 | tf_op jit(solution)/shard_map/all_to_all | solution.py:68
  124.9 0.0 copy-start.1
  124.9 0.0 copy-start.3
  124.9 1.6 cross.1.cross_hbm
  126.5 0.0 copy-start.4
  126.5 0.7 copy-done.4
  127.2 0.0 copy-done.1
  127.2 0.0 copy-done.3
  127.2 0.0 copy-start.9
  127.2 10.0 %own.1.own_hbm = f32[776,128]{1,0:T(8,128)S(1)} custom-call(s32[16]{0:T(128)S(1)} %copy-done.8, bf16[4,768,128]{2,1,0:T(8,128)(2,1)S(1)} %all-to-all-done.1.q_ref, bf16[2,768,128]{2,1,0:T(8,128)(2,1)S(1)} %get-tuple-element.19.b0.one, bf16[2,768,128]{2,1,0:T(8,128)(2,1)S(1)} %copy-done.1, bf16[2,768,128]{2,1,0:T(8,128)(2,1)S(1)} %copy-done.3, ...), custom_call_target="tpu_custom_call" | custom-call | flops 603979776 | bytes 1048576 | tf_op jit(solution)/shard_map/own/pallas_call | solution.py:506
  137.3 0.0 all-to-all-done.3.back_ref
  137.3 0.0 copy-done.9
  137.3 0.0 copy-start.5
  137.3 1.0 copy-done.5
  138.3 1.1 merge.1
  139.4 25.2 %all_to_all.26 = bf16[32,24,128]{2,1,0:T(8,128)(2,1)S(1)} all-to-all(bf16[32,24,128]{2,1,0:T(8,128)(2,1)S(1)} %bitcast.2), channel_id=1, replica_groups=mesh['group'=16,'seq'=32] {'seq'}, dimensions={0} | all-to-all | bytes 393216 | tf_op jit(solution)/shard_map/all_to_all | solution.py:629
  164.6 0.8 reshape.7
  (1 shorter events, 0.0 us)
Async XLA Ops:
  2.2 58.6 %copy-start.6 = (bf16[32,128]{1,0:T(8,128)(2,1)S(1)}, bf16[32,128]{1,0:T(8,128)(2,1)}, u32[]{:S(2)}) copy-start(bf16[32,128]{1,0:T(8,128)(2,1)} %tk_hbm.1) | copy-start | bytes 24580
  2.2 58.6 %copy-start.7 = (bf16[32,128]{1,0:T(8,128)(2,1)S(1)}, bf16[32,128]{1,0:T(8,128)(2,1)}, u32[]{:S(2)}) copy-start(bf16[32,128]{1,0:T(8,128)(2,1)} %tv_hbm.1) | copy-start | bytes 24580
  62.5 5.5 %collective-permute-start = (bf16[2,768,128]{2,1,0:T(8,128)(2,1)S(1)}, bf16[2,768,128]{2,1,0:T(8,128)(2,1)S(1)}, u32[]{:S(2)}, u32[]{:S(2)}) collective-permute-start(bf16[2,768,128]{2,1,0:T(8,128)(2,1)S(1)} %get-tuple-element.19.b0.one), channel_id=1, source_target_pairs={{0,32},{32,0},{64,96},{96,64},{128,160},{160,128},{192,224},{224,1... | collective-permute-start | bytes 1179656 | tf_op jit(solution)/shard_map/ppermute | solution.py:74
  66.0 12.6 %collective-permute-start.1 = (bf16[2,768,128]{2,1,0:T(8,128)(2,1)S(1)}, bf16[2,768,128]{2,1,0:T(8,128)(2,1)S(1)}, u32[]{:S(2)}, u32[]{:S(2)}) collective-permute-start(bf16[2,768,128]{2,1,0:T(8,128)(2,1)S(1)} %get-tuple-element.19.b0.one), channel_id=1, source_target_pairs={{0,64},{32,96},{64,0},{96,32},{128,192},{160,224},{192,128},{224,1... | collective-permute-start | bytes 1179656 | tf_op jit(solution)/shard_map/ppermute | solution.py:74
  68.1 23.0 %copy-start = (bf16[2,768,128]{2,1,0:T(8,128)(2,1)}, bf16[2,768,128]{2,1,0:T(8,128)(2,1)S(1)}, u32[]{:S(2)}) copy-start(bf16[2,768,128]{2,1,0:T(8,128)(2,1)S(1)} %collective-permute-done.b1.two) | copy-start | bytes 1179652
  68.1 13.2 %copy-start.8 = (s32[16]{0:T(128)S(1)}, s32[16]{0:T(128)}, u32[]{:S(2)}) copy-start(s32[16]{0:T(128)} %ids_ref.5) | copy-start | bytes 196
  68.1 16.8 %all-to-all-start.1 = ((bf16[4,768,128]{2,1,0:T(8,128)(2,1)}), bf16[4,768,128]{2,1,0:T(8,128)(2,1)S(1)}, u32[]{:S(2)}, u32[]{:S(2)}) async-start(bf16[4,768,128]{2,1,0:T(8,128)(2,1)} %get-tuple-element.20.q4_ref), calls=%async_computation.1 | async-start | bytes 1572864 | tf_op jit(solution)/shard_map/all_to_all | solution.py:68
  78.6 12.5 %copy-start.2 = (bf16[2,768,128]{2,1,0:T(8,128)(2,1)}, bf16[2,768,128]{2,1,0:T(8,128)(2,1)S(1)}, u32[]{:S(2)}) copy-start(bf16[2,768,128]{2,1,0:T(8,128)(2,1)S(1)} %collective-permute-done.1.b2) | copy-start | bytes 1179652
  78.6 12.5 %collective-permute-start.2 = (bf16[2,768,128]{2,1,0:T(8,128)(2,1)S(1)}, bf16[2,768,128]{2,1,0:T(8,128)(2,1)}, u32[]{:S(2)}, u32[]{:S(2)}) collective-permute-start(bf16[2,768,128]{2,1,0:T(8,128)(2,1)S(1)} %collective-permute-done.1.b2), channel_id=1, source_target_pairs={{0,32},{32,0},{64,96},{96,64},{128,160},{160,128},{192,224},{224,1... | collective-permute-start | bytes 1179656 | tf_op jit(solution)/shard_map/ppermute | solution.py:74
  84.9 31.2 %all-to-all-start.2 = ((bf16[16,2,32,128]{3,2,1,0:T(8,128)(2,1)}), bf16[16,2,32,128]{3,2,1,0:T(8,128)(2,1)S(1)}, u32[]{:S(2)}, u32[]{:S(2)}) async-start(bf16[16,2,32,128]{3,2,1,0:T(8,128)(2,1)} %get-tuple-element.25), calls=%async_computation.2 | async-start | bytes 524288 | tf_op jit(solution)/shard_map/all_to_all | solution.py:643
  116.1 21.2 %all-to-all-start.3 = ((bf16[4,800,128]{2,1,0:T(8,128)(2,1)}), bf16[4,800,128]{2,1,0:T(8,128)(2,1)S(1)}, u32[]{:S(2)}, u32[]{:S(2)}) async-start(bf16[4,800,128]{2,1,0:T(8,128)(2,1)} %attend.1), calls=%async_computation.3 | async-start | bytes 1638400 | tf_op jit(solution)/shard_map/all_to_all | solution.py:68
  124.9 2.4 %copy-start.1 = (bf16[2,768,128]{2,1,0:T(8,128)(2,1)S(1)}, bf16[2,768,128]{2,1,0:T(8,128)(2,1)}, u32[]{:S(2)}) copy-start(bf16[2,768,128]{2,1,0:T(8,128)(2,1)} %copy-done) | copy-start | bytes 1179652
  124.9 2.4 %copy-start.3 = (bf16[2,768,128]{2,1,0:T(8,128)(2,1)S(1)}, bf16[2,768,128]{2,1,0:T(8,128)(2,1)}, u32[]{:S(2)}) copy-start(bf16[2,768,128]{2,1,0:T(8,128)(2,1)} %copy-done.2) | copy-start | bytes 1179652
  126.5 0.7 copy-start.4
  127.2 10.1 %copy-start.9 = (f32[1,128]{1,0:T(1,128)S(1)}, f32[1,128]{1,0:T(1,128)}, u32[]{:S(2)}) copy-start(f32[1,128]{1,0:T(1,128)} %gate_hbm.1) | copy-start | bytes 1540
  137.3 1.0 copy-start.5

commit v6 on v5

--- a/solution.py
+++ b/solution.py
@@ -393,7 +393,7 @@
 
 
 def own_kernel(
-    ids_ref, q_ref, b0, b1, b2, b3, top_hbm, sum_hbm,
+    ids_ref, q_ref, b0, b1, b2, b3, cross_ref, top_hbm, sum_hbm,
     out_ref, queries, held, top_ref, sum_ref, sems, pair_ref, one_ref, full_ref, *scores,
 ):
     copies = [
@@ -411,11 +411,13 @@
     @pl.loop(0, count // TILE)
     def _(half):
         def write(start, part):
-            out_ref[pl.ds(pl.multiple_of(half * TILE + start, HD), HD), :] = part
+            where = pl.ds(pl.multiple_of(half * TILE + start, HD), HD)
+            out_ref[0, where, :] = cross_ref[where, :]
+            out_ref[1, where, :] = part
 
         means(sum_ref[0, half], write)
 
-    out_ref[pl.ds(count, 8), :] = log_sums(0, top_ref, sum_ref)
+    out_ref[1, pl.ds(count, 8), :] = log_sums(0, top_ref, sum_ref)
 
 
 def log_sums(place, top_ref, sum_ref):
@@ -501,13 +503,13 @@
     )(group_ids, queries, *blocks)
 
 
-def own(group_ids, queries, blocks, begun):
+def own(group_ids, queries, blocks, cross, begun):
     count = queries.shape[1]
     return pl.pallas_call(
         own_kernel,
-        in_specs=[SMEM] + [VMEM] * 5 + [HBM] * 2,
+        in_specs=[SMEM] + [VMEM] * 6 + [HBM] * 2,
         out_specs=VMEM,
-        out_shape=jax.ShapeDtypeStruct((count + 8, HD), jnp.float32),
+        out_shape=jax.ShapeDtypeStruct((2, count + 8, HD), jnp.float32),
         scratch_shapes=[
             *attend_scratch(1, count),
             pltpu.SemaphoreType.DMA((2,)),
@@ -517,7 +519,7 @@
         compiler_params=PARAMS,
         cost_estimate=cost(2),
         name="own",
-    )(group_ids, queries, *blocks, *begun)
+    )(group_ids, queries, *blocks, cross, *begun)
 
 
 def cross_kernel(len_ref, in_ref, text_ref, out_hbm, c_ref, cross_ref, sem):
@@ -568,19 +570,15 @@
     )(text_len, received, text)
 
 
-def merge_kernel(
-    own_hbm, cross_hbm, back_ref, gate_hbm, out_ref, own_ref, cross_ref, weight_ref, gate_ref, sems
-):
+def merge_kernel(mine_hbm, back_ref, gate_hbm, out_ref, mine_ref, weight_ref, gate_ref, sems):
     copies = [
-        pltpu.make_async_copy(source, target, sems.at[number])
-        for number, (source, target) in enumerate(
-            ((own_hbm, own_ref), (cross_hbm, cross_ref), (gate_hbm, gate_ref))
-        )
+        pltpu.make_async_copy(mine_hbm, mine_ref, sems.at[0]),
+        pltpu.make_async_copy(gate_hbm, gate_ref, sems.at[1]),
     ]
     for copy in copies:
         copy.start()
     slot = lax.axis_index("group")
-    count = cross_ref.shape[0]
+    count = out_ref.shape[0]
     received = [back_ref.at[place_across(slot, step)] for step in (1, 2, 3)]
     logs = []
     for ref in received:
@@ -588,7 +586,7 @@
         logs.append(tail[0:8] + tail[8:16] + tail[16:24])
     for copy in copies:
         copy.wait()
-    logs.append(own_ref[pl.ds(count, 8), :])
+    logs.append(mine_ref[1, pl.ds(count, 8), :])
     best = functools.reduce(jnp.maximum, logs)
     weights = [jnp.exp2(line - best) for line in logs]
     total = functools.reduce(jnp.add, weights)
@@ -599,30 +597,29 @@
     @pl.loop(0, count // HD)
     def _(step):
         rows = pl.ds(pl.multiple_of(step * HD, HD), HD)
-        mixed = weight_ref[3, pl.ds(step, 1), :] * own_ref[rows, :]
+        mixed = weight_ref[3, pl.ds(step, 1), :] * mine_ref[1, rows, :]
         for place, ref in enumerate(received):
             line = weight_ref[place, pl.ds(step, 1), :]
             mixed = mixed + line * ref[rows, :].astype(jnp.float32)
-        out_ref[rows, :] = (gate * mixed + cross_ref[rows, :]).astype(jnp.bfloat16).T
-
-
-def merge(mine, cross, back, gate):
+        out_ref[rows, :] = (gate * mixed + mine_ref[0, rows, :]).astype(jnp.bfloat16).T
+
+
+def merge(mine, back, gate):
     return pl.pallas_call(
         merge_kernel,
-        in_specs=[HBM, HBM, VMEM, HBM],
+        in_specs=[HBM, VMEM, HBM],
         out_specs=VMEM,
-        out_shape=jax.ShapeDtypeStruct(cross.shape, jnp.bfloat16),
+        out_shape=jax.ShapeDtypeStruct((mine.shape[1] - 8, HD), jnp.bfloat16),
         scratch_shapes=[
             pltpu.VMEM(mine.shape, jnp.float32),
-            pltpu.VMEM(cross.shape, jnp.float32),
             pltpu.VMEM((4, 8, HD), jnp.float32),
             pltpu.VMEM(gate.shape, jnp.float32),
-            pltpu.SemaphoreType.DMA((3,)),
+            pltpu.SemaphoreType.DMA((2,)),
         ],
         compiler_params=PARAMS,
         cost_estimate=cost(1),
         name="merge",
-    )(mine, cross, back, gate)
+    )(mine, back, gate)
 
 
 def to_heads(array):
@@ -645,8 +642,8 @@
     q = in_cluster(q)
     sent, q, text = lax.optimization_barrier((attend(group_ids, q, blocks), q, text))
     back = in_cluster(sent)
-    mine = own(group_ids, q, blocks, begun)
-    mixed = merge(mine, cross_part(text_len, received, text), back, group_gate)
+    mine = own(group_ids, q, blocks, cross_part(text_len, received, text), begun)
+    mixed = merge(mine, back, group_gate)
     count = mixed.shape[0]
     heads = lax.axis_size("seq")
     mixed = to_heads(mixed.reshape(heads, count // heads, HD))

time: 166 us -> 165 us (level)
  the two profiles are of different devices: /device:TPU:11 before, /device:TPU:1 now
where the time goes in v6:
time: 165 us; the launch traced here: 164 us
  blocking collectives  90.4 us (55%)
  starting transfers between devices  37.4 us (23%)
  Pallas kernels  30.5 us (18%)
  waiting for transfers between devices  4.13 us (3%)
    all_to_all x2, blocking collectives, to_heads(): return lax.all_to_all(array, 'seq', split_axis=0, concat_axis=0, tiled=True)  90.4 us
    all_to_all x2, starting transfers between devices, in_cluster(): lax.all_to_all(array, 'group', split_axis=0, concat_axis=0, axis_index_gr...  23.1 us
    pallas_call x1, Pallas kernels, attend(): pl.pallas_call(attend_kernel, in_specs=[SMEM] + [VMEM] * 5, out_specs=VME...  10.6 us
    pallas_call x1, Pallas kernels, own(): pl.pallas_call(own_kernel, in_specs=[SMEM] + [VMEM] * 6 + [HBM] * 2, out_...  10.1 us
    ppermute x3, starting transfers between devices, swap(): return lax.ppermute(array, 'group', [(i, partner(i)) for i in range(16)])  9.32 us
    all_to_all x1, starting transfers between devices, body(): lax.all_to_all(text, 'group', split_axis=0, concat_axis=0, tiled=True)  5.03 us
    ppermute x3, waiting for transfers between devices, swap(): return lax.ppermute(array, 'group', [(i, partner(i)) for i in range(16)])  3.88 us
    pallas_call x1, Pallas kernels, first(): pl.pallas_call(first_kernel, in_specs=[SMEM] + [VMEM] * 3, out_specs=[HBM...  3.55 us
  transfers between devices with their start and end apart: 6, of which 2 were waited for; matrix products, arithmetic and copies ran while one was open for 0% of the time, Pallas kernels for 16%

profile of v6, /device:TPU:1, one launch (start us, length us, event | category | flops | bytes accessed | tf_op | source)
XLA Modules:
  0.0 164.2 jit_solution(3021775247872513484)
XLA Ops:
  0.0 2.2 %pack.1 = bf16[32,4,24,128]{3,2,1,0:T(8,128)(2,1)} custom-call(bf16[1,24,4096]{2,1,0:T(8,128)(2,1)} %q_hbm.1, bf16[1,24,4096]{2,1,0:T(8,128)(2,1)} %k_hbm.1, bf16[1,24,4096]{2,1,0:T(8,128)(2,1)} %v_hbm.1, bf16[1,24,4096]{2,1,0:T(8,128)(2,1)} %c_hbm.1), custom_call_target="tpu_custom_call" | custom-call | tf_op jit(solution)/shard_map/pack/pallas_call | solution.py:103
  2.2 0.0 copy-start.4
  2.2 0.0 copy-start.5
  2.2 60.3 %all_to_all.25.in_ref = bf16[32,4,24,128]{3,2,1,0:T(8,128)(2,1)S(1)} all-to-all(bf16[32,4,24,128]{3,2,1,0:T(8,128)(2,1)} %pack.1), channel_id=1, replica_groups=mesh['group'=16,'seq'=32] {'seq'}, dimensions={0} | all-to-all | bytes 1572864 | tf_op jit(solution)/shard_map/all_to_all | solution.py:626
  62.5 0.0 copy-done.4
  62.5 0.0 copy-done.5
  62.5 1.8 %unpack.1 = (bf16[4,768,128]{2,1,0:T(8,128)(2,1)}, bf16[2,768,128]{2,1,0:T(8,128)(2,1)S(1)}, bf16[16,2,32,128]{3,2,1,0:T(8,128)(2,1)}) custom-call(bf16[32,4,24,128]{3,2,1,0:T(8,128)(2,1)S(1)} %all_to_all.25.in_ref, bf16[32,128]{1,0:T(8,128)(2,1)S(1)} %copy-done.4, bf16[32,128]{1,0:T(8,128)(2,1)S(1)} %copy-done.5), custom_call_target="tpu_custom_call" | custom-call | tf_op jit(solution)/shard_map/unpack/pallas_call | solution.py:165
  64.3 3.4 %collective-permute-start = (bf16[2,768,128]{2,1,0:T(8,128)(2,1)S(1)}, bf16[2,768,128]{2,1,0:T(8,128)(2,1)S(1)}, u32[]{:S(2)}, u32[]{:S(2)}) collective-permute-start(bf16[2,768,128]{2,1,0:T(8,128)(2,1)S(1)} %get-tuple-element.19.b0.one), channel_id=1, source_target_pairs={{0,32},{32,0},{64,96},{96,64},{128,160},{160,128},{192,224},{224,1... | collective-permute-start | bytes 1179656 | tf_op jit(solution)/shard_map/ppermute | solution.py:74
  67.7 3.2 %collective-permute-start.1 = (bf16[2,768,128]{2,1,0:T(8,128)(2,1)S(1)}, bf16[2,768,128]{2,1,0:T(8,128)(2,1)S(1)}, u32[]{:S(2)}, u32[]{:S(2)}) collective-permute-start(bf16[2,768,128]{2,1,0:T(8,128)(2,1)S(1)} %get-tuple-element.19.b0.one), channel_id=1, source_target_pairs={{0,64},{32,96},{64,0},{96,32},{128,192},{160,224},{192,128},{224,1... | collective-permute-start | bytes 1179656 | tf_op jit(solution)/shard_map/ppermute | solution.py:74
  70.9 0.0 collective-permute-done.b1.two
  70.9 0.0 copy-start
  70.9 0.0 copy-start.6
  70.9 5.5 %all-to-all-start.1 = ((bf16[4,768,128]{2,1,0:T(8,128)(2,1)}), bf16[4,768,128]{2,1,0:T(8,128)(2,1)S(1)}, u32[]{:S(2)}, u32[]{:S(2)}) async-start(bf16[4,768,128]{2,1,0:T(8,128)(2,1)} %get-tuple-element.20.q4_ref), calls=%async_computation.1 | async-start | bytes 1572864 | tf_op jit(solution)/shard_map/all_to_all | solution.py:68
  76.5 3.9 %collective-permute-done.1.b2 = bf16[2,768,128]{2,1,0:T(8,128)(2,1)S(1)} collective-permute-done((bf16[2,768,128]{2,1,0:T(8,128)(2,1)S(1)}, bf16[2,768,128]{2,1,0:T(8,128)(2,1)S(1)}, u32[]{:S(2)}, u32[]{:S(2)}) %collective-permute-start.1) | collective-permute-done | bytes 393248 | tf_op jit(solution)/shard_map/ppermute | solution.py:74
  80.3 0.0 copy-start.2
  80.3 2.7 %collective-permute-start.2 = (bf16[2,768,128]{2,1,0:T(8,128)(2,1)S(1)}, bf16[2,768,128]{2,1,0:T(8,128)(2,1)}, u32[]{:S(2)}, u32[]{:S(2)}) collective-permute-start(bf16[2,768,128]{2,1,0:T(8,128)(2,1)S(1)} %collective-permute-done.1.b2), channel_id=1, source_target_pairs={{0,32},{32,0},{64,96},{96,64},{128,160},{160,128},{192,224},{224,1... | collective-permute-start | bytes 1179656 | tf_op jit(solution)/shard_map/ppermute | solution.py:74
  83.0 0.0 copy-done.6
  83.0 3.6 %first.1 = (f32[1,2,1,384]{3,2,1,0:T(1,128)S(1)}, f32[1,2,144,384]{3,2,1,0:T(8,128)S(1)}) custom-call(s32[16]{0:T(128)S(1)} %copy-done.6, bf16[4,768,128]{2,1,0:T(8,128)(2,1)} %get-tuple-element.20.q4_ref, bf16[2,768,128]{2,1,0:T(8,128)(2,1)S(1)} %get-tuple-element.19.b0.one, bf16[2,768,128]{2,1,0:T(8,128)(2,1)S(1)} %collective-permute-done.b1.two), custom_call_target="tpu_custom_call" | custom-call | flops 603979776 | bytes 1048576 | tf_op jit(solution)/shard_map/first/pallas_call | solution.py:461
  86.6 0.2 all-to-all-done.1.q_ref
  86.8 5.0 %all-to-all-start.2 = ((bf16[16,2,32,128]{3,2,1,0:T(8,128)(2,1)}), bf16[16,2,32,128]{3,2,1,0:T(8,128)(2,1)S(1)}, u32[]{:S(2)}, u32[]{:S(2)}) async-start(bf16[16,2,32,128]{3,2,1,0:T(8,128)(2,1)} %get-tuple-element.25), calls=%async_computation.2 | async-start | bytes 524288 | tf_op jit(solution)/shard_map/all_to_all | solution.py:640
  91.9 0.0 collective-permute-done.2.b3
  91.9 0.0 copy-done
  91.9 0.0 copy-done.2
  91.9 10.6 %attend.1 = bf16[4,800,128]{2,1,0:T(8,128)(2,1)} custom-call(s32[16]{0:T(128)S(1)} %copy-done.6, bf16[4,768,128]{2,1,0:T(8,128)(2,1)S(1)} %all-to-all-done.1.q_ref, bf16[2,768,128]{2,1,0:T(8,128)(2,1)S(1)} %get-tuple-element.19.b0.one, bf16[2,768,128]{2,1,0:T(8,128)(2,1)S(1)} %collective-permute-done.b1.two, ...), custom_call_target="tpu_custom_call" | custom-call | flops 3623878656 | bytes 6291456 | tf_op jit(solution)/shard_map/attend/pallas_call | solution.py:494
  102.5 0.0 all-to-all-done.2.text_ref
  102.5 17.5 %all-to-all-start.3 = ((bf16[4,800,128]{2,1,0:T(8,128)(2,1)}), bf16[4,800,128]{2,1,0:T(8,128)(2,1)S(1)}, u32[]{:S(2)}, u32[]{:S(2)}) async-start(bf16[4,800,128]{2,1,0:T(8,128)(2,1)} %attend.1), calls=%async_computation.3 | async-start | bytes 1638400 | tf_op jit(solution)/shard_map/all_to_all | solution.py:68
  120.7 0.0 copy-start.1
  120.7 0.0 copy-start.3
  120.7 1.6 cross.1.cross_ref
  122.3 0.0 copy-done.1
  122.3 0.0 copy-done.3
  122.3 0.0 copy-start.7
  122.3 10.1 %own.1.mine_hbm = f32[2,776,128]{2,1,0:T(8,128)S(1)} custom-call(s32[16]{0:T(128)S(1)} %copy-done.6, bf16[4,768,128]{2,1,0:T(8,128)(2,1)S(1)} %all-to-all-done.1.q_ref, bf16[2,768,128]{2,1,0:T(8,128)(2,1)S(1)} %get-tuple-element.19.b0.one, bf16[2,768,128]{2,1,0:T(8,128)(2,1)S(1)} %copy-done.1, bf16[2,768,128]{2,1,0:T(8,128)(2,1)S(1)} %copy-done.3, ...), custom_call_target="tpu_custom_call" | custom-call | flops 603979776 | bytes 1048576 | tf_op jit(solution)/shard_map/own/pallas_call | solution.py:508
  132.4 0.0 all-to-all-done.3.back_ref
  132.4 0.0 copy-done.7
  132.4 0.8 merge.1
  133.2 30.2 %all_to_all.26 = bf16[32,24,128]{2,1,0:T(8,128)(2,1)S(1)} all-to-all(bf16[32,24,128]{2,1,0:T(8,128)(2,1)S(1)} %bitcast.2), channel_id=1, replica_groups=mesh['group'=16,'seq'=32] {'seq'}, dimensions={0} | all-to-all | bytes 393216 | tf_op jit(solution)/shard_map/all_to_all | solution.py:626
  163.4 0.8 reshape.7
  (1 shorter events, 0.0 us)
Async XLA Ops:
  2.2 60.3 %copy-start.4 = (bf16[32,128]{1,0:T(8,128)(2,1)S(1)}, bf16[32,128]{1,0:T(8,128)(2,1)}, u32[]{:S(2)}) copy-start(bf16[32,128]{1,0:T(8,128)(2,1)} %tk_hbm.1) | copy-start | bytes 24580
  2.2 60.3 %copy-start.5 = (bf16[32,128]{1,0:T(8,128)(2,1)S(1)}, bf16[32,128]{1,0:T(8,128)(2,1)}, u32[]{:S(2)}) copy-start(bf16[32,128]{1,0:T(8,128)(2,1)} %tv_hbm.1) | copy-start | bytes 24580
  64.3 6.6 %collective-permute-start = (bf16[2,768,128]{2,1,0:T(8,128)(2,1)S(1)}, bf16[2,768,128]{2,1,0:T(8,128)(2,1)S(1)}, u32[]{:S(2)}, u32[]{:S(2)}) collective-permute-start(bf16[2,768,128]{2,1,0:T(8,128)(2,1)S(1)} %get-tuple-element.19.b0.one), channel_id=1, source_target_pairs={{0,32},{32,0},{64,96},{96,64},{128,160},{160,128},{192,224},{224,1... | collective-permute-start | bytes 1179656 | tf_op jit(solution)/shard_map/ppermute | solution.py:74
  67.7 12.6 %collective-permute-start.1 = (bf16[2,768,128]{2,1,0:T(8,128)(2,1)S(1)}, bf16[2,768,128]{2,1,0:T(8,128)(2,1)S(1)}, u32[]{:S(2)}, u32[]{:S(2)}) collective-permute-start(bf16[2,768,128]{2,1,0:T(8,128)(2,1)S(1)} %get-tuple-element.19.b0.one), channel_id=1, source_target_pairs={{0,64},{32,96},{64,0},{96,32},{128,192},{160,224},{192,128},{224,1... | collective-permute-start | bytes 1179656 | tf_op jit(solution)/shard_map/ppermute | solution.py:74
  70.9 21.0 %copy-start = (bf16[2,768,128]{2,1,0:T(8,128)(2,1)}, bf16[2,768,128]{2,1,0:T(8,128)(2,1)S(1)}, u32[]{:S(2)}) copy-start(bf16[2,768,128]{2,1,0:T(8,128)(2,1)S(1)} %collective-permute-done.b1.two) | copy-start | bytes 1179652
  70.9 12.1 %copy-start.6 = (s32[16]{0:T(128)S(1)}, s32[16]{0:T(128)}, u32[]{:S(2)}) copy-start(s32[16]{0:T(128)} %ids_ref.5) | copy-start | bytes 196
  70.9 15.9 %all-to-all-start.1 = ((bf16[4,768,128]{2,1,0:T(8,128)(2,1)}), bf16[4,768,128]{2,1,0:T(8,128)(2,1)S(1)}, u32[]{:S(2)}, u32[]{:S(2)}) async-start(bf16[4,768,128]{2,1,0:T(8,128)(2,1)} %get-tuple-element.20.q4_ref), calls=%async_computation.1 | async-start | bytes 1572864 | tf_op jit(solution)/shard_map/all_to_all | solution.py:68
  80.3 11.6 %copy-start.2 = (bf16[2,768,128]{2,1,0:T(8,128)(2,1)}, bf16[2,768,128]{2,1,0:T(8,128)(2,1)S(1)}, u32[]{:S(2)}) copy-start(bf16[2,768,128]{2,1,0:T(8,128)(2,1)S(1)} %collective-permute-done.1.b2) | copy-start | bytes 1179652
  80.3 11.5 %collective-permute-start.2 = (bf16[2,768,128]{2,1,0:T(8,128)(2,1)S(1)}, bf16[2,768,128]{2,1,0:T(8,128)(2,1)}, u32[]{:S(2)}, u32[]{:S(2)}) collective-permute-start(bf16[2,768,128]{2,1,0:T(8,128)(2,1)S(1)} %collective-permute-done.1.b2), channel_id=1, source_target_pairs={{0,32},{32,0},{64,96},{96,64},{128,160},{160,128},{192,224},{224,1... | collective-permute-start | bytes 1179656 | tf_op jit(solution)/shard_map/ppermute | solution.py:74
  86.8 15.7 %all-to-all-start.2 = ((bf16[16,2,32,128]{3,2,1,0:T(8,128)(2,1)}), bf16[16,2,32,128]{3,2,1,0:T(8,128)(2,1)S(1)}, u32[]{:S(2)}, u32[]{:S(2)}) async-start(bf16[16,2,32,128]{3,2,1,0:T(8,128)(2,1)} %get-tuple-element.25), calls=%async_computation.2 | async-start | bytes 524288 | tf_op jit(solution)/shard_map/all_to_all | solution.py:640
  102.5 29.9 %all-to-all-start.3 = ((bf16[4,800,128]{2,1,0:T(8,128)(2,1)}), bf16[4,800,128]{2,1,0:T(8,128)(2,1)S(1)}, u32[]{:S(2)}, u32[]{:S(2)}) async-start(bf16[4,800,128]{2,1,0:T(8,128)(2,1)} %attend.1), calls=%async_computation.3 | async-start | bytes 1638400 | tf_op jit(solution)/shard_map/all_to_all | solution.py:68
  120.7 1.6 copy-start.1
  120.7 1.6 copy-start.3
  122.3 10.1 %copy-start.7 = (f32[1,128]{1,0:T(1,128)S(1)}, f32[1,128]{1,0:T(1,128)}, u32[]{:S(2)}) copy-start(f32[1,128]{1,0:T(1,128)} %gate_hbm.1) | copy-start | bytes 1540
